TPU v7x, 128 devices: a whole 4x4x4 slice. The times are simulated.
128 devices in a mesh: inst: 8 (over z, x_lo), blk: 16 (over y, x_hi, core).
Axes of the slice: x: 4 (x_hi: 2, x_lo: 2; x = x_hi * 2 + x_lo), y: 4, z: 4, core: 2. Of those that a mesh axis runs over, the one named last changes fastest.
Arguments:
- psi_start: float32 [8, 6, 128, 8192], P('inst', None, 'blk'), may hold values from -6 to 6
- coupling: float32 [8, 6, 6], P('inst'), may hold values from -2.5 to 2.5
- center: float32 [8, 128, 8192], P('inst', 'blk'), may hold values from 4 to 8
- spread: float32 [8, 128, 8192], P('inst', 'blk'), may hold values from 0.2 to 1
- source: float32 [8, 6, 128, 8192], P('inst', None, 'blk'), may hold values from -6 to 6
- wall_geo: float32 [8, 18, 32768], P('inst', None, 'blk'), may hold values from -6 to 6
- wall_cell: int32 [32768], P('blk'), may hold values from 0 to 65535
- wall_dest: int32 [32768, 1], P('blk'), may hold values from 0 to 15; in each aligned block of 2048 rows (0 to 2047, 2048 to 4095, ...) at most 256 rows name the same one
- wall_node: int32 [32768], P('blk'), may hold values from 0 to 4095
Outputs:
- psi_out: float32 [8, 6, 128, 8192], P('inst', None, 'blk')
- sensitivity: float32 [3, 65536], P(None, 'blk')
Inputs may be any that keep to these rules, and one draw needn't show every extreme that they name: `wall_dest`: among the 2048 wall faces of one grid block at most 256 go to one owner.
All inputs are finite; a program needn't handle non-finite values.
Results may differ from a plain program's by a relative error of at most 0.0001.
Values sent between devices are 32-bit elements; how exact they have to be, the bound alone decides.
No kernel may reach another device: no remote copies, remote signals or barrier semaphores. Data moves between devices by JAX's collectives and lax.ppermute only.
A program may use at most 192 MiB of HBM per device.

v0:
```python
import jax
import jax.numpy as jnp
from jax import lax
from jax.sharding import PartitionSpec as P

CAP = 256
NODE_DEV = 4096
ITERS = 2


def extended(shard, sides, width):
    for axis, dim in sides:
        devices, length = (lax.axis_size(axis), shard.shape[dim])
        up = [(i, (i + 1) % devices) for i in range(devices)]
        down = [(j, i) for i, j in up]
        last = lax.slice_in_dim(shard, length - width, length, axis=dim)
        leading = lax.slice_in_dim(shard, 0, width, axis=dim)
        before = lax.ppermute(last, axis, up)
        after = lax.ppermute(leading, axis, down)
        shard = jnp.concatenate([before, shard, after], axis=dim)
    return shard


def spectral_matrix(count):
    index = jnp.arange(count, dtype=jnp.int32)
    offset = index[:, None] - index[None, :]
    parity = (offset % 2).astype(jnp.float32)
    same = offset == 0
    angle = jnp.pi * offset.astype(jnp.float32) / count
    safe_angle = jnp.where(same, 1.0, angle)
    values = 0.5 * (1.0 - 2.0 * parity) / jnp.sin(safe_angle)
    return jnp.where(same, 0.0, values)


def spectral_source(psi, spec_mat):
    own_count = psi.shape[0]
    own_start = lax.axis_index("inst") * own_count
    piece = lax.all_gather(psi, "inst", axis=0, tiled=True)
    part_mat = lax.dynamic_slice(spec_mat, (0, own_start), (piece.shape[0], own_count))
    total = jnp.einsum("ji,jfxy->ifxy", part_mat, piece, precision=lax.Precision.HIGHEST)
    return 0.5 * total


def sweep(psi, coupling, center, spread, source, spec_mat):
    mixed = jnp.einsum("igf,igxy->ifxy", coupling, psi, precision=lax.Precision.HIGHEST)
    weighted = spread[:, None] * mixed
    rimmed = extended(weighted, (("blk", 2),), 1)
    beside = rimmed[:, :, 2:, :] + rimmed[:, :, :-2, :]
    padded = jnp.pad(weighted, ((0, 0), (0, 0), (0, 0), (1, 1)))
    beside = beside + padded[..., 2:] + padded[..., :-2]
    spectral = spectral_source(psi, spec_mat)
    update = center[:, None] * psi - beside + spectral - source
    return psi - (0.6 / center)[:, None] * update


def wall_partials(psi, wall_geo, wall_cell):
    inst_count, fields = (psi.shape[0], psi.shape[1])
    flat = psi.reshape(inst_count, fields, -1)
    picked = flat[:, :, wall_cell]
    geometry = wall_geo.reshape(inst_count, 3, fields, -1)
    partial_value = jnp.einsum("ikfe,ife->ike", geometry, picked, precision=lax.Precision.HIGHEST)
    return partial_value.reshape(inst_count * 3, -1)


def owner_slots(wall_dest, owners):
    dest = wall_dest[:, 0]
    onehot = (dest[:, None] == jnp.arange(owners, dtype=jnp.int32)[None, :]).astype(jnp.int32)
    before = jnp.cumsum(onehot, axis=0) - onehot
    rank = jnp.sum(before * onehot, axis=1)
    return (dest, rank)


def pack_slots(partial_value, dest, rank, wall_node, owners):
    rows = partial_value.shape[0]
    value_buf = jnp.zeros((rows, owners, CAP), jnp.float32).at[:, dest, rank].set(partial_value)
    node_buf = jnp.zeros((1, owners, CAP), jnp.int32).at[0, dest, rank].set(wall_node)
    return (value_buf, node_buf)


def unpack_slots(got_values, got_nodes):
    rows = got_values.shape[0]
    summed = jax.ops.segment_sum(
        got_values.reshape(rows, -1).T, got_nodes.reshape(-1), num_segments=NODE_DEV
    )
    return jnp.sum(summed.T.reshape(rows // 3, 3, NODE_DEV), axis=0)


def local(psi_start, coupling, center, spread, source, wall_geo, wall_cell, wall_dest, wall_node):
    owners = lax.axis_size("blk")
    spec_mat = spectral_matrix(psi_start.shape[0] * lax.axis_size("inst"))
    dest, rank = owner_slots(wall_dest, owners)
    sens_local = jnp.zeros((3, NODE_DEV), jnp.float32)
    psi = psi_start
    for step in range(ITERS):
        psi = sweep(psi, coupling, center, spread, source, spec_mat)
        partial_value = wall_partials(psi, wall_geo, wall_cell)
        value_buf, node_buf = pack_slots(partial_value, dest, rank, wall_node, owners)
        got_values, got_nodes = (
            lax.all_to_all(value_buf, "blk", split_axis=1, concat_axis=1, tiled=True),
            lax.all_to_all(node_buf, "blk", split_axis=1, concat_axis=1, tiled=True),
        )
        sens_local = sens_local + unpack_slots(got_values, got_nodes)
    sensitivity = lax.psum(sens_local, "inst")
    return (psi, sensitivity)


def solution(mesh):
    placed = (
        P("inst", None, "blk", None),
        P("inst", None, None),
        P("inst", "blk", None),
        P("inst", "blk", None),
        P("inst", None, "blk", None),
        P("inst", None, "blk"),
        P("blk"),
        P("blk", None),
        P("blk"),
    )
    return jax.shard_map(
        local,
        mesh=mesh,
        in_specs=placed,
        out_specs=(P("inst", None, "blk", None), P(None, "blk")),
        check_vma=False,
    )
```

profile of v0, /device:TPU:12, one launch (start us, length us, event | category | flops | bytes accessed | tf_op | source)
XLA Modules:
  0.0 804.5 jit_solution(17933240960903875595)
XLA Ops:
  7.2 0.0 copy-start.1
  7.2 0.0 all-gather.3.cloned.1.call-start
  7.2 0.7 all-gather.3.cloned.1.call-update
  7.9 0.0 all-gather.5.cloned.1.call-start
  8.0 0.6 copy-done.1
  8.6 4.3 fusion.4
  12.9 1.4 copy-done.3
  14.2 0.1 collective-permute-start
  14.3 0.6 collective-permute-start.1
  15.1 244.9 %all-gather.3.cloned.1.call-done = f32[8,6,8,8192]{3,2,1,0:T(8,128)} async-done(((f32[1,6,8,8192]{3,2,1,0:T(8,128)}), f32[8,6,8,8192]{3,2,1,0:T(8,128)}) %all-gather.3.cloned.1.call-update) | async-done | bytes 12582928 | tf_op jit(solution)/shard_map/all_gather | solution.py:38
  260.0 22.3 %fusion.2 = f32[1,6,8,8192]{3,0,2,1:T(1,128)S(1)} fusion(f32[8,6,8,8192]{3,2,1,0:T(8,128)} %all-gather.3.cloned.1.call-done, f32[8,8]{0,1:T(8,128)S(1)} %fusion.42, s32[]{:T(128)S(6)} %select_n.45), kind=kOutput, calls=%fused_computation.9 | convolution fusion | flops 37748736 | bytes 14156292 | tf_op jit(solution)/shard_map/ji,jfxy->ifxy/dot_general | solution.py:40
  282.3 0.0 collective-permute-done
  282.3 0.0 collective-permute-done.1
  282.4 5.1 copy_subtract_fusion
  287.5 0.0 copy-start.13
  287.5 2.1 copy.51
  289.5 0.0 all-gather.5.cloned.1.call-update
  289.6 4.5 reduce-window.6
  294.1 0.4 slice_reduce_fusion
  294.6 0.2 reduce-window.9
  294.7 0.1 broadcast_add_fusion
  294.9 0.1 fusion.31
  295.0 0.1 multiply_reduce_fusion
  295.1 0.1 and_reduce_fusion.1
  295.2 8.8 %scatter_custom_fusion.2 = s32[4096]{0:T(1024)} fusion(s32[2048]{0:T(1024)S(1)} %broadcast_select_fusion.1, s32[2048]{0:T(1024)} %param.17, s32[]{:T(128)} %constant.18.clone.1), kind=kCustom, calls=%fused_computation.69 | custom fusion | bytes 16896
  304.0 8.2 %all-to-all-start = ((s32[1,16,256]{2,0,1:T(1,128)}), s32[1,16,256]{2,0,1:T(1,128)S(1)}, u32[]{:S(2)}, u32[]{:S(2)}) async-start(s32[1,16,256]{2,0,1:T(1,128)} %bitcast.24), calls=%async_computation | async-start | bytes 32768 | tf_op jit(solution)/shard_map/all_to_all | solution.py:100
  312.1 0.3 reduce.7
  312.5 0.0 copy-start.18
  312.5 0.0 copy-start.17
  312.6 0.0 copy-start.15
  312.6 0.0 copy-start.11
  312.6 0.0 copy-start.14
  312.6 3.1 copy.70
  315.7 0.1 multiply_reduce_fusion.1
  315.8 0.1 and_reduce_fusion
  316.0 2.1 fusion.5
  318.1 1.3 copy-done.5
  319.4 0.7 fusion.53
  320.1 0.3 collective-permute-start.2
  320.4 0.2 collective-permute-start.3
  320.6 17.3 %copy.53 = f32[6,65536]{0,1:T(8,128)} copy(f32[6,65536]{1,0:T(8,128)S(1)} %bitcast.101) | data formatting | bytes 3145728 | tf_op jit(solution)/shard_map/reshape | solution.py:58
  337.9 18.2 %gather_fusion = f32[2048,6]{1,0:T(8,128)} fusion(f32[6,65536]{0,1:T(8,128)} %copy.53, s32[2048]{0:T(1024)S(1)} %fusion.33), kind=kCustom, calls=%fused_computation | custom fusion | bytes 106496 | tf_op jit(solution)/shard_map/gather | solution.py:59
  356.1 16.6 %fusion.55 = f32[2048,1,3]{2,1,0:T(1,128)} fusion(f32[6,2048,1]{0,2,1:T(1,128)} %bitcast.120, f32[3,6,2048]{1,0,2:T(4,128)} %copy.70), kind=kOutput, calls=%fused_computation.97 | convolution fusion | flops 442368 | bytes 221184 | tf_op jit(solution)/shard_map/ikfe,ife->ike/dot_general | solution.py:61
  372.7 7.4 scatter_custom_fusion.3
  380.1 2.8 copy.54
  382.9 161.9 %all-gather.5.cloned.1.call-done = f32[8,6,8,8192]{3,2,1,0:T(8,128)} async-done(((f32[1,6,8,8192]{3,2,1,0:T(8,128)}), f32[8,6,8,8192]{3,2,1,0:T(8,128)}) %all-gather.5.cloned.1.call-update) | async-done | bytes 12582928 | tf_op jit(solution)/shard_map/all_gather | solution.py:38
  544.8 22.5 %fusion = f32[1,6,8,8192]{3,0,2,1:T(1,128)S(1)} fusion(f32[8,6,8,8192]{3,2,1,0:T(8,128)} %all-gather.5.cloned.1.call-done, f32[8,8]{0,1:T(8,128)S(1)} %fusion.42, s32[]{:T(128)S(6)} %select_n.45), kind=kOutput, calls=%fused_computation.7 | convolution fusion | flops 37748736 | bytes 14156292 | tf_op jit(solution)/shard_map/ji,jfxy->ifxy/dot_general | solution.py:40
  567.3 5.0 fusion.8
  572.3 16.5 %copy.56 = f32[6,65536]{0,1:T(8,128)} copy(f32[6,65536]{1,0:T(8,128)} %bitcast.102) | data formatting | bytes 3145728 | tf_op jit(solution)/shard_map/reshape | solution.py:58
  588.8 16.0 %gather_fusion.1 = f32[2048,6]{1,0:T(8,128)S(1)} fusion(f32[6,65536]{0,1:T(8,128)} %copy.56, s32[2048]{0:T(1024)S(1)} %fusion.33), kind=kCustom, calls=%fused_computation.1 | custom fusion | bytes 106496 | tf_op jit(solution)/shard_map/gather | solution.py:59
  604.8 0.0 all-to-all-done
  604.8 7.3 all-to-all-start.1
  612.1 16.3 %fusion.56 = f32[2048,1,3]{2,1,0:T(1,128)} fusion(f32[6,2048,1]{0,2,1:T(1,128)S(1)} %bitcast.119, f32[3,6,2048]{1,0,2:T(4,128)} %copy.70), kind=kOutput, calls=%fused_computation.98 | convolution fusion | flops 442368 | bytes 221184 | tf_op jit(solution)/shard_map/ikfe,ife->ike/dot_general | solution.py:61
  628.3 6.5 scatter_custom_fusion.4
  634.8 1.3 copy.57
  636.0 7.6 all-to-all-start.2
  643.6 1.9 copy.55
  645.6 27.2 %scatter_custom_fusion = f32[4096,3]{1,0:T(8,128)} fusion(s32[4096]{0:T(1024)S(1)} %bitcast.117, f32[4096,3]{1,0:T(8,128)} %copy.55, f32[]{:T(128)} %constant.17.clone.1), kind=kCustom, calls=%fused_computation.47 | custom fusion | flops 12288 | bytes 49664 | tf_op jit(solution)/shard_map/scatter-add | solution.py:82
  672.8 2.1 copy.59
  674.8 2.0 copy.58
  676.8 27.1 %scatter_custom_fusion.1 = f32[4096,3]{1,0:T(8,128)} fusion(s32[4096]{0:T(1024)S(1)} %bitcast.118, f32[4096,3]{1,0:T(8,128)} %copy.58, f32[]{:T(128)} %constant.17.clone.1), kind=kCustom, calls=%fused_computation.45 | custom fusion | flops 12288 | bytes 49664 | tf_op jit(solution)/shard_map/scatter-add | solution.py:82
  703.9 3.1 add_bitcast_fusion
  707.0 89.2 %psum.7 = f32[3,4096]{0,1:T(8,128)S(1)} all-reduce(f32[3,4096]{0,1:T(8,128)} %add_bitcast_fusion), channel_id=1, replica_groups=mesh['inst'=8,'blk'=16] {'inst'}, use_global_device_ids=true, to_apply=%region_8.9 | all-reduce | flops 12288 | bytes 98304 | tf_op jit(solution)/shard_map/psum | solution.py:103
  796.2 1.2 copy.60
  (44 shorter events, 0.3 us)
Async XLA Ops:
  7.2 1.4 copy-start.1
  7.2 252.8 %all-gather.3.cloned.1.call-start = ((), (), s32[]{:S(2)}) async-start(), calls=%async_computation.3 | async-start | bytes 14155776 | tf_op jit(solution)/shard_map/all_gather | solution.py:38
  7.9 536.9 %all-gather.5.cloned.1.call-start = ((), (), s32[]{:S(2)}) async-start(), calls=%async_computation.4 | async-start | bytes 14155776 | tf_op jit(solution)/shard_map/all_gather | solution.py:38
  8.6 6.5 copy-start.10
  12.8 1.4 copy-start.3
  14.2 268.1 %collective-permute-start = (f32[1,6,1,8192]{3,1,2,0:T(8,128)S(1)}, f32[1,6,1,8192]{3,1,2,0:T(8,128)S(1)}, u32[]{:S(2)}, u32[]{:S(2)}) collective-permute-start(f32[1,6,1,8192]{3,1,2,0:T(8,128)S(1)} %get-tuple-element.12), channel_id=1, source_target_pairs={{1,0},{2,1},{3,2},{4,3},{5,4},{6,5},{7,6},{8,7},{9,8},{10,9},{11,1... | collective-permute-start | bytes 589832 | tf_op jit(solution)/shard_map/ppermute | solution.py:19
  14.3 268.0 %collective-permute-start.1 = (f32[1,6,1,8192]{3,1,2,0:T(8,128)S(1)}, f32[1,6,1,8192]{3,1,2,0:T(8,128)S(1)}, u32[]{:S(2)}, u32[]{:S(2)}) collective-permute-start(f32[1,6,1,8192]{3,1,2,0:T(8,128)S(1)} %get-tuple-element.13), channel_id=1, source_target_pairs={{0,1},{1,2},{2,3},{3,4},{4,5},{5,6},{6,7},{7,8},{8,9},{9,10},{10,1... | collective-permute-start | bytes 589832 | tf_op jit(solution)/shard_map/ppermute | solution.py:18
  260.0 22.3 %copy-start.2 = (f32[1,6,8,8192]{3,2,1,0:T(8,128)S(1)}, f32[1,6,8,8192]{3,2,1,0:T(8,128)}, u32[]{:S(2)}) copy-start(f32[1,6,8,8192]{3,2,1,0:T(8,128)} %param.9) | copy-start | bytes 4718596
  260.0 22.4 %copy-start.4 = (f32[1,6,8,8192]{3,1,2,0:T(8,128)S(1)}, f32[1,6,8,8192]{3,1,2,0:T(8,128)}, u32[]{:S(2)}) copy-start(f32[1,6,8,8192]{3,1,2,0:T(8,128)} %copy-done.3) | copy-start | bytes 4718596
  260.0 22.4 %copy-start.8 = (f32[1,6,8,8192]{3,2,1,0:T(8,128)S(1)}, f32[1,6,8,8192]{3,2,1,0:T(8,128)}, u32[]{:S(2)}) copy-start(f32[1,6,8,8192]{3,2,1,0:T(8,128)} %param.13) | copy-start | bytes 4718596
  287.5 2.1 copy-start.13
  289.5 5.4 copy-start.16
  289.5 5.5 copy-start.19
  289.5 22.6 %copy-start.12 = (f32[1,18,2048]{2,0,1:T(1,128)S(1)}, f32[1,18,2048]{2,0,1:T(1,128)}, u32[]{:S(2)}) copy-start(f32[1,18,2048]{2,0,1:T(1,128)} %param.14) | copy-start | bytes 442372
  304.0 300.8 %all-to-all-start = ((s32[1,16,256]{2,0,1:T(1,128)}), s32[1,16,256]{2,0,1:T(1,128)S(1)}, u32[]{:S(2)}, u32[]{:S(2)}) async-start(s32[1,16,256]{2,0,1:T(1,128)} %bitcast.24), calls=%async_computation | async-start | bytes 32768 | tf_op jit(solution)/shard_map/all_to_all | solution.py:100
  312.5 3.2 copy-start.18
  312.5 3.3 copy-start.17
  312.6 3.4 copy-start.15
  312.6 3.4 copy-start.11
  312.6 3.4 copy-start.14
  318.1 1.3 copy-start.5
  320.1 247.2 %collective-permute-start.2 = (f32[1,6,1,8192]{3,1,2,0:T(8,128)}, f32[1,6,1,8192]{3,1,2,0:T(8,128)S(1)}, u32[]{:S(2)}, u32[]{:S(2)}) collective-permute-start(f32[1,6,1,8192]{3,1,2,0:T(8,128)} %get-tuple-element.10), channel_id=1, source_target_pairs={{1,0},{2,1},{3,2},{4,3},{5,4},{6,5},{7,6},{8,7},{9,8},{10,9},{11,1... | collective-permute-start | bytes 589832 | tf_op jit(solution)/shard_map/ppermute | solution.py:19
  320.4 246.8 %collective-permute-start.3 = (f32[1,6,1,8192]{3,1,2,0:T(8,128)S(1)}, f32[1,6,1,8192]{3,1,2,0:T(8,128)S(1)}, u32[]{:S(2)}, u32[]{:S(2)}) collective-permute-start(f32[1,6,1,8192]{3,1,2,0:T(8,128)S(1)} %get-tuple-element.11), channel_id=1, source_target_pairs={{0,1},{1,2},{2,3},{3,4},{4,5},{5,6},{6,7},{7,8},{8,9},{9,10},{10,1... | collective-permute-start | bytes 589832 | tf_op jit(solution)/shard_map/ppermute | solution.py:18
  544.8 22.5 %copy-start.6 = (f32[1,6,8,8192]{3,1,2,0:T(8,128)S(1)}, f32[1,6,8,8192]{3,1,2,0:T(8,128)}, u32[]{:S(2)}) copy-start(f32[1,6,8,8192]{3,1,2,0:T(8,128)} %copy-done.5) | copy-start | bytes 4718596
  544.8 22.5 %copy-start.9 = (f32[1,6,8,8192]{3,2,1,0:T(8,128)S(1)}, f32[1,6,8,8192]{3,2,1,0:T(8,128)}, u32[]{:S(2)}) copy-start(f32[1,6,8,8192]{3,2,1,0:T(8,128)} %param.13) | copy-start | bytes 4718596
  604.8 31.2 %all-to-all-start.1 = ((f32[3,16,256]{2,0,1:T(4,128)}), f32[3,16,256]{2,0,1:T(4,128)S(1)}, u32[]{:S(2)}, u32[]{:S(2)}) async-start(f32[3,16,256]{2,0,1:T(4,128)} %copy.54), calls=%async_computation.1 | async-start | bytes 131072 | tf_op jit(solution)/shard_map/all_to_all | solution.py:99
  636.0 38.8 %all-to-all-start.2 = ((f32[3,16,256]{2,0,1:T(4,128)}), f32[3,16,256]{2,0,1:T(4,128)S(1)}, u32[]{:S(2)}, u32[]{:S(2)}) async-start(f32[3,16,256]{2,0,1:T(4,128)} %copy.57), calls=%async_computation.2 | async-start | bytes 131072 | tf_op jit(solution)/shard_map/all_to_all | solution.py:99
  643.6 29.1 %copy-start = (f32[1,6,8,8192]{3,1,2,0:T(8,128)S(1)}, f32[1,6,8,8192]{3,1,2,0:T(8,128)}, u32[]{:S(2)}) copy-start(f32[1,6,8,8192]{3,1,2,0:T(8,128)} %fusion.8) | copy-start | bytes 4718596
  674.8 29.1 %copy-start.7 = (f32[4096,3]{1,0:T(8,128)S(1)}, f32[4096,3]{1,0:T(8,128)}, u32[]{:S(2)}) copy-start(f32[4096,3]{1,0:T(8,128)} %scatter_custom_fusion) | copy-start | bytes 147460
Sparse Core Ops, SparseCore 0:
  9.7 250.3 all-gather.2
  289.7 255.0 all-gather.4
where the time goes:
time: 812 us; the launch traced here: 805 us
  waiting for transfers between devices  408 us (50%)
  local copies, waits for them, and re-layouts  112 us (14%)
  blocking collectives  89.2 us (11%)
  matrix products  83.9 us (10%)
  other arithmetic  73.2 us (9%)
  starting transfers between devices  24.3 us (3%)
  between operations  14.7 us (2%)
    all_gather x2, waiting for transfers between devices, spectral_source(): piece = lax.all_gather(psi, 'inst', axis=0, tiled=True)  407 us
    psum x1, blocking collectives, local(): sensitivity = lax.psum(sens_local, 'inst')  89.2 us
    scatter-add x2, other arithmetic, unpack_slots(): jax.ops.segment_sum(got_values.reshape(rows, -1).T, got_nodes.reshape(-1)...  54.3 us
    dot_general x2, matrix products, spectral_source(): jnp.einsum('ji,jfxy->ifxy', part_mat, piece, precision=lax.Precision.HIGH...  44.8 us
    gather x2, local copies, waits for them, and re-layouts, wall_partials(): picked = flat[:, :, wall_cell]  34.2 us
    reshape x2, local copies, waits for them, and re-layouts, wall_partials(): flat = psi.reshape(inst_count, fields, -1)  33.8 us
    dot_general x2, matrix products, wall_partials(): jnp.einsum('ikfe,ife->ike', geometry, picked, precision=lax.Precision.HIG...  32.8 us
    unnamed x45, local copies, waits for them, and re-layouts  29.3 us
  transfers between devices with their start and end apart: 9, of which 2 were waited for; matrix products, arithmetic and copies ran while one was open for 28% of the time, Pallas kernels for 0%

commit v1 on v0

v1 whole, which is shorter than its diff:
```python
import math

import jax
import jax.numpy as jnp
from jax import lax
from jax.experimental import pallas as pl
from jax.experimental.pallas import tpu as pltpu
from jax.sharding import PartitionSpec as P

CAP = 256
NODE_DEV = 4096
INST = 8
N_BLK = 16
F = 6
PLANES = 14
TILES = 8
FACES = 2048
GROUPS = FACES // 128
VMEM = 40 * 1024 * 1024

HALF_SPEC = [0.0] + [
    0.25 * (-1.0) ** d / math.sin(math.pi * d / INST) for d in range(1, INST)
]


def params():
    return pltpu.CompilerParams(vmem_limit_bytes=VMEM)


def cost(flops, nbytes):
    return pl.CostEstimate(flops=flops, bytes_accessed=nbytes, transcendentals=0)


def rows_iota(shape=(8, 128)):
    return lax.broadcasted_iota(jnp.int32, shape, 0)


def lanes_iota(shape=(8, 128)):
    return lax.broadcasted_iota(jnp.int32, shape, 1)


def full(shape):
    return pl.BlockSpec(shape, lambda *_: (0,) * len(shape))


def one(*shape):
    return pl.BlockSpec((1,) + shape, lambda i: (i,) + (0,) * len(shape))


def f32(*shape):
    return jax.ShapeDtypeStruct(shape, jnp.float32)


def pack_kernel(psi, source, center, spread, coupling, out):
    for t in range(TILES):
        cols = slice(t * 128, (t + 1) * 128)
        for f in range(F):
            out[0, t * PLANES + f] = psi[f, :, cols]
            out[0, t * PLANES + F + f] = source[f, :, cols]
        out[0, t * PLANES + 12] = 0.6 / center[:, cols]
        out[0, t * PLANES + 13] = spread[:, cols]
    out[0, TILES * PLANES] = jnp.zeros((8, 128), jnp.float32)
    out[0, TILES * PLANES, 0:F, 0:F] = coupling[0]


def pack(psi, source, center, spread, coupling):
    wide = pl.BlockSpec((F, 8, 1024), lambda c: (0, 0, c))
    flat = pl.BlockSpec((8, 1024), lambda c: (0, c))
    return pl.pallas_call(
        pack_kernel,
        grid=(INST,),
        in_specs=[wide, wide, flat, flat, full((1, F, F))],
        out_specs=one(TILES * PLANES + 1, 8, 128),
        out_shape=f32(INST, TILES * PLANES + 1, 8, 128),
        compiler_params=params(),
        cost_estimate=cost(10**6, 8 * 10**6),
    )(psi, source, center, spread, coupling)


def faces_kernel(cell, dest, chunk, list_cell, list_face, slot, count, loads):
    for owner in range(N_BLK):
        loads[owner] = 0

    def step(face, found):
        here = cell[face]
        owner = dest[face]
        rank = loads[owner]
        slot[face] = owner * CAP + rank
        loads[owner] = rank + 1
        list_cell[found] = here
        list_face[found] = face
        mine = ((here & 8191) >> 10) == chunk[0]
        return found + mine.astype(jnp.int32)

    found = lax.fori_loop(0, FACES, step, jnp.int32(0))
    count[0] = found

    def fill(at, carry):
        list_cell[at] = 0
        list_face[at] = -1
        return carry

    lax.fori_loop(found, jnp.minimum(found + 128, FACES), fill, 0)


def sort_faces(cell, dest, chunk):
    smem = pl.BlockSpec(memory_space=pltpu.SMEM)
    ints = jax.ShapeDtypeStruct((FACES,), jnp.int32)
    return pl.pallas_call(
        faces_kernel,
        in_specs=[smem] * 3,
        out_specs=[smem] * 4,
        out_shape=[ints, ints, ints, jax.ShapeDtypeStruct((1,), jnp.int32)],
        scratch_shapes=[pltpu.SMEM((N_BLK,), jnp.int32)],
        cost_estimate=cost(10**9, 10**7),
    )(cell, dest, chunk)


def fluxes(psi_of, spread_of, coupling, inner, top, bottom, left, right, held):
    row, lane = rows_iota(), lanes_iota()
    factor = [
        [jnp.broadcast_to(coupling[g : g + 1, f : f + 1], (8, 128)) for f in range(F)]
        for g in range(F)
    ]
    for t in range(TILES):
        psi = [psi_of(t, f) for f in range(F)]
        strength = spread_of(t)
        for f in range(F):
            total = factor[0][f] * psi[0]
            for g in range(1, F):
                total = total + factor[g][f] * psi[g]
            weighted = strength * total
            held[t * F + f] = weighted
            top[0, f, t : t + 1, :] = weighted[0:1, :]
            bottom[0, f, t : t + 1, :] = weighted[7:8, :]
    first = jnp.zeros((8, 128), jnp.float32)
    last = jnp.zeros((8, 128), jnp.float32)
    for f in range(F):
        tiles = [held[t * F + f] for t in range(TILES)]
        later = [pltpu.roll(x, 1, 1) for x in tiles]
        sooner = [pltpu.roll(x, 127, 1) for x in tiles]
        first = jnp.where(lane == f, jnp.broadcast_to(tiles[0][:, 0:1], (8, 128)), first)
        last = jnp.where(lane == f, jnp.broadcast_to(tiles[7][:, 127:128], (8, 128)), last)
        for t in range(TILES):
            before = later[t - 1] if t else jnp.zeros((8, 128), jnp.float32)
            after = sooner[t + 1] if t < TILES - 1 else jnp.zeros((8, 128), jnp.float32)
            total = jnp.where(lane == 0, before, later[t])
            total = total + jnp.where(lane == 127, after, sooner[t])
            total = total + jnp.where(row == 0, 0.0, pltpu.roll(tiles[t], 1, 0))
            total = total + jnp.where(row == 7, 0.0, pltpu.roll(tiles[t], 7, 0))
            inner[0, t * F + f] = total
    left[0] = first
    right[0] = last


def first_kernel(got, inner, top, bottom, left, right, scales, held):
    for t in range(TILES):
        scales[0, t] = got[0, t * PLANES + 12]
        scales[0, TILES + t] = got[0, t * PLANES + 13]
    fluxes(
        lambda t, f: got[0, t * PLANES + f],
        lambda t: got[0, t * PLANES + 13],
        got[0, TILES * PLANES],
        inner, top, bottom, left, right, held,
    )


FLUX_SPECS = [one(TILES * F, 8, 128), one(F, 8, 128), one(F, 8, 128), one(8, 128), one(8, 128)]
FLUX_SHAPES = [
    f32(INST, TILES * F, 8, 128),
    f32(INST, F, 8, 128),
    f32(INST, F, 8, 128),
    f32(INST, 8, 128),
    f32(INST, 8, 128),
]


def first_fluxes(got):
    return pl.pallas_call(
        first_kernel,
        grid=(INST,),
        in_specs=[one(TILES * PLANES + 1, 8, 128)],
        out_specs=FLUX_SPECS + [one(2 * TILES, 8, 128)],
        out_shape=FLUX_SHAPES + [f32(INST, 2 * TILES, 8, 128)],
        scratch_shapes=[pltpu.VMEM((TILES * F, 8, 128), jnp.float32)],
        compiler_params=params(),
        cost_estimate=cost(10**7, 7 * 10**6),
    )(got)


def rim(t, f, above, below, left, right):
    row, lane = rows_iota(), lanes_iota()
    total = jnp.where(row == 0, above[0, f, t : t + 1, :], 0.0)
    total = total + jnp.where(row == 7, below[0, f, t : t + 1, :], 0.0)
    if t == 0:
        total = total + jnp.where(lane == 0, jnp.broadcast_to(left[0, :, f : f + 1], (8, 128)), 0.0)
    if t == TILES - 1:
        total = total + jnp.where(lane == 127, jnp.broadcast_to(right[0, :, f : f + 1], (8, 128)), 0.0)
    return total


def second_kernel(most, scales, coupling, above, below, before, after,
                  psi, inner, top, bottom, left, right, held):
    for t in range(TILES):
        scale = scales[0, t]
        for f in range(F):
            psi[0, t * F + f] = most[0, t * F + f] + scale * rim(t, f, above, below, before, after)
    fluxes(
        lambda t, f: psi[0, t * F + f],
        lambda t: scales[0, TILES + t],
        coupling[0, 0],
        inner, top, bottom, left, right, held,
    )


HALO_SPECS = [one(F, 8, 128), one(F, 8, 128), one(8, 128), one(8, 128)]


def second_fluxes(most, scales, got, halo):
    return pl.pallas_call(
        second_kernel,
        grid=(INST,),
        in_specs=[
            one(TILES * F, 8, 128),
            one(2 * TILES, 8, 128),
            pl.BlockSpec((1, 1, 8, 128), lambda i: (i, TILES * PLANES, 0, 0)),
        ] + HALO_SPECS,
        out_specs=[one(TILES * F, 8, 128)] + FLUX_SPECS,
        out_shape=[f32(INST, TILES * F, 8, 128)] + FLUX_SHAPES,
        scratch_shapes=[pltpu.VMEM((TILES * F, 8, 128), jnp.float32)],
        compiler_params=params(),
        cost_estimate=cost(10**7, 7 * 10**6),
    )(most, scales, got, *halo)


def spectral(psi):
    def at(j):
        return (psi[j], 1) if j < INST else (psi[j - INST], -1)

    totals = []
    for i in range(INST):
        total = None
        for d in (1, 2, 3):
            (x, p), (y, q) = at(i + d), at(i + INST - d)
            pair = x + y if p == q else x - y
            sign = p
            term = (sign * HALF_SPEC[d]) * pair
            total = term if total is None else total + term
        x, p = at(i + 4)
        totals.append(total + (p * HALF_SPEC[4]) * x)
    return totals


def most_kernel(got, psi, inner, most):
    for f in range(F):
        state = [psi[i, f] for i in range(INST)]
        coupled = spectral(state)
        for i in range(INST):
            change = got[i, F + f] + inner[i, f] - coupled[i]
            most[i, f] = 0.4 * state[i] + got[i, 12] * change


def most_of_sweep(got, psi, inner):
    tile = pl.BlockSpec((INST, F, 8, 128), lambda t: (0, t, 0, 0))
    planes = pl.BlockSpec((INST, PLANES, 8, 128), lambda t: (0, t, 0, 0))
    kernel = most_kernel
    if psi is None:
        kernel = lambda got, inner, most: most_kernel(got, got, inner, most)
    return pl.pallas_call(
        kernel,
        grid=(TILES,),
        in_specs=[planes] + ([] if psi is None else [tile]) + [tile],
        out_specs=tile,
        out_shape=f32(INST, TILES * F, 8, 128),
        compiler_params=params(),
        cost_estimate=cost(10**7, 8 * 10**6),
    )(*[got] + ([] if psi is None else [psi]) + [inner])


def halos(edges):
    top, bottom, left, right = edges
    up = [(i, (i + 1) % N_BLK) for i in range(N_BLK)]
    down = [(j, i) for i, j in up]
    on = [(i, i + 1) for i in range(INST - 1)]
    back = [(j, i) for i, j in on]
    above = lax.ppermute(bottom, "blk", up)
    below = lax.ppermute(top, "blk", down)
    before = lax.ppermute(right, "inst", on)
    after = lax.ppermute(left, "inst", back)
    return above, below, before, after


def three_parts(x):
    a = x.astype(jnp.bfloat16)
    x = x - a.astype(jnp.float32)
    b = x.astype(jnp.bfloat16)
    x = x - b.astype(jnp.float32)
    return a, b, x.astype(jnp.bfloat16)


def last_kernel(count, most, psi, scales, above, below, before, after, list_cell, list_face,
                out, sums, found):
    i = pl.program_id(0)
    for t in range(TILES):
        scale = scales[0, t]
        for f in range(F):
            new = most[0, t * F + f] + scale * rim(t, f, above, below, before, after)
            out[i, t * F + f] = new
            both = new + psi[0, t * F + f]
            at = slice((t * F + f) * 8, (t * F + f) * 8 + 8)
            sums[at, :] = both
    groups = (count[0] + 127) // 128
    row = rows_iota()

    def pick(g, carry):
        cell = list_cell[pl.ds(g, 1), :]
        onehot = (rows_iota((128, 128)) == (cell & 127)).astype(jnp.bfloat16)
        lanes = jnp.concatenate([onehot] * 3, axis=0)
        state = jnp.concatenate(three_parts(sums[...]), axis=1)
        values = jnp.dot(state, lanes, preferred_element_type=jnp.float32)
        here = row == (cell >> 13)
        tile = (cell >> 7) & 7
        masks = [here & (tile == t) for t in range(TILES)]
        picked = jnp.zeros((8, 128), jnp.float32)
        for f in range(F):
            total = jnp.zeros((8, 128), jnp.float32)
            for t in range(TILES):
                at = (t * F + f) * 8
                total = jnp.where(masks[t], values[at : at + 8, :], total)
            total = jnp.sum(total, axis=0, keepdims=True)
            picked = jnp.where(row == f, total, picked)
        found[g, pl.ds(pl.multiple_of(i * 8, 8), 8), :] = picked
        return carry

    lax.fori_loop(0, groups, pick, 0)

    @pl.when(i == INST - 1)
    def _():
        for j in range(INST):
            for b in range(GROUPS):
                out[j, TILES * F + b] = jnp.zeros((8, 128), jnp.float32)

        def spread_out(g, carry):
            face = list_face[pl.ds(g, 1), :]
            parts = three_parts(found[g])
            for b in range(GROUPS):
                onehot = ((rows_iota((128, 128)) + b * 128) == face).astype(jnp.bfloat16)
                total = jnp.zeros((INST * 8, 128), jnp.float32)
                for part in parts:
                    total = total + lax.dot_general(
                        part, onehot, (((1,), (1,)), ((), ())),
                        preferred_element_type=jnp.float32)
                for j in range(INST):
                    at = TILES * F + b
                    out[j, at] = out[j, at] + total[j * 8 : j * 8 + 8, :]
            return carry

        lax.fori_loop(0, groups, spread_out, 0)


def last_state(count, most, psi, scales, halo, list_cell, list_face):
    block = one(TILES * F, 8, 128)
    faces = full((GROUPS, 128))
    shape = (INST, TILES * F + GROUPS, 8, 128)
    return pl.pallas_call(
        last_kernel,
        grid=(INST,),
        in_specs=[pl.BlockSpec(memory_space=pltpu.SMEM), block, block,
                  one(2 * TILES, 8, 128)] + HALO_SPECS + [faces, faces],
        out_specs=full(shape),
        out_shape=f32(*shape),
        scratch_shapes=[
            pltpu.VMEM((TILES * F * 8, 128), jnp.float32),
            pltpu.VMEM((GROUPS, INST * 8, 128), jnp.float32),
        ],
        compiler_params=params(),
        cost_estimate=cost(10**8, 7 * 10**6),
    )(count, most, psi, scales, *halo, list_cell.reshape(GROUPS, 128), list_face.reshape(GROUPS, 128))


def unpack_kernel(got, psi):
    for t in range(TILES):
        for f in range(F):
            psi[0, f, :, t * 128 : (t + 1) * 128] = got[0, t * F + f]


def unpack(got):
    return pl.pallas_call(
        unpack_kernel,
        grid=(INST,),
        in_specs=[one(TILES * F + GROUPS, 8, 128)],
        out_specs=pl.BlockSpec((1, F, 8, 1024), lambda c: (0, 0, 0, c)),
        out_shape=f32(1, F, 8, 8192),
        compiler_params=params(),
        cost_estimate=cost(10**6, 4 * 10**6),
    )(got)


def slots_kernel(got, geometry, slot, node, out):
    row = rows_iota()
    total = jnp.zeros((N_BLK * 8, 128), jnp.float32)
    for b in range(GROUPS):
        cols = slice(b * 128, (b + 1) * 128)
        picked = got[0, b]
        for c in range(1, INST):
            picked = picked + got[c, b]
        values = jnp.broadcast_to(node[:, cols].astype(jnp.float32), (8, 128))
        for k in range(3):
            part = jnp.sum(geometry[k * F : (k + 1) * F, cols] * picked[0:F, :], axis=0, keepdims=True)
            values = jnp.where((row >> 1) == k, part, values)
        place = slot[:, cols]
        half = (row & 1) == ((place >> 7) & 1)
        owner = place >> 8
        values = jnp.where(half, values, 0.0)
        rows = jnp.concatenate(
            [jnp.where(owner == d, values, 0.0) for d in range(N_BLK)], axis=0)
        onehot = (rows_iota((128, 128)) == (place & 127)).astype(jnp.bfloat16)
        for part in three_parts(rows):
            total = total + lax.dot_general(
                part, onehot, (((1,), (1,)), ((), ())), preferred_element_type=jnp.float32)
    for i in range(INST):
        for d in range(N_BLK):
            out[i * N_BLK + d] = total[d * 8 : d * 8 + 8, :]


def pack_slots(got, geometry, slot, node):
    return pl.pallas_call(
        slots_kernel,
        grid=(1,),
        in_specs=[pl.BlockSpec((INST, GROUPS, 8, 128), lambda _: (0, 3, 0, 0)),
                  full((3 * F, FACES)), full((1, FACES)), full((1, FACES))],
        out_specs=full((INST * N_BLK, 8, 128)),
        out_shape=f32(INST * N_BLK, 8, 128),
        compiler_params=params(),
        cost_estimate=cost(10**8, 2 * 10**6),
    )(got, geometry, slot.reshape(1, FACES), node.reshape(1, FACES))


def nodes_kernel(got, out):
    total = jnp.zeros((96, 128), jnp.float32)
    for b in range(N_BLK):
        values = got[b]
        for i in range(1, INST):
            values = values + got[i * N_BLK + b]
        nodes = got[b].astype(jnp.int32)
        for half in range(2):
            node = nodes[6 + half : 7 + half, :]
            high = rows_iota((32, 128)) == (node >> 7)
            rows = jnp.concatenate(
                [jnp.where(high, values[k * 2 + half : k * 2 + half + 1, :], 0.0) for k in range(3)],
                axis=0)
            onehot = (rows_iota((128, 128)) == (node & 127)).astype(jnp.bfloat16)
            for part in three_parts(rows):
                total = total + lax.dot_general(
                    part, onehot, (((1,), (1,)), ((), ())), preferred_element_type=jnp.float32)
    for k in range(3):
        for h in range(32):
            out[k : k + 1, h * 128 : (h + 1) * 128] = total[k * 32 + h : k * 32 + h + 1, :]


def to_nodes(got):
    return pl.pallas_call(
        nodes_kernel,
        in_specs=[pl.BlockSpec(memory_space=pltpu.VMEM)],
        out_specs=pl.BlockSpec(memory_space=pltpu.VMEM),
        out_shape=f32(3, NODE_DEV),
        compiler_params=params(),
        cost_estimate=cost(10**8, 10**6),
    )(got)


def local(psi_start, coupling, center, spread, source, wall_geo, wall_cell, wall_dest, wall_node):
    chunk = lax.axis_index("inst").astype(jnp.int32).reshape(1)
    sent = pack(psi_start[0], source[0], center[0], spread[0], coupling)
    got = lax.all_to_all(sent, "inst", 0, 0, tiled=True)
    list_cell, list_face, slot, count = sort_faces(wall_cell, wall_dest[:, 0], chunk)

    inner, *edges, scales = first_fluxes(got)
    halo = halos(edges)
    most = most_of_sweep(got, None, inner)
    psi, inner, *edges = second_fluxes(most, scales, got, halo)
    halo = halos(edges)
    most = most_of_sweep(got, psi, inner)
    back = last_state(count, most, psi, scales, halo, list_cell, list_face)

    home = lax.all_to_all(back, "inst", 0, 0, tiled=True)
    slots = pack_slots(home, wall_geo[0], slot, wall_node)
    owned = lax.all_to_all(slots, ("inst", "blk"), 0, 0, tiled=True)
    return unpack(home), to_nodes(owned)


def solution(mesh):
    placed = (
        P("inst", None, "blk", None),
        P("inst", None, None),
        P("inst", "blk", None),
        P("inst", "blk", None),
        P("inst", None, "blk", None),
        P("inst", None, "blk"),
        P("blk"),
        P("blk", None),
        P("blk"),
    )
    return jax.shard_map(
        local,
        mesh=mesh,
        in_specs=placed,
        out_specs=(P("inst", None, "blk", None), P(None, "blk")),
        check_vma=False,
    )
```

time: 812 us -> 183 us (0.23)
  the two profiles are of different devices: /device:TPU:12 before, /device:TPU:1 now
where the time goes in v1:
time: 183 us; the launch traced here: 181 us
  blocking collectives  50.4 us (28%)
  Pallas kernels  46 us (25%)
  starting transfers between devices  37.3 us (20%)
  waiting for transfers between devices  35.5 us (19%)
  local copies, waits for them, and re-layouts  11.4 us (6%)
    all_to_all x1, blocking collectives, local(): got = lax.all_to_all(sent, 'inst', 0, 0, tiled=True)  50.4 us
    all_to_all x1, waiting for transfers between devices, local(): home = lax.all_to_all(back, 'inst', 0, 0, tiled=True)  22.3 us
    pallas_call x1, Pallas kernels, sort_faces(): pl.pallas_call(faces_kernel, in_specs=[smem] * 3, out_specs=[smem] * 4, o...  19.9 us
    all_to_all x1, starting transfers between devices, local(): owned = lax.all_to_all(slots, ('inst', 'blk'), 0, 0, tiled=True)  12.1 us
    unnamed x30, local copies, waits for them, and re-layouts  11.4 us
    all_to_all x1, waiting for transfers between devices, local(): owned = lax.all_to_all(slots, ('inst', 'blk'), 0, 0, tiled=True)  10.8 us
    ppermute x2, starting transfers between devices, halos(): above = lax.ppermute(bottom, 'blk', up)  8.84 us
    all_to_all x1, starting transfers between devices, local(): home = lax.all_to_all(back, 'inst', 0, 0, tiled=True)  8.2 us
  transfers between devices with their start and end apart: 10, of which 3 were waited for; matrix products, arithmetic and copies ran while one was open for 0% of the time, Pallas kernels for 14%

profile of v1, /device:TPU:1, one launch (start us, length us, event | category | flops | bytes accessed | tf_op | source)
XLA Modules:
  0.0 181.4 jit_solution(17573767352885122886)
XLA Ops:
  0.6 0.7 copy.11.coupling
  1.3 0.0 copy-start.5
  1.3 1.4 copy-done.5
  2.7 0.0 copy-start.6
  2.7 1.4 copy-done.6
  4.1 0.0 copy-start.7
  4.1 0.9 copy-done.7
  5.1 0.0 copy-start.8
  5.1 0.9 copy-done.8
  6.0 0.7 shard_map.105
  6.7 50.4 %all_to_all.15.got.coupling = f32[8,113,8,128]{3,2,1,0:T(8,128)S(1)} all-to-all(f32[8,113,8,128]{3,2,1,0:T(8,128)S(1)} %shard_map.105), channel_id=1, replica_groups=mesh['inst'=8,'blk'=16] {'inst'}, dimensions={0} | all-to-all | bytes 7405568 | tf_op jit(solution)/shard_map/all_to_all | solution.py:475
  57.1 0.0 copy-start
  57.1 3.1 %shard_map.106 = (f32[8,48,8,128]{3,2,1,0:T(8,128)S(1)}, f32[8,6,8,128]{3,2,1,0:T(8,128)S(1)}, f32[8,6,8,128]{3,2,1,0:T(8,128)S(1)}, f32[8,8,128]{2,1,0:T(8,128)...) custom-call(f32[8,113,8,128]{3,2,1,0:T(8,128)S(1)} %all_to_all.15.got.coupling), custom_call_target="tpu_custom_call" | custom-call | flops 10000000 | bytes 7000000 | tf_op jit(solution)/shard_map/pallas_call | solution.py:179
  60.2 4.3 %collective-permute-start = (f32[8,6,8,128]{3,2,1,0:T(8,128)S(1)}, f32[8,6,8,128]{3,2,1,0:T(8,128)S(1)}, u32[]{:S(2)}, u32[]{:S(2)}) collective-permute-start(f32[8,6,8,128]{3,2,1,0:T(8,128)S(1)} %get-tuple-element.21), channel_id=1, source_target_pairs={{0,1},{1,2},{2,3},{3,4},{4,5},{5,6},{6,7},{7,8},{8,9},{9,10},{10,1... | collective-permute-start | bytes 589832 | tf_op jit(solution)/shard_map/ppermute | solution.py:286
  64.5 0.0 collective-permute-start.1
  64.5 1.8 %collective-permute-start.2 = (f32[8,8,128]{2,1,0:T(8,128)S(1)}, f32[8,8,128]{2,1,0:T(8,128)S(1)}, u32[]{:S(2)}, u32[]{:S(2)}) collective-permute-start(f32[8,8,128]{2,1,0:T(8,128)S(1)} %get-tuple-element.23), channel_id=1, source_target_pairs={{0,16},{16,32},{32,48},{48,64},{64,80},{80,96},{96,112},{1,17},{17... | collective-permute-start | bytes 98312 | tf_op jit(solution)/shard_map/ppermute | solution.py:288
  66.3 1.3 collective-permute-start.3
  67.6 1.6 shard_map.107.most
  69.2 0.0 collective-permute-done.2.before
  69.2 2.4 %collective-permute-done.3.after = f32[8,8,128]{2,1,0:T(8,128)S(1)} collective-permute-done((f32[8,8,128]{2,1,0:T(8,128)S(1)}, f32[8,8,128]{2,1,0:T(8,128)S(1)}, u32[]{:S(2)}, u32[]{:S(2)}) %collective-permute-start.3) | collective-permute-done | bytes 32800 | tf_op jit(solution)/shard_map/ppermute | solution.py:289
  71.7 0.0 collective-permute-done.above
  71.7 0.0 collective-permute-done.1.below
  71.7 0.0 copy-done
  71.7 3.3 %shard_map.108 = (f32[8,48,8,128]{3,2,1,0:T(8,128)S(1)}, f32[8,48,8,128]{3,2,1,0:T(8,128)S(1)}, f32[8,6,8,128]{3,2,1,0:T(8,128)S(1)}, f32[8,6,8,128]{3,2,1,0:T(8...) custom-call(f32[8,48,8,128]{3,2,1,0:T(8,128)S(1)} %shard_map.107.most, ...), custom_call_target="tpu_custom_call" | custom-call | flops 10000000 | bytes 7000000 | tf_op jit(solution)/shard_map/pallas_call | solution.py:220
  75.0 0.0 copy-start.3
  75.0 1.1 copy-done.3
  76.1 4.6 %collective-permute-start.4 = (f32[8,6,8,128]{3,2,1,0:T(8,128)S(1)}, f32[8,6,8,128]{3,2,1,0:T(8,128)S(1)}, u32[]{:S(2)}, u32[]{:S(2)}) collective-permute-start(f32[8,6,8,128]{3,2,1,0:T(8,128)S(1)} %get-tuple-element.27), channel_id=1, source_target_pairs={{0,1},{1,2},{2,3},{3,4},{4,5},{5,6},{6,7},{7,8},{8,9},{9,10},{10,1... | collective-permute-start | bytes 589832 | tf_op jit(solution)/shard_map/ppermute | solution.py:286
  80.7 0.0 collective-permute-start.5
  80.7 3.7 %collective-permute-start.6 = (f32[8,8,128]{2,1,0:T(8,128)S(1)}, f32[8,8,128]{2,1,0:T(8,128)S(1)}, u32[]{:S(2)}, u32[]{:S(2)}) collective-permute-start(f32[8,8,128]{2,1,0:T(8,128)S(1)} %get-tuple-element.29), channel_id=1, source_target_pairs={{0,16},{16,32},{32,48},{48,64},{64,80},{80,96},{96,112},{1,17},{17... | collective-permute-start | bytes 98312 | tf_op jit(solution)/shard_map/ppermute | solution.py:288
  84.4 1.3 collective-permute-start.7
  85.7 19.9 %shard_map.104 = (s32[2048]{0:T(1024)}, s32[2048]{0:T(1024)}, s32[2048]{0:T(1024)}, s32[1]{0:T(128)}) custom-call(s32[2048]{0:T(1024)} %cell.1, s32[2048]{0:T(1024)} %bitcast.22, s32[1]{0:T(128)} %bitcast.1.chunk), custom_call_target="tpu_custom_call" | custom-call | flops 1000000000 | bytes 10000000 | tf_op jit(solution)/shard_map/pallas_call | solution.py:109
  105.6 0.0 copy-start.1
  105.6 2.0 %copy-done.1 = f32[8,113,8,128]{3,2,1,0:T(8,128)S(1)} copy-done((f32[8,113,8,128]{3,2,1,0:T(8,128)S(1)}, f32[8,113,8,128]{3,2,1,0:T(8,128)}, u32[]{:S(2)}) %copy-start.1) | copy-done | bytes 3702808
  107.7 0.0 copy-start.4
  107.7 1.4 copy-done.4
  109.1 0.0 copy-start.11
  109.1 0.0 copy-start.12
  109.1 1.7 shard_map.109.most
  110.8 0.0 collective-permute-done.6.before
  110.8 0.0 collective-permute-done.7.after
  110.8 0.0 collective-permute-done.4.above
  110.8 0.0 collective-permute-done.5.below
  110.8 0.0 copy-done.11
  110.9 0.0 copy-done.12
  110.9 7.9 %shard_map.110 = f32[8,64,8,128]{3,2,1,0:T(8,128)S(1)} custom-call(s32[1]{0:T(128)} %get-tuple-element.18.count, f32[8,48,8,128]{3,2,1,0:T(8,128)S(1)} %shard_map.109.most, f32[8,48,8,128]{3,2,1,0:T(8,128)S(1)} %get-tuple-element.25.psi, f32[8,16,8,128]{3,2,1,0:T(8,128)S(1)} %get-tuple-element.20.scales, f32[8,6,8,128]{3,2,1,0:T(8,128)S(1)} %collective-permute-done.4.above, ...), custom_call_target="tpu_custom_call" | custom-call | flops 100000000 | bytes 7000000 | tf_op jit(solution)/shard_map/pallas_call | solution.py:365
  118.8 0.0 copy-start.2
  118.8 1.3 copy-done.2
  120.1 0.0 copy-start.13
  120.1 0.0 copy-start.9
  120.1 0.0 copy-start.10
  120.1 8.2 %all-to-all-start.1 = ((f32[8,64,8,128]{3,2,1,0:T(8,128)}), f32[8,64,8,128]{3,2,1,0:T(8,128)S(1)}, u32[]{:S(2)}, u32[]{:S(2)}) async-start(f32[8,64,8,128]{3,2,1,0:T(8,128)} %copy-done.2), calls=%async_computation.1 | async-start | bytes 4194304 | tf_op jit(solution)/shard_map/all_to_all | solution.py:486
  128.3 0.0 copy-done.13
  128.3 0.1 copy.14
  128.4 22.3 %all-to-all-done.1.got = f32[8,64,8,128]{3,2,1,0:T(8,128)S(1)} async-done(((f32[8,64,8,128]{3,2,1,0:T(8,128)}), f32[8,64,8,128]{3,2,1,0:T(8,128)S(1)}, u32[]{:S(2)}, u32[]{:S(2)}) %all-to-all-start.1) | async-done | bytes 2097184 | tf_op jit(solution)/shard_map/all_to_all | solution.py:486
  150.7 0.0 copy-done.9
  150.7 0.0 copy-done.10
  150.7 2.0 %shard_map.112 = f32[128,8,128]{2,1,0:T(8,128)} custom-call(f32[8,64,8,128]{3,2,1,0:T(8,128)S(1)} %all-to-all-done.1.got, f32[18,2048]{1,0:T(8,128)S(1)} %bitcast.15, s32[1,2048]{1,0:T(1,128)S(1)} %bitcast.19, s32[1,2048]{1,0:T(1,128)S(1)} %bitcast.18), custom_call_target="tpu_custom_call" | custom-call | flops 100000000 | bytes 2000000 | tf_op jit(solution)/shard_map/pallas_call | solution.py:427
  152.7 12.1 %all-to-all-start.2 = ((f32[128,8,128]{2,1,0:T(8,128)}), f32[128,8,128]{2,1,0:T(8,128)S(1)}, u32[]{:S(2)}, u32[]{:S(2)}) async-start(f32[128,8,128]{2,1,0:T(8,128)} %shard_map.112), calls=%async_computation.2 | async-start | bytes 1048576 | tf_op jit(solution)/shard_map/all_to_all | solution.py:488
  164.8 2.8 %shard_map.111 = f32[1,6,8,8192]{3,2,1,0:T(8,128)} custom-call(f32[8,64,8,128]{3,2,1,0:T(8,128)S(1)} %all-to-all-done.1.got), custom_call_target="tpu_custom_call" | custom-call | flops 1000000 | bytes 4000000 | tf_op jit(solution)/shard_map/pallas_call | solution.py:388
  167.7 10.8 %all-to-all-done.2.got = f32[128,8,128]{2,1,0:T(8,128)S(1)} async-done(((f32[128,8,128]{2,1,0:T(8,128)}), f32[128,8,128]{2,1,0:T(8,128)S(1)}, u32[]{:S(2)}, u32[]{:S(2)}) %all-to-all-start.2) | async-done | bytes 524320 | tf_op jit(solution)/shard_map/all_to_all | solution.py:488
  178.5 2.9 %shard_map.113 = f32[3,4096]{1,0:T(4,128)} custom-call(f32[128,8,128]{2,1,0:T(8,128)S(1)} %all-to-all-done.2.got), custom_call_target="tpu_custom_call" | custom-call | flops 100000000 | bytes 1000000 | tf_op jit(solution)/shard_map/pallas_call | solution.py:462
Async XLA Ops:
  1.3 1.4 copy-start.5
  2.7 1.4 copy-start.6
  4.1 0.9 copy-start.7
  5.1 0.9 copy-start.8
  57.1 14.6 %copy-start = (f32[8,113,8,128]{3,2,1,0:T(8,128)}, f32[8,113,8,128]{3,2,1,0:T(8,128)S(1)}, u32[]{:S(2)}) copy-start(f32[8,113,8,128]{3,2,1,0:T(8,128)S(1)} %all_to_all.15.got.coupling) | copy-start | bytes 11108356
  60.2 11.5 %collective-permute-start = (f32[8,6,8,128]{3,2,1,0:T(8,128)S(1)}, f32[8,6,8,128]{3,2,1,0:T(8,128)S(1)}, u32[]{:S(2)}, u32[]{:S(2)}) collective-permute-start(f32[8,6,8,128]{3,2,1,0:T(8,128)S(1)} %get-tuple-element.21), channel_id=1, source_target_pairs={{0,1},{1,2},{2,3},{3,4},{4,5},{5,6},{6,7},{7,8},{8,9},{9,10},{10,1... | collective-permute-start | bytes 589832 | tf_op jit(solution)/shard_map/ppermute | solution.py:286
  64.5 7.2 %collective-permute-start.1 = (f32[8,6,8,128]{3,2,1,0:T(8,128)S(1)}, f32[8,6,8,128]{3,2,1,0:T(8,128)S(1)}, u32[]{:S(2)}, u32[]{:S(2)}) collective-permute-start(f32[8,6,8,128]{3,2,1,0:T(8,128)S(1)} %get-tuple-element.22), channel_id=1, source_target_pairs={{1,0},{2,1},{3,2},{4,3},{5,4},{6,5},{7,6},{8,7},{9,8},{10,9},{11,1... | collective-permute-start | bytes 589832 | tf_op jit(solution)/shard_map/ppermute | solution.py:287
  64.5 4.8 %collective-permute-start.2 = (f32[8,8,128]{2,1,0:T(8,128)S(1)}, f32[8,8,128]{2,1,0:T(8,128)S(1)}, u32[]{:S(2)}, u32[]{:S(2)}) collective-permute-start(f32[8,8,128]{2,1,0:T(8,128)S(1)} %get-tuple-element.23), channel_id=1, source_target_pairs={{0,16},{16,32},{32,48},{48,64},{64,80},{80,96},{96,112},{1,17},{17... | collective-permute-start | bytes 98312 | tf_op jit(solution)/shard_map/ppermute | solution.py:288
  66.3 5.4 %collective-permute-start.3 = (f32[8,8,128]{2,1,0:T(8,128)S(1)}, f32[8,8,128]{2,1,0:T(8,128)S(1)}, u32[]{:S(2)}, u32[]{:S(2)}) collective-permute-start(f32[8,8,128]{2,1,0:T(8,128)S(1)} %get-tuple-element.24), channel_id=1, source_target_pairs={{16,0},{32,16},{48,32},{64,48},{80,64},{96,80},{112,96},{17,1},{33... | collective-permute-start | bytes 98312 | tf_op jit(solution)/shard_map/ppermute | solution.py:289
  75.0 1.1 copy-start.3
  76.1 34.7 %collective-permute-start.4 = (f32[8,6,8,128]{3,2,1,0:T(8,128)S(1)}, f32[8,6,8,128]{3,2,1,0:T(8,128)S(1)}, u32[]{:S(2)}, u32[]{:S(2)}) collective-permute-start(f32[8,6,8,128]{3,2,1,0:T(8,128)S(1)} %get-tuple-element.27), channel_id=1, source_target_pairs={{0,1},{1,2},{2,3},{3,4},{4,5},{5,6},{6,7},{7,8},{8,9},{9,10},{10,1... | collective-permute-start | bytes 589832 | tf_op jit(solution)/shard_map/ppermute | solution.py:286
  80.7 30.2 %collective-permute-start.5 = (f32[8,6,8,128]{3,2,1,0:T(8,128)S(1)}, f32[8,6,8,128]{3,2,1,0:T(8,128)S(1)}, u32[]{:S(2)}, u32[]{:S(2)}) collective-permute-start(f32[8,6,8,128]{3,2,1,0:T(8,128)S(1)} %get-tuple-element.28), channel_id=1, source_target_pairs={{1,0},{2,1},{3,2},{4,3},{5,4},{6,5},{7,6},{8,7},{9,8},{10,9},{11,1... | collective-permute-start | bytes 589832 | tf_op jit(solution)/shard_map/ppermute | solution.py:287
  80.7 30.1 %collective-permute-start.6 = (f32[8,8,128]{2,1,0:T(8,128)S(1)}, f32[8,8,128]{2,1,0:T(8,128)S(1)}, u32[]{:S(2)}, u32[]{:S(2)}) collective-permute-start(f32[8,8,128]{2,1,0:T(8,128)S(1)} %get-tuple-element.29), channel_id=1, source_target_pairs={{0,16},{16,32},{32,48},{48,64},{64,80},{80,96},{96,112},{1,17},{17... | collective-permute-start | bytes 98312 | tf_op jit(solution)/shard_map/ppermute | solution.py:288
  84.4 26.4 %collective-permute-start.7 = (f32[8,8,128]{2,1,0:T(8,128)S(1)}, f32[8,8,128]{2,1,0:T(8,128)S(1)}, u32[]{:S(2)}, u32[]{:S(2)}) collective-permute-start(f32[8,8,128]{2,1,0:T(8,128)S(1)} %get-tuple-element.30), channel_id=1, source_target_pairs={{16,0},{32,16},{48,32},{64,48},{80,64},{96,80},{112,96},{17,1},{33... | collective-permute-start | bytes 98312 | tf_op jit(solution)/shard_map/ppermute | solution.py:289
  105.6 2.0 %copy-start.1 = (f32[8,113,8,128]{3,2,1,0:T(8,128)S(1)}, f32[8,113,8,128]{3,2,1,0:T(8,128)}, u32[]{:S(2)}) copy-start(f32[8,113,8,128]{3,2,1,0:T(8,128)} %copy-done) | copy-start | bytes 11108356
  107.7 1.4 copy-start.4
  109.1 1.8 copy-start.11
  109.1 1.8 copy-start.12
  118.8 1.4 copy-start.2
  120.1 8.2 %copy-start.13 = (f32[1,18,2048]{2,0,1:T(1,128)S(1)}, f32[1,18,2048]{2,0,1:T(1,128)}, u32[]{:S(2)}) copy-start(f32[1,18,2048]{2,0,1:T(1,128)} %param.14) | copy-start | bytes 442372
  120.1 30.5 %copy-start.9 = (s32[2048]{0:T(1024)S(1)}, s32[2048]{0:T(1024)}, u32[]{:S(2)}) copy-start(s32[2048]{0:T(1024)} %param.17) | copy-start | bytes 24580
  120.1 30.5 %copy-start.10 = (s32[2048]{0:T(1024)S(1)}, s32[2048]{0:T(1024)}, u32[]{:S(2)}) copy-start(s32[2048]{0:T(1024)} %get-tuple-element.33) | copy-start | bytes 24580
  120.1 30.5 %all-to-all-start.1 = ((f32[8,64,8,128]{3,2,1,0:T(8,128)}), f32[8,64,8,128]{3,2,1,0:T(8,128)S(1)}, u32[]{:S(2)}, u32[]{:S(2)}) async-start(f32[8,64,8,128]{3,2,1,0:T(8,128)} %copy-done.2), calls=%async_computation.1 | async-start | bytes 4194304 | tf_op jit(solution)/shard_map/all_to_all | solution.py:486
  152.7 25.8 %all-to-all-start.2 = ((f32[128,8,128]{2,1,0:T(8,128)}), f32[128,8,128]{2,1,0:T(8,128)S(1)}, u32[]{:S(2)}, u32[]{:S(2)}) async-start(f32[128,8,128]{2,1,0:T(8,128)} %shard_map.112), calls=%async_computation.2 | async-start | bytes 1048576 | tf_op jit(solution)/shard_map/all_to_all | solution.py:488

commit v2 on v1

v2 whole, which is shorter than its diff:
```python
import math

import jax
import jax.numpy as jnp
from jax import lax
from jax.experimental import pallas as pl
from jax.experimental.pallas import tpu as pltpu
from jax.sharding import PartitionSpec as P

CAP = 256
NODE_DEV = 4096
INST = 8
N_BLK = 16
F = 6
PLANES = 14
TILES = 8
FACES = 2048
GROUPS = FACES // 128
VMEM = 16 * 1024 * 1024
SENT = TILES * PLANES + 1

HALF_SPEC = [0.0] + [
    0.25 * (-1.0) ** d / math.sin(math.pi * d / INST) for d in range(1, INST)
]


def params(limit=VMEM):
    return pltpu.CompilerParams(vmem_limit_bytes=limit)


def cost(flops, nbytes):
    return pl.CostEstimate(flops=flops, bytes_accessed=nbytes, transcendentals=0)


def rows_iota(shape=(8, 128)):
    return lax.broadcasted_iota(jnp.int32, shape, 0)


def lanes_iota(shape=(8, 128)):
    return lax.broadcasted_iota(jnp.int32, shape, 1)


def full(shape):
    return pl.BlockSpec(shape, lambda *_: (0,) * len(shape))


def one(*shape):
    return pl.BlockSpec((1,) + shape, lambda i: (i,) + (0,) * len(shape))


def f32(*shape):
    return jax.ShapeDtypeStruct(shape, jnp.float32)


def tiled(x):
    x = x.reshape(x.shape[:-1] + (INST * TILES, 128))
    return jnp.swapaxes(x, -3, -2)


def pack_kernel(flip, psi, source, center, spread, coupling, out, flat, held, sems, more):
    def tiles_of(d):
        return pl.ds((d ^ flip[0]) * TILES, TILES)

    def load(d, n):
        start = (psi if n < F else source).at[n % F, tiles_of(d)]
        return pltpu.make_async_copy(start, held.at[d, pl.ds(n * TILES, TILES)], sems.at[d, n])

    def send(d):
        return pltpu.make_async_copy(held.at[d], out.at[d], more.at[2 + d])

    flats = [
        pltpu.make_async_copy(center, flat.at[0], more.at[0]),
        pltpu.make_async_copy(spread, flat.at[1], more.at[1]),
    ]
    for copy in flats:
        copy.start()
    for d in range(INST):
        for n in range(2 * F):
            load(d, n).start()
    for copy in flats:
        copy.wait()
    for d in range(INST):
        at = 2 * F * TILES
        held[d, at : at + TILES] = 0.6 / flat[0, tiles_of(d)]
        held[d, at + TILES : at + 2 * TILES] = flat[1, tiles_of(d)]
        held[d, SENT - 1] = jnp.zeros((8, 128), jnp.float32)
        held[d, SENT - 1, 0:F, 0:F] = coupling[0]
        for n in range(2 * F):
            load(d, n).wait()
        send(d).start()
    for d in range(INST):
        send(d).wait()


def pack(psi, source, center, spread, coupling, flip):
    vmem = pl.BlockSpec(memory_space=pltpu.VMEM)
    anywhere = pl.BlockSpec(memory_space=pl.ANY)
    return pl.pallas_call(
        pack_kernel,
        in_specs=[pl.BlockSpec(memory_space=pltpu.SMEM)] + [anywhere] * 4 + [vmem],
        out_specs=anywhere,
        out_shape=f32(INST, SENT, 8, 128),
        scratch_shapes=[
            pltpu.VMEM((2, INST * TILES, 8, 128), jnp.float32),
            pltpu.VMEM((INST, SENT, 8, 128), jnp.float32),
            pltpu.SemaphoreType.DMA((INST, 2 * F)),
            pltpu.SemaphoreType.DMA((2 + INST,)),
        ],
        compiler_params=params(60 * 1024 * 1024),
        cost_estimate=cost(10**6, 8 * 10**6),
    )(flip, tiled(psi), tiled(source), tiled(center), tiled(spread), coupling)


def faces_kernel(cell, dest, chunk, list_cell, list_face, slot, count, loads):
    for owner in range(N_BLK):
        loads[owner] = 0

    def step(face, found):
        here = cell[face]
        owner = dest[face]
        rank = loads[owner]
        slot[face] = owner * CAP + rank
        loads[owner] = rank + 1
        list_cell[found] = here
        list_face[found] = face
        mine = ((here & 8191) >> 10) == chunk[0]
        return found + mine.astype(jnp.int32)

    found = lax.fori_loop(0, FACES, step, jnp.int32(0))
    count[0] = found

    def fill(at, carry):
        list_cell[at] = 0
        list_face[at] = -1
        return carry

    lax.fori_loop(found, jnp.minimum(found + 128, FACES), fill, 0)


def sort_faces(cell, dest, chunk):
    smem = pl.BlockSpec(memory_space=pltpu.SMEM)
    ints = jax.ShapeDtypeStruct((FACES,), jnp.int32)
    return pl.pallas_call(
        faces_kernel,
        in_specs=[smem] * 3,
        out_specs=[smem] * 4,
        out_shape=[ints, ints, ints, jax.ShapeDtypeStruct((1,), jnp.int32)],
        scratch_shapes=[pltpu.SMEM((N_BLK,), jnp.int32)],
        compiler_params=pltpu.CompilerParams(vmem_limit_bytes=2**20),
        cost_estimate=cost(10**9, 10**7),
    )(cell, dest, chunk)


def fluxes(i, psi_of, spread_of, coupling, inner, top, bottom, left, right, held):
    row, lane = rows_iota(), lanes_iota()
    factor = [
        [jnp.broadcast_to(coupling[g : g + 1, f : f + 1], (8, 128)) for f in range(F)]
        for g in range(F)
    ]
    for t in range(TILES):
        psi = [psi_of(t, f) for f in range(F)]
        strength = spread_of(t)
        for f in range(F):
            total = factor[0][f] * psi[0]
            for g in range(1, F):
                total = total + factor[g][f] * psi[g]
            weighted = strength * total
            held[f * TILES + t] = weighted
            top[i, f, t : t + 1, :] = weighted[0:1, :]
            bottom[i, f, t : t + 1, :] = weighted[7:8, :]
    first = jnp.zeros((8, 128), jnp.float32)
    last = jnp.zeros((8, 128), jnp.float32)
    for f in range(F):
        tiles = [held[f * TILES + t] for t in range(TILES)]
        later = [pltpu.roll(x, 1, 1) for x in tiles]
        sooner = [pltpu.roll(x, 127, 1) for x in tiles]
        first = jnp.where(lane == f, jnp.broadcast_to(tiles[0][:, 0:1], (8, 128)), first)
        last = jnp.where(lane == f, jnp.broadcast_to(tiles[7][:, 127:128], (8, 128)), last)
        for t in range(TILES):
            before = later[t - 1] if t else jnp.zeros((8, 128), jnp.float32)
            after = sooner[t + 1] if t < TILES - 1 else jnp.zeros((8, 128), jnp.float32)
            total = jnp.where(lane == 0, before, later[t])
            total = total + jnp.where(lane == 127, after, sooner[t])
            total = total + jnp.where(row == 0, 0.0, pltpu.roll(tiles[t], 1, 0))
            total = total + jnp.where(row == 7, 0.0, pltpu.roll(tiles[t], 7, 0))
            inner[i, f * TILES + t] = total
    left[i] = first
    right[i] = last


def first_kernel(got, inner, top, bottom, left, right, psi, source, scales, held, sems):
    def loads(i, n):
        at = (0, F * TILES, 2 * F * TILES)[n]
        to = (psi, source, scales)[n]
        return pltpu.make_async_copy(got.at[i, pl.ds(at, to.shape[1])], to.at[i], sems.at[n, i])

    for i in range(INST):
        loads(i, 0).start()
        loads(i, 2).start()
    for i in range(INST):
        loads(i, 1).start()

    def step(i, carry):
        loads(i, 0).wait()
        loads(i, 2).wait()
        fluxes(
            i,
            lambda t, f: psi[i, f * TILES + t],
            lambda t: scales[i, TILES + t],
            scales[i, 2 * TILES],
            inner, top, bottom, left, right, held,
        )
        return carry

    lax.fori_loop(0, INST, step, 0)
    for i in range(INST):
        loads(i, 1).wait()


FLUX_SPECS = [one(TILES * F, 8, 128), one(F, 8, 128), one(F, 8, 128), one(8, 128), one(8, 128)]
FLUX_SHAPES = [
    f32(INST, TILES * F, 8, 128),
    f32(INST, F, 8, 128),
    f32(INST, F, 8, 128),
    f32(INST, 8, 128),
    f32(INST, 8, 128),
]


def first_fluxes(got):
    vmem = pl.BlockSpec(memory_space=pltpu.VMEM)
    state = f32(INST, TILES * F, 8, 128)
    return pl.pallas_call(
        first_kernel,
        in_specs=[pl.BlockSpec(memory_space=pl.ANY)],
        out_specs=[vmem] * 8,
        out_shape=FLUX_SHAPES + [state, state, f32(INST, 2 * TILES + 1, 8, 128)],
        scratch_shapes=[
            pltpu.VMEM((TILES * F, 8, 128), jnp.float32),
            pltpu.SemaphoreType.DMA((3, INST)),
        ],
        compiler_params=params(),
        cost_estimate=cost(10**7, 7 * 10**6),
    )(got)


def rim(t, f, above, below, left, right):
    row, lane = rows_iota(), lanes_iota()
    total = jnp.where(row == 0, above[0, f, t : t + 1, :], 0.0)
    total = total + jnp.where(row == 7, below[0, f, t : t + 1, :], 0.0)
    if t == 0:
        total = total + jnp.where(lane == 0, jnp.broadcast_to(left[0, :, f : f + 1], (8, 128)), 0.0)
    if t == TILES - 1:
        total = total + jnp.where(lane == 127, jnp.broadcast_to(right[0, :, f : f + 1], (8, 128)), 0.0)
    return total


def second_kernel(most, scales, above, below, before, after,
                  psi, inner, top, bottom, left, right, held):
    for t in range(TILES):
        scale = scales[0, t]
        for f in range(F):
            psi[0, f * TILES + t] = most[0, f * TILES + t] + scale * rim(t, f, above, below, before, after)
    fluxes(
        0,
        lambda t, f: psi[0, f * TILES + t],
        lambda t: scales[0, TILES + t],
        scales[0, 2 * TILES],
        inner, top, bottom, left, right, held,
    )


HALO_SPECS = [one(F, 8, 128), one(F, 8, 128), one(8, 128), one(8, 128)]


def second_fluxes(most, scales, halo):
    return pl.pallas_call(
        second_kernel,
        grid=(INST,),
        in_specs=[
            one(TILES * F, 8, 128),
            one(2 * TILES + 1, 8, 128),
        ] + HALO_SPECS,
        out_specs=[one(TILES * F, 8, 128)] + FLUX_SPECS,
        out_shape=[f32(INST, TILES * F, 8, 128)] + FLUX_SHAPES,
        scratch_shapes=[pltpu.VMEM((TILES * F, 8, 128), jnp.float32)],
        compiler_params=params(),
        cost_estimate=cost(10**7, 7 * 10**6),
    )(most, scales, *halo)


def spectral(psi):
    def at(j):
        return (psi[j], 1) if j < INST else (psi[j - INST], -1)

    totals = []
    for i in range(INST):
        total = None
        for d in (1, 2, 3):
            (x, p), (y, q) = at(i + d), at(i + INST - d)
            pair = x + y if p == q else x - y
            sign = p
            term = (sign * HALF_SPEC[d]) * pair
            total = term if total is None else total + term
        x, p = at(i + 4)
        totals.append(total + (p * HALF_SPEC[4]) * x)
    return totals


def most_kernel(psi, source, scale, inner, most):
    for t in range(TILES):
        state = [psi[i, t] for i in range(INST)]
        coupled = spectral(state)
        for i in range(INST):
            change = source[i, t] + inner[i, t] - coupled[i]
            most[i, t] = 0.4 * state[i] + scale[i, t] * change


def most_of_sweep(psi, source, scales, inner):
    field = pl.BlockSpec((INST, TILES, 8, 128), lambda f: (0, f, 0, 0))
    scale = pl.BlockSpec((INST, TILES, 8, 128), lambda f: (0, 0, 0, 0))
    return pl.pallas_call(
        most_kernel,
        grid=(F,),
        in_specs=[field, field, scale, field],
        out_specs=field,
        out_shape=f32(INST, TILES * F, 8, 128),
        compiler_params=params(),
        cost_estimate=cost(10**7, 8 * 10**6),
    )(psi, source, scales, inner)


def device(chunk, block):
    return (chunk ^ ((block >> 1) & 1)) * N_BLK + block


def halos(edges):
    top, bottom, left, right = edges
    axes = ("inst", "blk")
    places = [(c, b) for c in range(INST) for b in range(N_BLK)]
    up = [(device(c, b), device(c, (b + 1) % N_BLK)) for c, b in places]
    down = [(j, i) for i, j in up]
    on = [(device(c, b), device(c + 1, b)) for c, b in places if c + 1 < INST]
    back = [(j, i) for i, j in on]
    above = lax.ppermute(bottom, axes, up)
    below = lax.ppermute(top, axes, down)
    before = lax.ppermute(right, axes, on)
    after = lax.ppermute(left, axes, back)
    return above, below, before, after


def stacked(x):
    return jnp.concatenate(three_parts(x), axis=0)


def times_transposed(x, y):
    return lax.dot_general(x, y, (((1,), (1,)), ((), ())), preferred_element_type=jnp.float32)


def three_parts(x):
    a = x.astype(jnp.bfloat16)
    x = x - a.astype(jnp.float32)
    b = x.astype(jnp.bfloat16)
    x = x - b.astype(jnp.float32)
    return a, b, x.astype(jnp.bfloat16)


def last_kernel(count, faces, most, psi, scales, above, below, before, after, list_cell, list_face,
                out, *sums):
    i = pl.program_id(0)
    both = [[] for f in range(F)]
    for t in range(TILES):
        scale = scales[0, t]
        for f in range(F):
            new = most[0, f * TILES + t] + scale * rim(t, f, above, below, before, after)
            out[i, f * TILES + t] = new
            both[f].append(new + psi[0, f * TILES + t])
            if t % 2:
                rows = slice((f * TILES + t - 1) * 8, (f * TILES + t + 1) * 8)
                for part, value in zip(sums, three_parts(jnp.concatenate(both[f][-2:], axis=0))):
                    part[i, rows, :] = value

    @pl.when(i == INST - 1)
    def _():
        groups = (count[0] + 127) // 128
        row = rows_iota()
        for j in range(INST):
            for b in range(GROUPS):
                out[j, TILES * F + b] = jnp.zeros((8, 128), jnp.float32)

        def pick(g, carry):
            cell = list_cell[pl.ds(g, 1), :]
            onehot = (rows_iota((128, 128)) == (cell & 127)).astype(jnp.bfloat16)
            here = row == (cell >> 13)
            tile = (cell >> 7) & 7
            masks = [here & (tile == t) for t in range(TILES)]
            found = []
            for j in range(INST):
                taken = sum(
                    jnp.dot(part[j], onehot, preferred_element_type=jnp.float32) for part in sums)
                picked = jnp.zeros((8, 128), jnp.float32)
                for f in range(F):
                    total = jnp.zeros((8, 128), jnp.float32)
                    for t in range(TILES):
                        at = (f * TILES + t) * 8
                        total = jnp.where(masks[t], taken[at : at + 8, :], total)
                    total = jnp.sum(total, axis=0, keepdims=True)
                    picked = jnp.where(row == f, total, picked)
                found.append(picked)
            parts = jnp.concatenate(three_parts(jnp.concatenate(found, axis=0)), axis=0)
            face = list_face[pl.ds(g, 1), :]
            last = jnp.minimum(g * 128 + 127, count[0] - 1)

            def place(b, carry):
                onehot = ((rows_iota((128, 128)) + b * 128) == face).astype(jnp.bfloat16)
                total = lax.dot_general(
                    parts, onehot, (((1,), (1,)), ((), ())), preferred_element_type=jnp.float32)
                at = TILES * F + b
                for j in range(INST):
                    rows = [total[n : n + 8, :] for n in (j * 8, 64 + j * 8, 128 + j * 8)]
                    out[j, at] = out[j, at] + (rows[0] + rows[1] + rows[2])
                return carry

            lax.fori_loop(faces[g * 128] >> 7, (faces[last] >> 7) + 1, place, 0)
            return carry

        lax.fori_loop(0, groups, pick, 0)


def last_state(count, most, psi, scales, halo, list_cell, list_face):
    block = one(TILES * F, 8, 128)
    faces = full((GROUPS, 128))
    shape = (INST, TILES * F + GROUPS, 8, 128)
    return pl.pallas_call(
        last_kernel,
        grid=(INST,),
        in_specs=[pl.BlockSpec(memory_space=pltpu.SMEM)] * 2 + [block, block,
                  one(2 * TILES, 8, 128)] + HALO_SPECS + [faces, faces],
        out_specs=full(shape),
        out_shape=f32(*shape),
        scratch_shapes=[pltpu.VMEM((INST, TILES * F * 8, 128), jnp.bfloat16)] * 3,
        compiler_params=params(),
        cost_estimate=cost(10**8, 7 * 10**6),
    )(count, list_face, most, psi, scales, *halo, list_cell.reshape(GROUPS, 128), list_face.reshape(GROUPS, 128))


def unpack_kernel(flip, got, psi):
    for t in range(TILES):
        for f in range(F):
            psi[0, f, :, t * 128 : (t + 1) * 128] = got[0, f * TILES + t]


def unpack(got, flip):
    return pl.pallas_call(
        unpack_kernel,
        grid_spec=pltpu.PrefetchScalarGridSpec(
            num_scalar_prefetch=1,
            grid=(INST,),
            in_specs=[pl.BlockSpec((1, TILES * F, 8, 128), lambda d, flip: (d, 0, 0, 0))],
            out_specs=pl.BlockSpec((1, F, 8, 1024), lambda d, flip: (0, 0, 0, d ^ flip[0])),
        ),
        out_shape=f32(1, F, 8, 8192),
        compiler_params=params(),
        cost_estimate=cost(10**6, 4 * 10**6),
    )(flip, got)


def slots_kernel(got, geometry, slot, node, out):
    row = rows_iota()
    total = jnp.zeros((3 * N_BLK * 8, 128), jnp.float32)
    for b in range(GROUPS):
        cols = slice(b * 128, (b + 1) * 128)
        picked = got[0, b]
        for c in range(1, INST):
            picked = picked + got[c, b]
        values = jnp.broadcast_to(node[:, cols].astype(jnp.float32), (8, 128))
        for k in range(3):
            part = jnp.sum(geometry[k * F : (k + 1) * F, cols] * picked[0:F, :], axis=0, keepdims=True)
            values = jnp.where((row >> 1) == k, part, values)
        place = slot[:, cols]
        half = (row & 1) == ((place >> 7) & 1)
        owner = place >> 8
        values = jnp.where(half, values, 0.0)
        rows = jnp.concatenate(
            [jnp.where(owner == d, values, 0.0) for d in range(N_BLK)], axis=0)
        onehot = (rows_iota((128, 128)) == (place & 127)).astype(jnp.bfloat16)
        total = total + times_transposed(stacked(rows), onehot)
    total = total[0:128] + total[128:256] + total[256:384]
    for i in range(INST):
        for d in range(N_BLK):
            out[i * N_BLK + d] = total[d * 8 : d * 8 + 8, :]


def pack_slots(got, geometry, slot, node):
    return pl.pallas_call(
        slots_kernel,
        grid=(1,),
        in_specs=[pl.BlockSpec((INST, GROUPS, 8, 128), lambda _: (0, 3, 0, 0)),
                  full((3 * F, FACES)), full((1, FACES)), full((1, FACES))],
        out_specs=full((INST * N_BLK, 8, 128)),
        out_shape=f32(INST * N_BLK, 8, 128),
        compiler_params=params(),
        cost_estimate=cost(10**8, 2 * 10**6),
    )(got, geometry, slot.reshape(1, FACES), node.reshape(1, FACES))


def nodes_kernel(got, out):
    total = jnp.zeros((3 * 96, 128), jnp.float32)
    for b in range(N_BLK):
        values = got[b]
        for i in range(1, INST):
            values = values + got[i * N_BLK + b]
        nodes = got[b].astype(jnp.int32)
        for half in range(2):
            node = nodes[6 + half : 7 + half, :]
            high = rows_iota((32, 128)) == (node >> 7)
            rows = jnp.concatenate(
                [jnp.where(high, values[k * 2 + half : k * 2 + half + 1, :], 0.0) for k in range(3)],
                axis=0)
            onehot = (rows_iota((128, 128)) == (node & 127)).astype(jnp.bfloat16)
            total = total + times_transposed(stacked(rows), onehot)
    total = total[0:96] + total[96:192] + total[192:288]
    for k in range(3):
        for h in range(32):
            out[k : k + 1, h * 128 : (h + 1) * 128] = total[k * 32 + h : k * 32 + h + 1, :]


def to_nodes(got):
    return pl.pallas_call(
        nodes_kernel,
        in_specs=[pl.BlockSpec(memory_space=pltpu.VMEM)],
        out_specs=pl.BlockSpec(memory_space=pltpu.VMEM),
        out_shape=f32(3, NODE_DEV),
        compiler_params=params(),
        cost_estimate=cost(10**8, 10**6),
    )(got)


def local(psi_start, coupling, center, spread, source, wall_geo, wall_cell, wall_dest, wall_node):
    flip = ((lax.axis_index("blk").astype(jnp.int32) >> 1) & 1).reshape(1)
    chunk = lax.axis_index("inst").astype(jnp.int32).reshape(1) ^ flip
    sent = pack(psi_start[0], source[0], center[0], spread[0], coupling, flip)
    got = lax.all_to_all(sent, "inst", 0, 0, tiled=True)
    faces = sort_faces(wall_cell, wall_dest[:, 0], chunk)
    got, (list_cell, list_face, slot, count) = lax.optimization_barrier((got, faces))

    inner, *edges, psi, source, scales = first_fluxes(got)
    halo = halos(edges)
    most = most_of_sweep(psi, source, scales, inner)
    psi, inner, *edges = second_fluxes(most, scales, halo)
    halo = halos(edges)
    most = most_of_sweep(psi, source, scales, inner)
    back = last_state(count, most, psi, scales, halo, list_cell, list_face)

    home = lax.all_to_all(back, "inst", 0, 0, tiled=True)
    slots = pack_slots(home, wall_geo[0], slot, wall_node)
    owned = lax.all_to_all(slots, ("inst", "blk"), 0, 0, tiled=True)
    return unpack(home, flip), to_nodes(owned)


def solution(mesh):
    placed = (
        P("inst", None, "blk", None),
        P("inst", None, None),
        P("inst", "blk", None),
        P("inst", "blk", None),
        P("inst", None, "blk", None),
        P("inst", None, "blk"),
        P("blk"),
        P("blk", None),
        P("blk"),
    )
    return jax.shard_map(
        local,
        mesh=mesh,
        in_specs=placed,
        out_specs=(P("inst", None, "blk", None), P(None, "blk")),
        check_vma=False,
    )
```

time: 183 us -> 153 us (0.84)
  blocking collectives: 50.4 us -> 0 us
  waiting for transfers between devices: 35.5 us -> 60.4 us
  local copies, waits for them, and re-layouts: 11.4 us -> 2.69 us
  Pallas kernels: 46 us -> 49.1 us
  starting transfers between devices: 37.3 us -> 39.7 us
    all_to_all x1 -> x0, blocking collectives: 50.4 us -> none  [local(): got = lax.all_to_all(sent, 'inst', 0, 0, tiled=True)]
    all_to_all x0 -> x1, waiting for transfers between devices: none -> 23.5 us  [local(): got = lax.all_to_all(sent, 'inst', 0, 0, tiled=True)]
    unnamed x30 -> x12, local copies, waits for them, and re-layouts: 11.4 us -> 2.69 us
    all_to_all x0 -> x1, starting transfers between devices: none -> 6.8 us  [local(): got = lax.all_to_all(sent, 'inst', 0, 0, tiled=True)]
    pallas_call x5, Pallas kernels: 9.93 us -> 15.4 us  [the longest x1 5.59 us: pack(): pl.pallas_call(pack_kernel, in_specs=[pl.BlockSpec(memory_space=pltpu.SME...]
    all_to_all x1, starting transfers between devices: 8.2 us -> 4.61 us  [local(): home = lax.all_to_all(back, 'inst', 0, 0, tiled=True)]
  transfers between devices with their start and end apart: 10 -> 11, of which waited for: 3 -> 6; matrix products, arithmetic and copies ran while one was open for 0% -> 0% of each run, Pallas kernels for 14% -> 17%
where the time goes in v2:
time: 153 us
  waiting for transfers between devices  60.4 us (39%)
  Pallas kernels  49.1 us (32%)
  starting transfers between devices  39.7 us (26%)
  local copies, waits for them, and re-layouts  2.69 us (2%)
    all_to_all x1, waiting for transfers between devices, local(): got = lax.all_to_all(sent, 'inst', 0, 0, tiled=True)  23.5 us
    all_to_all x1, waiting for transfers between devices, local(): home = lax.all_to_all(back, 'inst', 0, 0, tiled=True)  22 us
    pallas_call x1, Pallas kernels, sort_faces(): pl.pallas_call(faces_kernel, in_specs=[smem] * 3, out_specs=[smem] * 4, o...  19.9 us
    all_to_all x1, starting transfers between devices, local(): owned = lax.all_to_all(slots, ('inst', 'blk'), 0, 0, tiled=True)  11.4 us
    all_to_all x1, waiting for transfers between devices, local(): owned = lax.all_to_all(slots, ('inst', 'blk'), 0, 0, tiled=True)  10.8 us
    pallas_call x1, Pallas kernels, last_state(): pl.pallas_call(last_kernel, grid=(INST,), in_specs=[pl.BlockSpec(memory_s...  7.57 us
    ppermute x2, starting transfers between devices, halos(): above = lax.ppermute(bottom, axes, up)  7.33 us
    all_to_all x1, starting transfers between devices, local(): got = lax.all_to_all(sent, 'inst', 0, 0, tiled=True)  6.8 us
  transfers between devices with their start and end apart: 11, of which 6 were waited for; matrix products, arithmetic and copies ran while one was open for 0% of the time, Pallas kernels for 17%

profile of v2, /device:TPU:1, one launch (start us, length us, event | category | flops | bytes accessed | tf_op | source)
XLA Modules:
  0.0 152.7 jit_solution(11820018214470596594)
XLA Ops:
  0.6 1.3 copy.11.coupling
  1.9 5.6 %shard_map.104 = f32[8,113,8,128]{3,2,1,0:T(8,128)} custom-call(s32[1]{0:T(128)} %bitcast.flip, f32[6,64,8,128]{3,2,1,0:T(8,128)} %bitcast.28, f32[6,64,8,128]{3,2,1,0:T(8,128)} %bitcast.29, f32[64,8,128]{2,1,0:T(8,128)} %bitcast.30, f32[64,8,128]{2,1,0:T(8,128)} %bitcast.31, f32[1,6,6]{2,1,0:T(8,128)} %copy.11.coupling), custom_call_target="tpu_custom_call" | custom-call | flops 1000000 | bytes 8000000 | tf_op jit(solution)/shard_map/pallas_call | solution.py:98
  7.5 0.0 copy-start.2
  7.5 0.0 copy-start.3
  7.5 6.8 %all-to-all-start = ((f32[8,113,8,128]{3,2,1,0:T(8,128)}), f32[8,113,8,128]{3,2,1,0:T(8,128)}, u32[]{:S(2)}, u32[]{:S(2)}) async-start(f32[8,113,8,128]{3,2,1,0:T(8,128)} %shard_map.104), calls=%async_computation | async-start | bytes 7405568 | tf_op jit(solution)/shard_map/all_to_all | solution.py:543
  14.3 0.0 copy-done.2
  14.3 0.0 copy-done.3
  14.4 19.9 %shard_map.105 = (s32[2048]{0:T(1024)S(1)}, s32[2048]{0:T(1024)S(1)}, s32[2048]{0:T(1024)S(1)}, s32[1]{0:T(128)}) custom-call(s32[2048]{0:T(1024)S(1)} %copy-done.2, s32[2048]{0:T(1024)S(1)} %bitcast.27, s32[1]{0:T(128)S(6)} %xor.3.chunk), custom_call_target="tpu_custom_call" | custom-call | flops 1000000000 | bytes 10000000 | tf_op jit(solution)/shard_map/pallas_call | solution.py:143
  34.2 23.5 %all-to-all-done.got = f32[8,113,8,128]{3,2,1,0:T(8,128)} async-done(((f32[8,113,8,128]{3,2,1,0:T(8,128)}), f32[8,113,8,128]{3,2,1,0:T(8,128)}, u32[]{:S(2)}, u32[]{:S(2)}) %all-to-all-start) | async-done | bytes 3702816 | tf_op jit(solution)/shard_map/all_to_all | solution.py:543
  57.7 4.3 %shard_map.106 = (f32[8,48,8,128]{3,2,1,0:T(8,128)S(1)}, f32[8,6,8,128]{3,2,1,0:T(8,128)S(1)}, f32[8,6,8,128]{3,2,1,0:T(8,128)S(1)}, f32[8,8,128]{2,1,0:T(8,128)...) custom-call(f32[8,113,8,128]{3,2,1,0:T(8,128)} %all-to-all-done.got), custom_call_target="tpu_custom_call" | custom-call | flops 10000000 | bytes 7000000 | tf_op jit(solution)/shard_map/pallas_call | solution.py:233
  62.0 3.6 %collective-permute-start = (f32[8,6,8,128]{3,2,1,0:T(8,128)S(1)}, f32[8,6,8,128]{3,2,1,0:T(8,128)S(1)}, u32[]{:S(2)}, u32[]{:S(2)}) collective-permute-start(f32[8,6,8,128]{3,2,1,0:T(8,128)S(1)} %get-tuple-element.36), channel_id=1, source_target_pairs={{0,1},{1,18},{18,19},{19,4},{4,5},{5,22},{22,23},{23,8},{8,9},{9,2... | collective-permute-start | bytes 589832 | tf_op jit(solution)/shard_map/ppermute | solution.py:345
  65.6 0.0 collective-permute-start.1
  65.6 2.2 %collective-permute-start.2 = (f32[8,8,128]{2,1,0:T(8,128)S(1)}, f32[8,8,128]{2,1,0:T(8,128)S(1)}, u32[]{:S(2)}, u32[]{:S(2)}) collective-permute-start(f32[8,8,128]{2,1,0:T(8,128)S(1)} %get-tuple-element.38), channel_id=1, source_target_pairs={{0,16},{1,17},{18,2},{19,3},{4,20},{5,21},{22,6},{23,7},{8,24},{9,... | collective-permute-start | bytes 98312 | tf_op jit(solution)/shard_map/ppermute | solution.py:347
  67.8 1.3 collective-permute-start.3
  69.1 1.4 shard_map.107.most
  70.5 0.0 collective-permute-done.2.before
  70.5 2.0 %collective-permute-done.3.after = f32[8,8,128]{2,1,0:T(8,128)S(1)} collective-permute-done((f32[8,8,128]{2,1,0:T(8,128)S(1)}, f32[8,8,128]{2,1,0:T(8,128)S(1)}, u32[]{:S(2)}, u32[]{:S(2)}) %collective-permute-start.3) | collective-permute-done | bytes 32800 | tf_op jit(solution)/shard_map/ppermute | solution.py:348
  72.5 0.0 collective-permute-done.above
  72.5 0.2 collective-permute-done.1.below
  72.6 3.3 %shard_map.108 = (f32[8,48,8,128]{3,2,1,0:T(8,128)S(1)}, f32[8,48,8,128]{3,2,1,0:T(8,128)S(1)}, f32[8,6,8,128]{3,2,1,0:T(8,128)S(1)}, f32[8,6,8,128]{3,2,1,0:T(8...) custom-call(f32[8,48,8,128]{3,2,1,0:T(8,128)S(1)} %shard_map.107.most, ...), custom_call_target="tpu_custom_call" | custom-call | flops 10000000 | bytes 7000000 | tf_op jit(solution)/shard_map/pallas_call | solution.py:277
  75.9 3.7 %collective-permute-start.4 = (f32[8,6,8,128]{3,2,1,0:T(8,128)S(1)}, f32[8,6,8,128]{3,2,1,0:T(8,128)S(1)}, u32[]{:S(2)}, u32[]{:S(2)}) collective-permute-start(f32[8,6,8,128]{3,2,1,0:T(8,128)S(1)} %get-tuple-element.42), channel_id=1, source_target_pairs={{0,1},{1,18},{18,19},{19,4},{4,5},{5,22},{22,23},{23,8},{8,9},{9,2... | collective-permute-start | bytes 589832 | tf_op jit(solution)/shard_map/ppermute | solution.py:345
  79.6 0.2 collective-permute-start.5
  79.8 4.5 %collective-permute-start.6 = (f32[8,8,128]{2,1,0:T(8,128)S(1)}, f32[8,8,128]{2,1,0:T(8,128)S(1)}, u32[]{:S(2)}, u32[]{:S(2)}) collective-permute-start(f32[8,8,128]{2,1,0:T(8,128)S(1)} %get-tuple-element.44), channel_id=1, source_target_pairs={{0,16},{1,17},{18,2},{19,3},{4,20},{5,21},{22,6},{23,7},{8,24},{9,... | collective-permute-start | bytes 98312 | tf_op jit(solution)/shard_map/ppermute | solution.py:347
  84.4 1.3 collective-permute-start.7
  85.7 1.4 shard_map.109.most
  87.0 0.0 collective-permute-done.6.before
  87.0 2.0 %collective-permute-done.7.after = f32[8,8,128]{2,1,0:T(8,128)S(1)} collective-permute-done((f32[8,8,128]{2,1,0:T(8,128)S(1)}, f32[8,8,128]{2,1,0:T(8,128)S(1)}, u32[]{:S(2)}, u32[]{:S(2)}) %collective-permute-start.7) | collective-permute-done | bytes 32800 | tf_op jit(solution)/shard_map/ppermute | solution.py:348
  89.0 0.0 collective-permute-done.4.above
  89.0 0.0 collective-permute-done.5.below
  89.0 7.6 %shard_map.110 = f32[8,64,8,128]{3,2,1,0:T(8,128)S(1)} custom-call(s32[1]{0:T(128)} %get-tuple-element.29.count, s32[2048]{0:T(1024)S(1)} %get-tuple-element.30.faces, f32[8,48,8,128]{3,2,1,0:T(8,128)S(1)} %shard_map.109.most, f32[8,48,8,128]{3,2,1,0:T(8,128)S(1)} %get-tuple-element.40.psi, f32[8,17,8,128]{3,2,1,0:T(8,128)S(1)} %get-tuple-element.34.scale.scales, ...), custom_call_target="tpu_custom_call" | custom-call | flops 100000000 | bytes 7000000 | tf_op jit(solution)/shard_map/pallas_call | solution.py:434
  96.6 0.0 copy-start
  96.6 1.3 copy-done
  98.0 0.0 copy-start.4
  98.0 0.0 copy-start.1
  98.0 4.6 %all-to-all-start.1 = ((f32[8,64,8,128]{3,2,1,0:T(8,128)}), f32[8,64,8,128]{3,2,1,0:T(8,128)S(1)}, u32[]{:S(2)}, u32[]{:S(2)}) async-start(f32[8,64,8,128]{3,2,1,0:T(8,128)} %copy-done), calls=%async_computation.1 | async-start | bytes 4194304 | tf_op jit(solution)/shard_map/all_to_all | solution.py:555
  102.6 0.0 copy-done.4
  102.6 0.1 copy.14
  102.7 22.0 %all-to-all-done.1.got = f32[8,64,8,128]{3,2,1,0:T(8,128)S(1)} async-done(((f32[8,64,8,128]{3,2,1,0:T(8,128)}), f32[8,64,8,128]{3,2,1,0:T(8,128)S(1)}, u32[]{:S(2)}, u32[]{:S(2)}) %all-to-all-start.1) | async-done | bytes 2097184 | tf_op jit(solution)/shard_map/all_to_all | solution.py:555
  124.6 0.0 copy-done.1
  124.6 1.6 %shard_map.112 = f32[128,8,128]{2,1,0:T(8,128)} custom-call(f32[8,64,8,128]{3,2,1,0:T(8,128)S(1)} %all-to-all-done.1.got, f32[18,2048]{1,0:T(8,128)S(1)} %bitcast.22, s32[1,2048]{1,0:T(1,128)S(1)} %bitcast.25, s32[1,2048]{1,0:T(1,128)S(1)} %bitcast.24), custom_call_target="tpu_custom_call" | custom-call | flops 100000000 | bytes 2000000 | tf_op jit(solution)/shard_map/pallas_call | solution.py:495
  126.2 11.4 %all-to-all-start.2 = ((f32[128,8,128]{2,1,0:T(8,128)}), f32[128,8,128]{2,1,0:T(8,128)S(1)}, u32[]{:S(2)}, u32[]{:S(2)}) async-start(f32[128,8,128]{2,1,0:T(8,128)} %shard_map.112), calls=%async_computation.2 | async-start | bytes 1048576 | tf_op jit(solution)/shard_map/all_to_all | solution.py:557
  137.6 2.9 %shard_map.111 = f32[1,6,8,8192]{3,2,1,0:T(8,128)} custom-call(s32[1]{0:T(128)} %bitcast.flip, f32[8,64,8,128]{3,2,1,0:T(8,128)S(1)} %all-to-all-done.1.got), custom_call_target="tpu_custom_call" | custom-call | flops 1000000 | bytes 4000000 | tf_op jit(solution)/shard_map/pallas_call | solution.py:454
  140.5 10.8 %all-to-all-done.2.got = f32[128,8,128]{2,1,0:T(8,128)S(1)} async-done(((f32[128,8,128]{2,1,0:T(8,128)}), f32[128,8,128]{2,1,0:T(8,128)S(1)}, u32[]{:S(2)}, u32[]{:S(2)}) %all-to-all-start.2) | async-done | bytes 524320 | tf_op jit(solution)/shard_map/all_to_all | solution.py:557
  151.2 1.5 shard_map.113
Async XLA Ops:
  7.5 6.8 %copy-start.2 = (s32[2048]{0:T(1024)S(1)}, s32[2048]{0:T(1024)}, u32[]{:S(2)}) copy-start(s32[2048]{0:T(1024)} %cell.1) | copy-start | bytes 24580
  7.5 6.8 %copy-start.3 = (s32[2048,1]{0,1:T(1,128)S(1)}, s32[2048,1]{0,1:T(1,128)}, u32[]{:S(2)}) copy-start(s32[2048,1]{0,1:T(1,128)} %param.16) | copy-start | bytes 24580
  7.5 50.2 %all-to-all-start = ((f32[8,113,8,128]{3,2,1,0:T(8,128)}), f32[8,113,8,128]{3,2,1,0:T(8,128)}, u32[]{:S(2)}, u32[]{:S(2)}) async-start(f32[8,113,8,128]{3,2,1,0:T(8,128)} %shard_map.104), calls=%async_computation | async-start | bytes 7405568 | tf_op jit(solution)/shard_map/all_to_all | solution.py:543
  62.0 10.5 %collective-permute-start = (f32[8,6,8,128]{3,2,1,0:T(8,128)S(1)}, f32[8,6,8,128]{3,2,1,0:T(8,128)S(1)}, u32[]{:S(2)}, u32[]{:S(2)}) collective-permute-start(f32[8,6,8,128]{3,2,1,0:T(8,128)S(1)} %get-tuple-element.36), channel_id=1, source_target_pairs={{0,1},{1,18},{18,19},{19,4},{4,5},{5,22},{22,23},{23,8},{8,9},{9,2... | collective-permute-start | bytes 589832 | tf_op jit(solution)/shard_map/ppermute | solution.py:345
  65.6 7.0 %collective-permute-start.1 = (f32[8,6,8,128]{3,2,1,0:T(8,128)S(1)}, f32[8,6,8,128]{3,2,1,0:T(8,128)S(1)}, u32[]{:S(2)}, u32[]{:S(2)}) collective-permute-start(f32[8,6,8,128]{3,2,1,0:T(8,128)S(1)} %get-tuple-element.37), channel_id=1, source_target_pairs={{1,0},{18,1},{19,18},{4,19},{5,4},{22,5},{23,22},{8,23},{9,8},{26,... | collective-permute-start | bytes 589832 | tf_op jit(solution)/shard_map/ppermute | solution.py:346
  65.6 4.9 %collective-permute-start.2 = (f32[8,8,128]{2,1,0:T(8,128)S(1)}, f32[8,8,128]{2,1,0:T(8,128)S(1)}, u32[]{:S(2)}, u32[]{:S(2)}) collective-permute-start(f32[8,8,128]{2,1,0:T(8,128)S(1)} %get-tuple-element.38), channel_id=1, source_target_pairs={{0,16},{1,17},{18,2},{19,3},{4,20},{5,21},{22,6},{23,7},{8,24},{9,... | collective-permute-start | bytes 98312 | tf_op jit(solution)/shard_map/ppermute | solution.py:347
  67.8 4.7 %collective-permute-start.3 = (f32[8,8,128]{2,1,0:T(8,128)S(1)}, f32[8,8,128]{2,1,0:T(8,128)S(1)}, u32[]{:S(2)}, u32[]{:S(2)}) collective-permute-start(f32[8,8,128]{2,1,0:T(8,128)S(1)} %get-tuple-element.39), channel_id=1, source_target_pairs={{16,0},{17,1},{2,18},{3,19},{20,4},{21,5},{6,22},{7,23},{24,8},{25... | collective-permute-start | bytes 98312 | tf_op jit(solution)/shard_map/ppermute | solution.py:348
  75.9 13.1 %collective-permute-start.4 = (f32[8,6,8,128]{3,2,1,0:T(8,128)S(1)}, f32[8,6,8,128]{3,2,1,0:T(8,128)S(1)}, u32[]{:S(2)}, u32[]{:S(2)}) collective-permute-start(f32[8,6,8,128]{3,2,1,0:T(8,128)S(1)} %get-tuple-element.42), channel_id=1, source_target_pairs={{0,1},{1,18},{18,19},{19,4},{4,5},{5,22},{22,23},{23,8},{8,9},{9,2... | collective-permute-start | bytes 589832 | tf_op jit(solution)/shard_map/ppermute | solution.py:345
  79.6 9.4 %collective-permute-start.5 = (f32[8,6,8,128]{3,2,1,0:T(8,128)S(1)}, f32[8,6,8,128]{3,2,1,0:T(8,128)S(1)}, u32[]{:S(2)}, u32[]{:S(2)}) collective-permute-start(f32[8,6,8,128]{3,2,1,0:T(8,128)S(1)} %get-tuple-element.43), channel_id=1, source_target_pairs={{1,0},{18,1},{19,18},{4,19},{5,4},{22,5},{23,22},{8,23},{9,8},{26,... | collective-permute-start | bytes 589832 | tf_op jit(solution)/shard_map/ppermute | solution.py:346
  79.8 7.2 %collective-permute-start.6 = (f32[8,8,128]{2,1,0:T(8,128)S(1)}, f32[8,8,128]{2,1,0:T(8,128)S(1)}, u32[]{:S(2)}, u32[]{:S(2)}) collective-permute-start(f32[8,8,128]{2,1,0:T(8,128)S(1)} %get-tuple-element.44), channel_id=1, source_target_pairs={{0,16},{1,17},{18,2},{19,3},{4,20},{5,21},{22,6},{23,7},{8,24},{9,... | collective-permute-start | bytes 98312 | tf_op jit(solution)/shard_map/ppermute | solution.py:347
  84.4 4.7 %collective-permute-start.7 = (f32[8,8,128]{2,1,0:T(8,128)S(1)}, f32[8,8,128]{2,1,0:T(8,128)S(1)}, u32[]{:S(2)}, u32[]{:S(2)}) collective-permute-start(f32[8,8,128]{2,1,0:T(8,128)S(1)} %get-tuple-element.45), channel_id=1, source_target_pairs={{16,0},{17,1},{2,18},{3,19},{20,4},{21,5},{6,22},{7,23},{24,8},{25... | collective-permute-start | bytes 98312 | tf_op jit(solution)/shard_map/ppermute | solution.py:348
  96.6 1.4 copy-start
  98.0 4.6 %copy-start.4 = (f32[1,18,2048]{2,0,1:T(1,128)S(1)}, f32[1,18,2048]{2,0,1:T(1,128)}, u32[]{:S(2)}) copy-start(f32[1,18,2048]{2,0,1:T(1,128)} %param.14) | copy-start | bytes 442372
  98.0 26.7 %copy-start.1 = (s32[2048]{0:T(1024)S(1)}, s32[2048]{0:T(1024)}, u32[]{:S(2)}) copy-start(s32[2048]{0:T(1024)} %param.17) | copy-start | bytes 24580
  98.0 26.7 %all-to-all-start.1 = ((f32[8,64,8,128]{3,2,1,0:T(8,128)}), f32[8,64,8,128]{3,2,1,0:T(8,128)S(1)}, u32[]{:S(2)}, u32[]{:S(2)}) async-start(f32[8,64,8,128]{3,2,1,0:T(8,128)} %copy-done), calls=%async_computation.1 | async-start | bytes 4194304 | tf_op jit(solution)/shard_map/all_to_all | solution.py:555
  126.2 25.0 %all-to-all-start.2 = ((f32[128,8,128]{2,1,0:T(8,128)}), f32[128,8,128]{2,1,0:T(8,128)S(1)}, u32[]{:S(2)}, u32[]{:S(2)}) async-start(f32[128,8,128]{2,1,0:T(8,128)} %shard_map.112), calls=%async_computation.2 | async-start | bytes 1048576 | tf_op jit(solution)/shard_map/all_to_all | solution.py:557

commit v3 on v2

v3 whole, which is shorter than its diff:
```python
import math

import jax
import jax.numpy as jnp
from jax import lax
from jax.experimental import pallas as pl
from jax.experimental.pallas import tpu as pltpu
from jax.sharding import PartitionSpec as P

CAP = 256
NODE_DEV = 4096
INST = 8
N_BLK = 16
F = 6
TILES = 8
FACES = 2048
GROUPS = FACES // 128
PACKED = GROUPS * F // 8
VMEM = 16 * 1024 * 1024
STATE = F * TILES
SENT = STATE + 2 * TILES + 1

HALF_SPEC = [0.0] + [
    0.25 * (-1.0) ** d / math.sin(math.pi * d / INST) for d in range(1, INST)
]


def params(limit=VMEM):
    return pltpu.CompilerParams(vmem_limit_bytes=limit)


def cost(flops, nbytes):
    return pl.CostEstimate(flops=flops, bytes_accessed=nbytes, transcendentals=0)


def rows_iota(shape=(8, 128)):
    return lax.broadcasted_iota(jnp.int32, shape, 0)


def lanes_iota(shape=(8, 128)):
    return lax.broadcasted_iota(jnp.int32, shape, 1)


def full(shape):
    return pl.BlockSpec(shape, lambda *_: (0,) * len(shape))


def one(*shape):
    return pl.BlockSpec((1,) + shape, lambda i: (i,) + (0,) * len(shape))


def f32(*shape):
    return jax.ShapeDtypeStruct(shape, jnp.float32)


def tiled(x):
    x = x.reshape(x.shape[:-1] + (INST * TILES, 128))
    return jnp.swapaxes(x, -3, -2)


def tiles_of(d, flip):
    return pl.ds((d ^ flip[0]) * TILES, TILES)


def pack_kernel(flip, psi, center, spread, coupling, out, flat, held, sems, more):
    def load(d, f):
        start = psi.at[f, tiles_of(d, flip)]
        return pltpu.make_async_copy(start, held.at[d, pl.ds(f * TILES, TILES)], sems.at[d, f])

    def send(d):
        return pltpu.make_async_copy(held.at[d], out.at[d], more.at[2 + d])

    flats = [
        pltpu.make_async_copy(center, flat.at[0], more.at[0]),
        pltpu.make_async_copy(spread, flat.at[1], more.at[1]),
    ]
    for copy in flats:
        copy.start()
    for d in range(INST):
        for f in range(F):
            load(d, f).start()
    for copy in flats:
        copy.wait()
    for d in range(INST):
        held[d, STATE : STATE + TILES] = 0.6 / flat[0, tiles_of(d, flip)]
        held[d, STATE + TILES : STATE + 2 * TILES] = flat[1, tiles_of(d, flip)]
        held[d, SENT - 1] = jnp.zeros((8, 128), jnp.float32)
        for g in range(F):
            held[d, SENT - 1, g : g + 1, 0:F] = coupling[g]
        for f in range(F):
            load(d, f).wait()
        send(d).start()
    for d in range(INST):
        send(d).wait()


def pack(psi, center, spread, coupling, flip):
    vmem = pl.BlockSpec(memory_space=pltpu.VMEM)
    anywhere = pl.BlockSpec(memory_space=pl.ANY)
    return pl.pallas_call(
        pack_kernel,
        in_specs=[pl.BlockSpec(memory_space=pltpu.SMEM)] + [anywhere] * 3 + [vmem],
        out_specs=anywhere,
        out_shape=f32(INST, SENT, 8, 128),
        scratch_shapes=[
            pltpu.VMEM((2, INST * TILES, 8, 128), jnp.float32),
            pltpu.VMEM((INST, SENT, 8, 128), jnp.float32),
            pltpu.SemaphoreType.DMA((INST, F)),
            pltpu.SemaphoreType.DMA((2 + INST,)),
        ],
        compiler_params=params(60 * 1024 * 1024),
        cost_estimate=cost(10**6, 5 * 10**6),
    )(flip, tiled(psi), tiled(center), tiled(spread), jnp.swapaxes(coupling, 0, 1))


def pack_source_kernel(flip, source, out, held, sems, more):
    def load(d, f):
        start = source.at[f, tiles_of(d, flip)]
        return pltpu.make_async_copy(start, held.at[d, pl.ds(f * TILES, TILES)], sems.at[d, f])

    def send(d):
        return pltpu.make_async_copy(held.at[d], out.at[d], more.at[d])

    for d in range(INST):
        for f in range(F):
            load(d, f).start()
    for d in range(INST):
        for f in range(F):
            load(d, f).wait()
        send(d).start()
    for d in range(INST):
        send(d).wait()


def pack_source(source, flip):
    anywhere = pl.BlockSpec(memory_space=pl.ANY)
    return pl.pallas_call(
        pack_source_kernel,
        in_specs=[pl.BlockSpec(memory_space=pltpu.SMEM), anywhere],
        out_specs=anywhere,
        out_shape=f32(INST, STATE, 8, 128),
        scratch_shapes=[
            pltpu.VMEM((INST, STATE, 8, 128), jnp.float32),
            pltpu.SemaphoreType.DMA((INST, F)),
            pltpu.SemaphoreType.DMA((INST,)),
        ],
        compiler_params=params(60 * 1024 * 1024),
        cost_estimate=cost(10**6, 4 * 10**6),
    )(flip, tiled(source))


def faces_kernel(cell, dest, chunk, list_cell, list_face, slot, count, loads):
    for owner in range(N_BLK):
        loads[owner] = 0

    def step(face, found):
        here = cell[face]
        owner = dest[face]
        rank = loads[owner]
        slot[face] = owner * CAP + rank
        loads[owner] = rank + 1
        list_cell[found] = here
        list_face[found] = face
        mine = ((here & 8191) >> 10) == chunk[0]
        return found + mine.astype(jnp.int32)

    found = lax.fori_loop(0, FACES, step, jnp.int32(0))
    count[0] = found

    def fill(at, carry):
        list_cell[at] = 0
        list_face[at] = -1
        return carry

    lax.fori_loop(found, jnp.minimum(found + 128, FACES), fill, 0)


def sort_faces(cell, dest, chunk):
    smem = pl.BlockSpec(memory_space=pltpu.SMEM)
    ints = jax.ShapeDtypeStruct((FACES,), jnp.int32)
    return pl.pallas_call(
        faces_kernel,
        in_specs=[smem] * 3,
        out_specs=[smem] * 4,
        out_shape=[ints, ints, ints, jax.ShapeDtypeStruct((1,), jnp.int32)],
        scratch_shapes=[pltpu.SMEM((N_BLK,), jnp.int32)],
        compiler_params=pltpu.CompilerParams(vmem_limit_bytes=2**20),
        cost_estimate=cost(10**9, 10**7),
    )(cell, dest, chunk)


def fluxes(i, side, psi_of, spread_of, coupling, inner, near, far, near_side, far_side, held):
    row, lane = rows_iota(), lanes_iota()
    factor = [
        [jnp.broadcast_to(coupling[g : g + 1, f : f + 1], (8, 128)) for f in range(F)]
        for g in range(F)
    ]
    for t in range(TILES):
        psi = [psi_of(t, f) for f in range(F)]
        strength = spread_of(t)
        for f in range(F):
            total = factor[0][f] * psi[0]
            for g in range(1, F):
                total = total + factor[g][f] * psi[g]
            weighted = strength * total
            held[f * TILES + t] = weighted
            top, bottom = weighted[0:1, :], weighted[7:8, :]
            near[i, f, t : t + 1, :] = jnp.where(side[0] == 1, top, bottom)
            far[i, f, t : t + 1, :] = jnp.where(side[0] == 1, bottom, top)
    first = jnp.zeros((8, 128), jnp.float32)
    last = jnp.zeros((8, 128), jnp.float32)
    for f in range(F):
        tiles = [held[f * TILES + t] for t in range(TILES)]
        later = [pltpu.roll(x, 1, 1) for x in tiles]
        sooner = [pltpu.roll(x, 127, 1) for x in tiles]
        first = jnp.where(lane == f, jnp.broadcast_to(tiles[0][:, 0:1], (8, 128)), first)
        last = jnp.where(lane == f, jnp.broadcast_to(tiles[7][:, 127:128], (8, 128)), last)
        for t in range(TILES):
            before = later[t - 1] if t else jnp.zeros((8, 128), jnp.float32)
            after = sooner[t + 1] if t < TILES - 1 else jnp.zeros((8, 128), jnp.float32)
            total = jnp.where(lane == 0, before, later[t])
            total = total + jnp.where(lane == 127, after, sooner[t])
            total = total + jnp.where(row == 0, 0.0, pltpu.roll(tiles[t], 1, 0))
            total = total + jnp.where(row == 7, 0.0, pltpu.roll(tiles[t], 7, 0))
            inner[i, f * TILES + t] = total
    near_side[i] = jnp.where(side[1] == 1, first, last)
    far_side[i] = jnp.where(side[1] == 1, last, first)


FLUX_SHAPES = [
    f32(INST, STATE, 8, 128),
    f32(INST, F, 8, 128),
    f32(INST, F, 8, 128),
    f32(INST, 8, 128),
    f32(INST, 8, 128),
]


def first_kernel(side, got, inner, near, far, near_side, far_side, psi, scales, held, sems):
    def loads(i, n):
        to = (psi, scales)[n]
        start = got.at[i, pl.ds(n * STATE, to.shape[1])]
        return pltpu.make_async_copy(start, to.at[i], sems.at[n, i])

    for i in range(INST):
        loads(i, 0).start()
        loads(i, 1).start()

    def step(i, carry):
        loads(i, 0).wait()
        loads(i, 1).wait()
        fluxes(
            i, side,
            lambda t, f: psi[i, f * TILES + t],
            lambda t: scales[i, TILES + t],
            scales[i, 2 * TILES],
            inner, near, far, near_side, far_side, held,
        )
        return carry

    lax.fori_loop(0, INST, step, 0)


def first_fluxes(side, got):
    vmem = pl.BlockSpec(memory_space=pltpu.VMEM)
    return pl.pallas_call(
        first_kernel,
        in_specs=[pl.BlockSpec(memory_space=pltpu.SMEM), pl.BlockSpec(memory_space=pl.ANY)],
        out_specs=[vmem] * 7,
        out_shape=FLUX_SHAPES + [f32(INST, STATE, 8, 128), f32(INST, 2 * TILES + 1, 8, 128)],
        scratch_shapes=[
            pltpu.VMEM((STATE, 8, 128), jnp.float32),
            pltpu.SemaphoreType.DMA((2, INST)),
        ],
        compiler_params=params(),
        cost_estimate=cost(10**7, 7 * 10**6),
    )(side, got)


def rim(i, t, f, side, near, far, near_side, far_side):
    row, lane = rows_iota(), lanes_iota()
    near_row = jnp.where(side[0] == 1, 0, 7)
    total = jnp.where(row == near_row, near[i, f, t : t + 1, :], 0.0)
    total = total + jnp.where(row == 7 - near_row, far[i, f, t : t + 1, :], 0.0)
    if t == 0:
        left = jnp.where(side[1] == 1, near_side[i], far_side[i])
        total = total + jnp.where(lane == 0, jnp.broadcast_to(left[:, f : f + 1], (8, 128)), 0.0)
    if t == TILES - 1:
        right = jnp.where(side[1] == 1, far_side[i], near_side[i])
        total = total + jnp.where(lane == 127, jnp.broadcast_to(right[:, f : f + 1], (8, 128)), 0.0)
    return total


def second_kernel(side, got, most, scales, a, b, c, d,
                  psi, source, inner, near, far, near_side, far_side, held, sems):
    def load(i):
        return pltpu.make_async_copy(got.at[i], source.at[i], sems.at[i])

    for i in range(INST):
        load(i).start()

    def step(i, carry):
        load(i).wait()
        for t in range(TILES):
            scale = scales[i, t]
            for f in range(F):
                at = f * TILES + t
                psi[i, at] = most[i, at] + scale * (source[i, at] + rim(i, t, f, side, a, b, c, d))
        fluxes(
            i, side,
            lambda t, f: psi[i, f * TILES + t],
            lambda t: scales[i, TILES + t],
            scales[i, 2 * TILES],
            inner, near, far, near_side, far_side, held,
        )
        return carry

    lax.fori_loop(0, INST, step, 0)


HALO_SPECS = [one(F, 8, 128), one(F, 8, 128), one(8, 128), one(8, 128)]


def second_fluxes(side, got, most, scales, halo):
    vmem = pl.BlockSpec(memory_space=pltpu.VMEM)
    state = f32(INST, STATE, 8, 128)
    return pl.pallas_call(
        second_kernel,
        in_specs=[pl.BlockSpec(memory_space=pltpu.SMEM), pl.BlockSpec(memory_space=pl.ANY)] + [vmem] * 6,
        out_specs=[vmem] * 7,
        out_shape=[state, state] + FLUX_SHAPES,
        scratch_shapes=[
            pltpu.VMEM((STATE, 8, 128), jnp.float32),
            pltpu.SemaphoreType.DMA((INST,)),
        ],
        compiler_params=params(),
        cost_estimate=cost(10**7, 7 * 10**6),
    )(side, got, most, scales, *halo)


def spectral(psi):
    def at(j):
        return (psi[j], 1) if j < INST else (psi[j - INST], -1)

    totals = []
    for i in range(INST):
        total = None
        for d in (1, 2, 3):
            (x, p), (y, q) = at(i + d), at(i + INST - d)
            pair = x + y if p == q else x - y
            sign = p
            term = (sign * HALF_SPEC[d]) * pair
            total = term if total is None else total + term
        x, p = at(i + 4)
        totals.append(total + (p * HALF_SPEC[4]) * x)
    return totals


def most_kernel(psi, scale, inner, *rest):
    most = rest[-1]
    for t in range(TILES):
        state = [psi[i, t] for i in range(INST)]
        coupled = spectral(state)
        for i in range(INST):
            change = inner[i, t] - coupled[i]
            if len(rest) > 1:
                change = change + rest[0][i, t]
            most[i, t] = 0.4 * state[i] + scale[i, t] * change


def most_of_sweep(psi, scales, inner, *source):
    field = pl.BlockSpec((INST, TILES, 8, 128), lambda f: (0, f, 0, 0))
    scale = pl.BlockSpec((INST, TILES, 8, 128), lambda f: (0, 0, 0, 0))
    return pl.pallas_call(
        most_kernel,
        grid=(F,),
        in_specs=[field, scale, field] + [field] * len(source),
        out_specs=field,
        out_shape=f32(INST, STATE, 8, 128),
        compiler_params=params(),
        cost_estimate=cost(10**7, 8 * 10**6),
    )(psi, scales, inner, *source)


def device(chunk, block):
    return (chunk ^ ((block >> 1) & 1)) * N_BLK + block


def halos(edges):
    near, far, near_side, far_side = edges
    axes = ("inst", "blk")
    places = [(c, b) for c in range(INST) for b in range(N_BLK)]
    in_pair = [(device(c, b), device(c, b ^ 1)) for c, b in places]
    across = [
        (device(c, b), device(c, (b + 2 * (b % 2) - 1) % N_BLK)) for c, b in places]
    sides_in_pair = [(device(c, b), device(c ^ 1, b)) for c, b in places]
    sides_across = [
        (device(c, b), device(c + 2 * (c % 2) - 1, b))
        for c, b in places if 0 < c < INST - 1]
    return (
        lax.ppermute(near, axes, in_pair),
        lax.ppermute(far, axes, across),
        lax.ppermute(near_side, axes, sides_in_pair),
        lax.ppermute(far_side, axes, sides_across),
    )


def stacked(x):
    return jnp.concatenate(two_parts(x), axis=0)


def times_transposed(x, y):
    return lax.dot_general(x, y, (((1,), (1,)), ((), ())), preferred_element_type=jnp.float32)


def two_parts(x):
    a = x.astype(jnp.bfloat16)
    return a, (x - a.astype(jnp.float32)).astype(jnp.bfloat16)


def last_kernel(count, faces, side, most, psi, scales, a, b, c, d, list_cell, list_face,
                out, placed, *sums):
    i = pl.program_id(0)
    both = [[] for f in range(F)]
    for t in range(TILES):
        scale = scales[0, t]
        for f in range(F):
            new = most[0, f * TILES + t] + scale * rim(0, t, f, side, a, b, c, d)
            out[i, f * TILES + t] = new
            both[f].append(new + psi[0, f * TILES + t])
            if t % 2:
                rows = slice((f * TILES + t - 1) * 8, (f * TILES + t + 1) * 8)
                for part, value in zip(sums, two_parts(jnp.concatenate(both[f][-2:], axis=0))):
                    part[i, rows, :] = value

    @pl.when(i == INST - 1)
    def _():
        groups = (count[0] + 127) // 128
        row = rows_iota()
        placed[...] = jnp.zeros_like(placed)

        def pick(g, carry):
            cell = list_cell[pl.ds(g, 1), :]
            onehot = (rows_iota((128, 128)) == (cell & 127)).astype(jnp.bfloat16)
            here = row == (cell >> 13)
            tile = (cell >> 7) & 7
            masks = [here & (tile == t) for t in range(TILES)]
            found = []
            for j in range(INST):
                taken = sum(
                    jnp.dot(part[j], onehot, preferred_element_type=jnp.float32) for part in sums)
                picked = jnp.zeros((8, 128), jnp.float32)
                for f in range(F):
                    total = jnp.zeros((8, 128), jnp.float32)
                    for t in range(TILES):
                        at = (f * TILES + t) * 8
                        total = jnp.where(masks[t], taken[at : at + 8, :], total)
                    total = jnp.sum(total, axis=0, keepdims=True)
                    picked = jnp.where(row == f, total, picked)
                found.append(picked)
            parts = stacked(jnp.concatenate(found, axis=0))
            face = list_face[pl.ds(g, 1), :]
            last = jnp.minimum(g * 128 + 127, count[0] - 1)

            def place(b, carry):
                onehot = ((rows_iota((128, 128)) + b * 128) == face).astype(jnp.bfloat16)
                total = lax.dot_general(
                    parts, onehot, (((1,), (1,)), ((), ())), preferred_element_type=jnp.float32)
                for j in range(INST):
                    rows = [total[n : n + 8, :] for n in (j * 8, 64 + j * 8)]
                    placed[j, b] = placed[j, b] + (rows[0] + rows[1])
                return carry

            lax.fori_loop(faces[g * 128] >> 7, (faces[last] >> 7) + 1, place, 0)
            return carry

        lax.fori_loop(0, groups, pick, 0)
        for j in range(INST):
            for b in range(PACKED):
                rest = pltpu.roll(placed[j, PACKED + b // 3], 6 - 2 * (b % 3), 0)
                out[j, STATE + b] = jnp.where(row < F, placed[j, b], rest)


def last_state(count, side, most, psi, scales, halo, list_cell, list_face):
    block = one(STATE, 8, 128)
    faces = full((GROUPS, 128))
    shape = (INST, STATE + PACKED, 8, 128)
    return pl.pallas_call(
        last_kernel,
        grid=(INST,),
        in_specs=[pl.BlockSpec(memory_space=pltpu.SMEM)] * 3 + [block, block,
                  one(2 * TILES, 8, 128)] + HALO_SPECS + [faces, faces],
        out_specs=full(shape),
        out_shape=f32(*shape),
        scratch_shapes=[pltpu.VMEM((INST, GROUPS, 8, 128), jnp.float32)]
        + [pltpu.VMEM((INST, STATE * 8, 128), jnp.bfloat16)] * 2,
        compiler_params=params(),
        cost_estimate=cost(10**8, 7 * 10**6),
    )(count, list_face, side, most, psi, scales, *halo, list_cell.reshape(GROUPS, 128), list_face.reshape(GROUPS, 128))


def unpack_kernel(flip, got, psi):
    for t in range(TILES):
        for f in range(F):
            psi[0, f, :, t * 128 : (t + 1) * 128] = got[0, f * TILES + t]


def unpack(got, flip):
    return pl.pallas_call(
        unpack_kernel,
        grid_spec=pltpu.PrefetchScalarGridSpec(
            num_scalar_prefetch=1,
            grid=(INST,),
            in_specs=[pl.BlockSpec((1, STATE, 8, 128), lambda d, flip: (d, 0, 0, 0))],
            out_specs=pl.BlockSpec((1, F, 8, 1024), lambda d, flip: (0, 0, 0, d ^ flip[0])),
        ),
        out_shape=f32(1, F, 8, 8192),
        compiler_params=params(),
        cost_estimate=cost(10**6, 4 * 10**6),
    )(flip, got)


def slots_kernel(got, geometry, slot, node, out):
    row = rows_iota()
    total = jnp.zeros((2 * N_BLK * 8, 128), jnp.float32)
    sums = []
    for b in range(PACKED):
        picked = got[0, b]
        for c in range(1, INST):
            picked = picked + got[c, b]
        sums.append(picked)
    for q in range(GROUPS - PACKED):
        picked = pltpu.roll(sums[3 * q], 2, 0)
        for m in (1, 2):
            rest = pltpu.roll(sums[3 * q + m], 2 + 2 * m, 0)
            picked = jnp.where((row >> 1) == m, rest, picked)
        sums.append(picked)
    for b in range(GROUPS):
        cols = slice(b * 128, (b + 1) * 128)
        picked = sums[b]
        values = jnp.broadcast_to(node[:, cols].astype(jnp.float32), (8, 128))
        for k in range(3):
            part = jnp.sum(geometry[k * F : (k + 1) * F, cols] * picked[0:F, :], axis=0, keepdims=True)
            values = jnp.where((row >> 1) == k, part, values)
        place = slot[:, cols]
        half = (row & 1) == ((place >> 7) & 1)
        owner = place >> 8
        values = jnp.where(half, values, 0.0)
        rows = jnp.concatenate(
            [jnp.where(owner == d, values, 0.0) for d in range(N_BLK)], axis=0)
        onehot = (rows_iota((128, 128)) == (place & 127)).astype(jnp.bfloat16)
        total = total + times_transposed(stacked(rows), onehot)
    total = total[0:128] + total[128:256]
    for i in range(INST):
        for d in range(N_BLK):
            out[i * N_BLK + d] = total[d * 8 : d * 8 + 8, :]


def pack_slots(got, geometry, slot, node):
    return pl.pallas_call(
        slots_kernel,
        grid=(1,),
        in_specs=[pl.BlockSpec((INST, PACKED, 8, 128), lambda _: (0, STATE // PACKED, 0, 0)),
                  full((3 * F, FACES)), full((1, FACES)), full((1, FACES))],
        out_specs=full((INST * N_BLK, 8, 128)),
        out_shape=f32(INST * N_BLK, 8, 128),
        compiler_params=params(),
        cost_estimate=cost(10**8, 2 * 10**6),
    )(got, geometry, slot.reshape(1, FACES), node.reshape(1, FACES))


def nodes_kernel(got, out):
    total = jnp.zeros((2 * 96, 128), jnp.float32)
    for b in range(N_BLK):
        values = got[b]
        for i in range(1, INST):
            values = values + got[i * N_BLK + b]
        nodes = got[b].astype(jnp.int32)
        for half in range(2):
            node = nodes[6 + half : 7 + half, :]
            high = rows_iota((32, 128)) == (node >> 7)
            rows = jnp.concatenate(
                [jnp.where(high, values[k * 2 + half : k * 2 + half + 1, :], 0.0) for k in range(3)],
                axis=0)
            onehot = (rows_iota((128, 128)) == (node & 127)).astype(jnp.bfloat16)
            total = total + times_transposed(stacked(rows), onehot)
    total = total[0:96] + total[96:192]
    for k in range(3):
        for h in range(32):
            out[k : k + 1, h * 128 : (h + 1) * 128] = total[k * 32 + h : k * 32 + h + 1, :]


def to_nodes(got):
    return pl.pallas_call(
        nodes_kernel,
        in_specs=[pl.BlockSpec(memory_space=pltpu.VMEM)],
        out_specs=pl.BlockSpec(memory_space=pltpu.VMEM),
        out_shape=f32(3, NODE_DEV),
        compiler_params=params(),
        cost_estimate=cost(10**8, 10**6),
    )(got)


def local(psi_start, coupling, center, spread, source, wall_geo, wall_cell, wall_dest, wall_node):
    block = lax.axis_index("blk").astype(jnp.int32)
    flip = ((block >> 1) & 1).reshape(1)
    chunk = lax.axis_index("inst").astype(jnp.int32).reshape(1) ^ flip
    side = jnp.concatenate([(block & 1).reshape(1), chunk & 1])

    got = lax.all_to_all(
        pack(psi_start[0], center[0], spread[0], coupling, flip), "inst", 0, 0, tiled=True)
    faces = sort_faces(wall_cell, wall_dest[:, 0], chunk)
    sent = pack_source(source[0], flip)
    got, sent, (list_cell, list_face, slot, count) = lax.optimization_barrier((got, sent, faces))
    got_source = lax.all_to_all(sent, "inst", 0, 0, tiled=True)

    inner, *edges, psi, scales = first_fluxes(side, got)
    halo = halos(edges)
    most = most_of_sweep(psi, scales, inner)
    psi, source, inner, *edges = second_fluxes(side, got_source, most, scales, halo)
    halo = halos(edges)
    most = most_of_sweep(psi, scales, inner, source)
    back = last_state(count, side, most, psi, scales, halo, list_cell, list_face)

    home = lax.all_to_all(back, "inst", 0, 0, tiled=True)
    slots = pack_slots(home, wall_geo[0], slot, wall_node)
    owned = lax.all_to_all(slots, ("inst", "blk"), 0, 0, tiled=True)
    return unpack(home, flip), to_nodes(owned)


def solution(mesh):
    placed = (
        P("inst", None, "blk", None),
        P("inst", None, None),
        P("inst", "blk", None),
        P("inst", "blk", None),
        P("inst", None, "blk", None),
        P("inst", None, "blk"),
        P("blk"),
        P("blk", None),
        P("blk"),
    )
    return jax.shard_map(
        local,
        mesh=mesh,
        in_specs=placed,
        out_specs=(P("inst", None, "blk", None), P(None, "blk")),
        check_vma=False,
    )
```

time: 153 us -> 140 us (0.915)
  waiting for transfers between devices: 60.4 us -> 45.9 us
  Pallas kernels: 49.1 us -> 52.3 us
    all_to_all x1 -> x2, waiting for transfers between devices: 23.5 us -> 5.12 us  [the longest x1 3.98 us: local(): lax.all_to_all(pack(psi_start[0], center[0], spread[0], coupling, flip),...]
    pallas_call x5 -> x6, Pallas kernels: 11.8 us -> 17.8 us  [the longest x1 6.43 us: first_fluxes(): pl.pallas_call(first_kernel, in_specs=[pl.BlockSpec(memory_space=pltpu.SM...]
    ppermute x8, starting transfers between devices: 16.9 us -> 12.1 us  [the longest x2 5.46 us: halos(): lax.ppermute(near, axes, in_pair)]
    ppermute x8, waiting for transfers between devices: 4.11 us -> 8.75 us  [the longest x2 4.94 us: halos(): lax.ppermute(near_side, axes, sides_in_pair)]
    all_to_all x1 -> x2, starting transfers between devices: 6.8 us -> 11.1 us  [the longest x1 6.8 us: local(): lax.all_to_all(pack(psi_start[0], center[0], spread[0], coupling, flip),...]
  transfers between devices with their start and end apart: 11 -> 12, of which waited for: 6 -> 7; matrix products, arithmetic and copies ran while one was open for 0% -> 0% of each run, Pallas kernels for 17% -> 25%
where the time goes in v3:
time: 140 us; the launch traced here: 139 us
  Pallas kernels  52.3 us (37%)
  waiting for transfers between devices  45.9 us (33%)
  starting transfers between devices  39 us (28%)
    all_to_all x1, waiting for transfers between devices, local(): home = lax.all_to_all(back, 'inst', 0, 0, tiled=True)  21.3 us
    pallas_call x1, Pallas kernels, sort_faces(): pl.pallas_call(faces_kernel, in_specs=[smem] * 3, out_specs=[smem] * 4, o...  19.9 us
    all_to_all x1, starting transfers between devices, local(): owned = lax.all_to_all(slots, ('inst', 'blk'), 0, 0, tiled=True)  11.9 us
    all_to_all x1, waiting for transfers between devices, local(): owned = lax.all_to_all(slots, ('inst', 'blk'), 0, 0, tiled=True)  10.8 us
    all_to_all x1, starting transfers between devices, local(): lax.all_to_all(pack(psi_start[0], center[0], spread[0], coupling, flip),...  6.8 us
    pallas_call x1, Pallas kernels, first_fluxes(): pl.pallas_call(first_kernel, in_specs=[pl.BlockSpec(memory_space=pltpu.SM...  6.43 us
    pallas_call x1, Pallas kernels, last_state(): pl.pallas_call(last_kernel, grid=(INST,), in_specs=[pl.BlockSpec(memory_s...  6.16 us
    ppermute x2, starting transfers between devices, halos(): lax.ppermute(near, axes, in_pair)  5.46 us
  transfers between devices with their start and end apart: 12, of which 7 were waited for; matrix products, arithmetic and copies ran while one was open for 0% of the time, Pallas kernels for 25%

profile of v3, /device:TPU:1, one launch (start us, length us, event | category | flops | bytes accessed | tf_op | source)
XLA Modules:
  0.0 139.5 jit_solution(13726619029124780298)
XLA Ops:
  0.6 4.2 %shard_map.104 = f32[8,65,8,128]{3,2,1,0:T(8,128)} custom-call(s32[1]{0:T(128)} %bitcast.flip, f32[6,64,8,128]{3,2,1,0:T(8,128)} %bitcast.30, f32[64,8,128]{2,1,0:T(8,128)} %bitcast.32, f32[64,8,128]{2,1,0:T(8,128)} %bitcast.33, f32[6,1,6]{2,1,0:T(1,128)} %bitcast.34), custom_call_target="tpu_custom_call" | custom-call | flops 1000000 | bytes 5000000 | tf_op jit(solution)/shard_map/pallas_call | solution.py:100
  4.8 6.8 %all-to-all-start = ((f32[8,65,8,128]{3,2,1,0:T(8,128)}), f32[8,65,8,128]{3,2,1,0:T(8,128)S(1)}, u32[]{:S(2)}, u32[]{:S(2)}) async-start(f32[8,65,8,128]{3,2,1,0:T(8,128)} %shard_map.104), calls=%async_computation | async-start | bytes 4259840 | tf_op jit(solution)/shard_map/all_to_all | solution.py:610
  11.6 0.0 copy-start.2
  11.6 0.0 copy-start.3
  11.6 2.5 %shard_map.105 = f32[8,48,8,128]{3,2,1,0:T(8,128)} custom-call(s32[1]{0:T(128)} %bitcast.flip, f32[6,64,8,128]{3,2,1,0:T(8,128)} %bitcast.31), custom_call_target="tpu_custom_call" | custom-call | flops 1000000 | bytes 4000000 | tf_op jit(solution)/shard_map/pallas_call | solution.py:137
  14.2 0.0 copy-done.2
  14.2 0.0 copy-done.3
  14.2 19.9 %shard_map.106 = (s32[2048]{0:T(1024)S(1)}, s32[2048]{0:T(1024)S(1)}, s32[2048]{0:T(1024)S(1)}, s32[1]{0:T(128)}) custom-call(s32[2048]{0:T(1024)S(1)} %copy-done.2, s32[2048]{0:T(1024)S(1)} %bitcast.29, s32[1]{0:T(128)S(6)} %xor.3.chunk), custom_call_target="tpu_custom_call" | custom-call | flops 1000000000 | bytes 10000000 | tf_op jit(solution)/shard_map/pallas_call | solution.py:181
  34.1 4.0 %all-to-all-done.got = f32[8,65,8,128]{3,2,1,0:T(8,128)S(1)} async-done(((f32[8,65,8,128]{3,2,1,0:T(8,128)}), f32[8,65,8,128]{3,2,1,0:T(8,128)S(1)}, u32[]{:S(2)}, u32[]{:S(2)}) %all-to-all-start) | async-done | bytes 2129952 | tf_op jit(solution)/shard_map/all_to_all | solution.py:610
  38.0 4.3 %all-to-all-start.1 = ((f32[8,48,8,128]{3,2,1,0:T(8,128)}), f32[8,48,8,128]{3,2,1,0:T(8,128)}, u32[]{:S(2)}, u32[]{:S(2)}) async-start(f32[8,48,8,128]{3,2,1,0:T(8,128)} %shard_map.105), calls=%async_computation.1 | async-start | bytes 3145728 | tf_op jit(solution)/shard_map/all_to_all | solution.py:615
  42.3 0.1 pad_add_fusion.side
  42.4 6.4 %shard_map.107 = (f32[8,48,8,128]{3,2,1,0:T(8,128)S(1)}, f32[8,6,8,128]{3,2,1,0:T(8,128)S(1)}, f32[8,6,8,128]{3,2,1,0:T(8,128)S(1)}, f32[8,8,128]{2,1,0:T(8,128)...) custom-call(s32[2]{0:T(128)S(1)} %pad_add_fusion.side, ...), custom_call_target="tpu_custom_call" | custom-call | flops 10000000 | bytes 7000000 | tf_op jit(solution)/shard_map/pallas_call | solution.py:266
  48.9 1.9 %collective-permute-start = (f32[8,6,8,128]{3,2,1,0:T(8,128)S(1)}, f32[8,6,8,128]{3,2,1,0:T(8,128)S(1)}, u32[]{:S(2)}, u32[]{:S(2)}) collective-permute-start(f32[8,6,8,128]{3,2,1,0:T(8,128)S(1)} %get-tuple-element.37), channel_id=1, source_target_pairs={{0,1},{1,0},{18,19},{19,18},{4,5},{5,4},{22,23},{23,22},{8,9},{9,8... | collective-permute-start | bytes 589832 | tf_op jit(solution)/shard_map/ppermute | solution.py:401
  50.8 2.9 %collective-permute-start.1 = (f32[8,6,8,128]{3,2,1,0:T(8,128)S(1)}, f32[8,6,8,128]{3,2,1,0:T(8,128)S(1)}, u32[]{:S(2)}, u32[]{:S(2)}) collective-permute-start(f32[8,6,8,128]{3,2,1,0:T(8,128)S(1)} %get-tuple-element.38), channel_id=1, source_target_pairs={{0,31},{1,18},{18,1},{19,4},{4,19},{5,22},{22,5},{23,8},{8,23},{9,... | collective-permute-start | bytes 589832 | tf_op jit(solution)/shard_map/ppermute | solution.py:402
  53.7 0.0 collective-permute-start.2
  53.7 0.7 collective-permute-start.3
  54.3 1.2 shard_map.108.most
  55.5 4.9 %collective-permute-done.2.c = f32[8,8,128]{2,1,0:T(8,128)S(1)} collective-permute-done((f32[8,8,128]{2,1,0:T(8,128)S(1)}, f32[8,8,128]{2,1,0:T(8,128)S(1)}, u32[]{:S(2)}, u32[]{:S(2)}) %collective-permute-start.2) | collective-permute-done | bytes 32800 | tf_op jit(solution)/shard_map/ppermute | solution.py:403
  60.4 0.0 collective-permute-done.3.d
  60.4 0.0 collective-permute-done.a
  60.4 0.0 collective-permute-done.1.b
  60.4 1.1 all-to-all-done.1.got
  61.5 4.7 %shard_map.109 = (f32[8,48,8,128]{3,2,1,0:T(8,128)S(1)}, f32[8,48,8,128]{3,2,1,0:T(8,128)S(1)}, f32[8,48,8,128]{3,2,1,0:T(8,128)S(1)}, f32[8,6,8,128]{3,2,1,0:T(...) custom-call(s32[2]{0:T(128)S(1)} %pad_add_fusion.side, ...), custom_call_target="tpu_custom_call" | custom-call | flops 10000000 | bytes 7000000 | tf_op jit(solution)/shard_map/pallas_call | solution.py:327
  66.3 3.5 %collective-permute-start.4 = (f32[8,6,8,128]{3,2,1,0:T(8,128)S(1)}, f32[8,6,8,128]{3,2,1,0:T(8,128)S(1)}, u32[]{:S(2)}, u32[]{:S(2)}) collective-permute-start(f32[8,6,8,128]{3,2,1,0:T(8,128)S(1)} %get-tuple-element.44), channel_id=1, source_target_pairs={{0,1},{1,0},{18,19},{19,18},{4,5},{5,4},{22,23},{23,22},{8,9},{9,8... | collective-permute-start | bytes 589832 | tf_op jit(solution)/shard_map/ppermute | solution.py:401
  69.8 1.8 %collective-permute-start.5 = (f32[8,6,8,128]{3,2,1,0:T(8,128)S(1)}, f32[8,6,8,128]{3,2,1,0:T(8,128)S(1)}, u32[]{:S(2)}, u32[]{:S(2)}) collective-permute-start(f32[8,6,8,128]{3,2,1,0:T(8,128)S(1)} %get-tuple-element.45), channel_id=1, source_target_pairs={{0,31},{1,18},{18,1},{19,4},{4,19},{5,22},{22,5},{23,8},{8,23},{9,... | collective-permute-start | bytes 589832 | tf_op jit(solution)/shard_map/ppermute | solution.py:402
  71.6 0.6 collective-permute-start.6
  72.3 0.7 collective-permute-start.7
  72.9 1.4 shard_map.110.most
  74.3 0.1 collective-permute-done.6.c
  74.4 0.0 collective-permute-done.7.d
  74.4 0.0 collective-permute-done.4.a
  74.4 3.8 %collective-permute-done.5.b = f32[8,6,8,128]{3,2,1,0:T(8,128)S(1)} collective-permute-done((f32[8,6,8,128]{3,2,1,0:T(8,128)S(1)}, f32[8,6,8,128]{3,2,1,0:T(8,128)S(1)}, u32[]{:S(2)}, u32[]{:S(2)}) %collective-permute-start.5) | collective-permute-done | bytes 196640 | tf_op jit(solution)/shard_map/ppermute | solution.py:402
  78.2 6.2 %shard_map.111 = f32[8,60,8,128]{3,2,1,0:T(8,128)S(1)} custom-call(s32[1]{0:T(128)} %get-tuple-element.30.count, s32[2048]{0:T(1024)S(1)} %get-tuple-element.31.faces, s32[2]{0:T(128)S(1)} %pad_add_fusion.side, f32[8,48,8,128]{3,2,1,0:T(8,128)S(1)} %shard_map.110.most, f32[8,48,8,128]{3,2,1,0:T(8,128)S(1)} %get-tuple-element.41.psi, ...), custom_call_target="tpu_custom_call" | custom-call | flops 100000000 | bytes 7000000 | tf_op jit(solution)/shard_map/pallas_call | solution.py:488
  84.3 0.0 copy-start
  84.3 1.3 copy-done
  85.6 0.0 copy-start.4
  85.6 0.0 copy-start.1
  85.6 3.9 %all-to-all-start.2 = ((f32[8,60,8,128]{3,2,1,0:T(8,128)}), f32[8,60,8,128]{3,2,1,0:T(8,128)S(1)}, u32[]{:S(2)}, u32[]{:S(2)}) async-start(f32[8,60,8,128]{3,2,1,0:T(8,128)} %copy-done), calls=%async_computation.2 | async-start | bytes 3932160 | tf_op jit(solution)/shard_map/all_to_all | solution.py:625
  89.5 0.0 copy-done.4
  89.5 0.1 copy.13
  89.6 21.3 %all-to-all-done.2.got = f32[8,60,8,128]{3,2,1,0:T(8,128)S(1)} async-done(((f32[8,60,8,128]{3,2,1,0:T(8,128)}), f32[8,60,8,128]{3,2,1,0:T(8,128)S(1)}, u32[]{:S(2)}, u32[]{:S(2)}) %all-to-all-start.2) | async-done | bytes 1966112 | tf_op jit(solution)/shard_map/all_to_all | solution.py:625
  110.9 0.0 copy-done.1
  110.9 1.5 %shard_map.113 = f32[128,8,128]{2,1,0:T(8,128)} custom-call(f32[8,60,8,128]{3,2,1,0:T(8,128)S(1)} %all-to-all-done.2.got, f32[18,2048]{1,0:T(8,128)S(1)} %bitcast.24, s32[1,2048]{1,0:T(1,128)S(1)} %bitcast.27, s32[1,2048]{1,0:T(1,128)S(1)} %bitcast.26), custom_call_target="tpu_custom_call" | custom-call | flops 100000000 | bytes 2000000 | tf_op jit(solution)/shard_map/pallas_call | solution.py:560
  112.4 11.9 %all-to-all-start.3 = ((f32[128,8,128]{2,1,0:T(8,128)}), f32[128,8,128]{2,1,0:T(8,128)S(1)}, u32[]{:S(2)}, u32[]{:S(2)}) async-start(f32[128,8,128]{2,1,0:T(8,128)} %shard_map.113), calls=%async_computation.3 | async-start | bytes 1048576 | tf_op jit(solution)/shard_map/all_to_all | solution.py:627
  124.4 2.9 %shard_map.112 = f32[1,6,8,8192]{3,2,1,0:T(8,128)} custom-call(s32[1]{0:T(128)} %bitcast.flip, f32[8,60,8,128]{3,2,1,0:T(8,128)S(1)} %all-to-all-done.2.got), custom_call_target="tpu_custom_call" | custom-call | flops 1000000 | bytes 4000000 | tf_op jit(solution)/shard_map/pallas_call | solution.py:509
  127.2 10.8 %all-to-all-done.3.got = f32[128,8,128]{2,1,0:T(8,128)S(1)} async-done(((f32[128,8,128]{2,1,0:T(8,128)}), f32[128,8,128]{2,1,0:T(8,128)S(1)}, u32[]{:S(2)}, u32[]{:S(2)}) %all-to-all-start.3) | async-done | bytes 524320 | tf_op jit(solution)/shard_map/all_to_all | solution.py:627
  138.0 1.5 %shard_map.114 = f32[3,4096]{1,0:T(4,128)} custom-call(f32[128,8,128]{2,1,0:T(8,128)S(1)} %all-to-all-done.3.got), custom_call_target="tpu_custom_call" | custom-call | flops 100000000 | bytes 1000000 | tf_op jit(solution)/shard_map/pallas_call | solution.py:594
Async XLA Ops:
  4.8 33.2 %all-to-all-start = ((f32[8,65,8,128]{3,2,1,0:T(8,128)}), f32[8,65,8,128]{3,2,1,0:T(8,128)S(1)}, u32[]{:S(2)}, u32[]{:S(2)}) async-start(f32[8,65,8,128]{3,2,1,0:T(8,128)} %shard_map.104), calls=%async_computation | async-start | bytes 4259840 | tf_op jit(solution)/shard_map/all_to_all | solution.py:610
  11.6 2.6 %copy-start.2 = (s32[2048]{0:T(1024)S(1)}, s32[2048]{0:T(1024)}, u32[]{:S(2)}) copy-start(s32[2048]{0:T(1024)} %cell.1) | copy-start | bytes 24580
  11.6 2.6 %copy-start.3 = (s32[2048,1]{0,1:T(1,128)S(1)}, s32[2048,1]{0,1:T(1,128)}, u32[]{:S(2)}) copy-start(s32[2048,1]{0,1:T(1,128)} %param.16) | copy-start | bytes 24580
  38.0 23.5 %all-to-all-start.1 = ((f32[8,48,8,128]{3,2,1,0:T(8,128)}), f32[8,48,8,128]{3,2,1,0:T(8,128)}, u32[]{:S(2)}, u32[]{:S(2)}) async-start(f32[8,48,8,128]{3,2,1,0:T(8,128)} %shard_map.105), calls=%async_computation.1 | async-start | bytes 3145728 | tf_op jit(solution)/shard_map/all_to_all | solution.py:615
  48.9 11.5 %collective-permute-start = (f32[8,6,8,128]{3,2,1,0:T(8,128)S(1)}, f32[8,6,8,128]{3,2,1,0:T(8,128)S(1)}, u32[]{:S(2)}, u32[]{:S(2)}) collective-permute-start(f32[8,6,8,128]{3,2,1,0:T(8,128)S(1)} %get-tuple-element.37), channel_id=1, source_target_pairs={{0,1},{1,0},{18,19},{19,18},{4,5},{5,4},{22,23},{23,22},{8,9},{9,8... | collective-permute-start | bytes 589832 | tf_op jit(solution)/shard_map/ppermute | solution.py:401
  50.8 9.6 %collective-permute-start.1 = (f32[8,6,8,128]{3,2,1,0:T(8,128)S(1)}, f32[8,6,8,128]{3,2,1,0:T(8,128)S(1)}, u32[]{:S(2)}, u32[]{:S(2)}) collective-permute-start(f32[8,6,8,128]{3,2,1,0:T(8,128)S(1)} %get-tuple-element.38), channel_id=1, source_target_pairs={{0,31},{1,18},{18,1},{19,4},{4,19},{5,22},{22,5},{23,8},{8,23},{9,... | collective-permute-start | bytes 589832 | tf_op jit(solution)/shard_map/ppermute | solution.py:402
  53.7 6.7 %collective-permute-start.2 = (f32[8,8,128]{2,1,0:T(8,128)S(1)}, f32[8,8,128]{2,1,0:T(8,128)S(1)}, u32[]{:S(2)}, u32[]{:S(2)}) collective-permute-start(f32[8,8,128]{2,1,0:T(8,128)S(1)} %get-tuple-element.39), channel_id=1, source_target_pairs={{0,16},{1,17},{18,2},{19,3},{4,20},{5,21},{22,6},{23,7},{8,24},{9,... | collective-permute-start | bytes 98312 | tf_op jit(solution)/shard_map/ppermute | solution.py:403
  53.7 6.7 %collective-permute-start.3 = (f32[8,8,128]{2,1,0:T(8,128)S(1)}, f32[8,8,128]{2,1,0:T(8,128)S(1)}, u32[]{:S(2)}, u32[]{:S(2)}) collective-permute-start(f32[8,8,128]{2,1,0:T(8,128)S(1)} %get-tuple-element.40), channel_id=1, source_target_pairs={{16,32},{17,33},{2,50},{3,51},{20,36},{21,37},{6,54},{7,55},{24,40... | collective-permute-start | bytes 98312 | tf_op jit(solution)/shard_map/ppermute | solution.py:404
  66.3 8.1 %collective-permute-start.4 = (f32[8,6,8,128]{3,2,1,0:T(8,128)S(1)}, f32[8,6,8,128]{3,2,1,0:T(8,128)S(1)}, u32[]{:S(2)}, u32[]{:S(2)}) collective-permute-start(f32[8,6,8,128]{3,2,1,0:T(8,128)S(1)} %get-tuple-element.44), channel_id=1, source_target_pairs={{0,1},{1,0},{18,19},{19,18},{4,5},{5,4},{22,23},{23,22},{8,9},{9,8... | collective-permute-start | bytes 589832 | tf_op jit(solution)/shard_map/ppermute | solution.py:401
  69.8 8.4 %collective-permute-start.5 = (f32[8,6,8,128]{3,2,1,0:T(8,128)S(1)}, f32[8,6,8,128]{3,2,1,0:T(8,128)S(1)}, u32[]{:S(2)}, u32[]{:S(2)}) collective-permute-start(f32[8,6,8,128]{3,2,1,0:T(8,128)S(1)} %get-tuple-element.45), channel_id=1, source_target_pairs={{0,31},{1,18},{18,1},{19,4},{4,19},{5,22},{22,5},{23,8},{8,23},{9,... | collective-permute-start | bytes 589832 | tf_op jit(solution)/shard_map/ppermute | solution.py:402
  71.6 2.8 %collective-permute-start.6 = (f32[8,8,128]{2,1,0:T(8,128)S(1)}, f32[8,8,128]{2,1,0:T(8,128)S(1)}, u32[]{:S(2)}, u32[]{:S(2)}) collective-permute-start(f32[8,8,128]{2,1,0:T(8,128)S(1)} %get-tuple-element.46), channel_id=1, source_target_pairs={{0,16},{1,17},{18,2},{19,3},{4,20},{5,21},{22,6},{23,7},{8,24},{9,... | collective-permute-start | bytes 98312 | tf_op jit(solution)/shard_map/ppermute | solution.py:403
  72.3 2.1 %collective-permute-start.7 = (f32[8,8,128]{2,1,0:T(8,128)S(1)}, f32[8,8,128]{2,1,0:T(8,128)S(1)}, u32[]{:S(2)}, u32[]{:S(2)}) collective-permute-start(f32[8,8,128]{2,1,0:T(8,128)S(1)} %get-tuple-element.47), channel_id=1, source_target_pairs={{16,32},{17,33},{2,50},{3,51},{20,36},{21,37},{6,54},{7,55},{24,40... | collective-permute-start | bytes 98312 | tf_op jit(solution)/shard_map/ppermute | solution.py:404
  84.3 1.3 copy-start
  85.6 3.9 %copy-start.4 = (f32[1,18,2048]{2,0,1:T(1,128)S(1)}, f32[1,18,2048]{2,0,1:T(1,128)}, u32[]{:S(2)}) copy-start(f32[1,18,2048]{2,0,1:T(1,128)} %param.14) | copy-start | bytes 442372
  85.6 25.2 %copy-start.1 = (s32[2048]{0:T(1024)S(1)}, s32[2048]{0:T(1024)}, u32[]{:S(2)}) copy-start(s32[2048]{0:T(1024)} %param.17) | copy-start | bytes 24580
  85.6 25.2 %all-to-all-start.2 = ((f32[8,60,8,128]{3,2,1,0:T(8,128)}), f32[8,60,8,128]{3,2,1,0:T(8,128)S(1)}, u32[]{:S(2)}, u32[]{:S(2)}) async-start(f32[8,60,8,128]{3,2,1,0:T(8,128)} %copy-done), calls=%async_computation.2 | async-start | bytes 3932160 | tf_op jit(solution)/shard_map/all_to_all | solution.py:625
  112.4 25.6 %all-to-all-start.3 = ((f32[128,8,128]{2,1,0:T(8,128)}), f32[128,8,128]{2,1,0:T(8,128)S(1)}, u32[]{:S(2)}, u32[]{:S(2)}) async-start(f32[128,8,128]{2,1,0:T(8,128)} %shard_map.113), calls=%async_computation.3 | async-start | bytes 1048576 | tf_op jit(solution)/shard_map/all_to_all | solution.py:627

commit v4 on v3

--- a/solution.py
+++ b/solution.py
@@ -58,11 +58,22 @@
     return jnp.swapaxes(x, -3, -2)
 
 
+def flipped():
+    return (lax.axis_index("blk").astype(jnp.int32) >> 1) & 1
+
+
+def sides():
+    chunk = lax.axis_index("inst").astype(jnp.int32) ^ flipped()
+    return lax.axis_index("blk").astype(jnp.int32) & 1, chunk & 1
+
+
 def tiles_of(d, flip):
-    return pl.ds((d ^ flip[0]) * TILES, TILES)
-
-
-def pack_kernel(flip, psi, center, spread, coupling, out, flat, held, sems, more):
+    return pl.ds((d ^ flip) * TILES, TILES)
+
+
+def pack_kernel(psi, center, spread, coupling, out, flat, factors, held, sems, more):
+    flip = flipped()
+
     def load(d, f):
         start = psi.at[f, tiles_of(d, flip)]
         return pltpu.make_async_copy(start, held.at[d, pl.ds(f * TILES, TILES)], sems.at[d, f])
@@ -71,6 +82,7 @@
         return pltpu.make_async_copy(held.at[d], out.at[d], more.at[2 + d])
 
     flats = [
+        pltpu.make_async_copy(coupling, factors, more.at[2 + INST]),
         pltpu.make_async_copy(center, flat.at[0], more.at[0]),
         pltpu.make_async_copy(spread, flat.at[1], more.at[1]),
     ]
@@ -86,7 +98,7 @@
         held[d, STATE + TILES : STATE + 2 * TILES] = flat[1, tiles_of(d, flip)]
         held[d, SENT - 1] = jnp.zeros((8, 128), jnp.float32)
         for g in range(F):
-            held[d, SENT - 1, g : g + 1, 0:F] = coupling[g]
+            held[d, SENT - 1, g : g + 1, 0:F] = factors[g]
         for f in range(F):
             load(d, f).wait()
         send(d).start()
@@ -94,26 +106,28 @@
         send(d).wait()
 
 
-def pack(psi, center, spread, coupling, flip):
-    vmem = pl.BlockSpec(memory_space=pltpu.VMEM)
+def pack(psi, center, spread, coupling):
     anywhere = pl.BlockSpec(memory_space=pl.ANY)
     return pl.pallas_call(
         pack_kernel,
-        in_specs=[pl.BlockSpec(memory_space=pltpu.SMEM)] + [anywhere] * 3 + [vmem],
+        in_specs=[anywhere] * 4,
         out_specs=anywhere,
         out_shape=f32(INST, SENT, 8, 128),
         scratch_shapes=[
             pltpu.VMEM((2, INST * TILES, 8, 128), jnp.float32),
+            pltpu.VMEM((F, 1, F), jnp.float32),
             pltpu.VMEM((INST, SENT, 8, 128), jnp.float32),
             pltpu.SemaphoreType.DMA((INST, F)),
-            pltpu.SemaphoreType.DMA((2 + INST,)),
+            pltpu.SemaphoreType.DMA((3 + INST,)),
         ],
         compiler_params=params(60 * 1024 * 1024),
         cost_estimate=cost(10**6, 5 * 10**6),
-    )(flip, tiled(psi), tiled(center), tiled(spread), jnp.swapaxes(coupling, 0, 1))
-
-
-def pack_source_kernel(flip, source, out, held, sems, more):
+    )(tiled(psi), tiled(center), tiled(spread), jnp.swapaxes(coupling, 0, 1))
+
+
+def pack_source_kernel(source, out, held, sems, more):
+    flip = flipped()
+
     def load(d, f):
         start = source.at[f, tiles_of(d, flip)]
         return pltpu.make_async_copy(start, held.at[d, pl.ds(f * TILES, TILES)], sems.at[d, f])
@@ -132,11 +146,11 @@
         send(d).wait()
 
 
-def pack_source(source, flip):
+def pack_source(source):
     anywhere = pl.BlockSpec(memory_space=pl.ANY)
     return pl.pallas_call(
         pack_source_kernel,
-        in_specs=[pl.BlockSpec(memory_space=pltpu.SMEM), anywhere],
+        in_specs=[anywhere],
         out_specs=anywhere,
         out_shape=f32(INST, STATE, 8, 128),
         scratch_shapes=[
@@ -146,7 +160,7 @@
         ],
         compiler_params=params(60 * 1024 * 1024),
         cost_estimate=cost(10**6, 4 * 10**6),
-    )(flip, tiled(source))
+    )(tiled(source))
 
 
 def faces_kernel(cell, dest, chunk, list_cell, list_face, slot, count, loads):
@@ -203,14 +217,15 @@
             for g in range(1, F):
                 total = total + factor[g][f] * psi[g]
             weighted = strength * total
-            held[f * TILES + t] = weighted
-            top, bottom = weighted[0:1, :], weighted[7:8, :]
-            near[i, f, t : t + 1, :] = jnp.where(side[0] == 1, top, bottom)
-            far[i, f, t : t + 1, :] = jnp.where(side[0] == 1, bottom, top)
+            at = (f * TILES + t) * 8
+            held[at : at + 8, :] = weighted
+    near_row = jnp.where(side[0] == 1, 0, 7)
     first = jnp.zeros((8, 128), jnp.float32)
     last = jnp.zeros((8, 128), jnp.float32)
     for f in range(F):
-        tiles = [held[f * TILES + t] for t in range(TILES)]
+        near[i, f] = held[pl.ds(f * TILES * 8 + near_row, TILES, stride=8), :]
+        far[i, f] = held[pl.ds(f * TILES * 8 + 7 - near_row, TILES, stride=8), :]
+        tiles = [held[(f * TILES + t) * 8 : (f * TILES + t + 1) * 8, :] for t in range(TILES)]
         later = [pltpu.roll(x, 1, 1) for x in tiles]
         sooner = [pltpu.roll(x, 127, 1) for x in tiles]
         first = jnp.where(lane == f, jnp.broadcast_to(tiles[0][:, 0:1], (8, 128)), first)
@@ -236,7 +251,9 @@
 ]
 
 
-def first_kernel(side, got, inner, near, far, near_side, far_side, psi, scales, held, sems):
+def first_kernel(got, inner, near, far, near_side, far_side, psi, scales, held, sems):
+    side = sides()
+
     def loads(i, n):
         to = (psi, scales)[n]
         start = got.at[i, pl.ds(n * STATE, to.shape[1])]
@@ -261,20 +278,20 @@
     lax.fori_loop(0, INST, step, 0)
 
 
-def first_fluxes(side, got):
+def first_fluxes(got):
     vmem = pl.BlockSpec(memory_space=pltpu.VMEM)
     return pl.pallas_call(
         first_kernel,
-        in_specs=[pl.BlockSpec(memory_space=pltpu.SMEM), pl.BlockSpec(memory_space=pl.ANY)],
+        in_specs=[pl.BlockSpec(memory_space=pl.ANY)],
         out_specs=[vmem] * 7,
         out_shape=FLUX_SHAPES + [f32(INST, STATE, 8, 128), f32(INST, 2 * TILES + 1, 8, 128)],
         scratch_shapes=[
-            pltpu.VMEM((STATE, 8, 128), jnp.float32),
+            pltpu.VMEM((STATE * 8, 128), jnp.float32),
             pltpu.SemaphoreType.DMA((2, INST)),
         ],
         compiler_params=params(),
         cost_estimate=cost(10**7, 7 * 10**6),
-    )(side, got)
+    )(got)
 
 
 def rim(i, t, f, side, near, far, near_side, far_side):
@@ -291,16 +308,23 @@
     return total
 
 
-def second_kernel(side, got, most, scales, a, b, c, d,
+def second_kernel(got, most, scales, a, b, c, d,
                   psi, source, inner, near, far, near_side, far_side, held, sems):
+    side = sides()
+
     def load(i):
         return pltpu.make_async_copy(got.at[i], source.at[i], sems.at[i])
 
-    for i in range(INST):
+    for i in range(2):
         load(i).start()
 
     def step(i, carry):
         load(i).wait()
+
+        @pl.when(i + 2 < INST)
+        def _():
+            load(i + 2).start()
+
         for t in range(TILES):
             scale = scales[i, t]
             for f in range(F):
@@ -321,21 +345,21 @@
 HALO_SPECS = [one(F, 8, 128), one(F, 8, 128), one(8, 128), one(8, 128)]
 
 
-def second_fluxes(side, got, most, scales, halo):
+def second_fluxes(got, most, scales, halo):
     vmem = pl.BlockSpec(memory_space=pltpu.VMEM)
     state = f32(INST, STATE, 8, 128)
     return pl.pallas_call(
         second_kernel,
-        in_specs=[pl.BlockSpec(memory_space=pltpu.SMEM), pl.BlockSpec(memory_space=pl.ANY)] + [vmem] * 6,
+        in_specs=[pl.BlockSpec(memory_space=pl.ANY)] + [vmem] * 6,
         out_specs=[vmem] * 7,
         out_shape=[state, state] + FLUX_SHAPES,
         scratch_shapes=[
-            pltpu.VMEM((STATE, 8, 128), jnp.float32),
+            pltpu.VMEM((STATE * 8, 128), jnp.float32),
             pltpu.SemaphoreType.DMA((INST,)),
         ],
         compiler_params=params(),
         cost_estimate=cost(10**7, 7 * 10**6),
-    )(side, got, most, scales, *halo)
+    )(got, most, scales, *halo)
 
 
 def spectral(psi):
@@ -418,9 +442,10 @@
     return a, (x - a.astype(jnp.float32)).astype(jnp.bfloat16)
 
 
-def last_kernel(count, faces, side, most, psi, scales, a, b, c, d, list_cell, list_face,
+def last_kernel(count, faces, most, psi, scales, a, b, c, d, list_cell, list_face,
                 out, placed, *sums):
     i = pl.program_id(0)
+    side = sides()
     both = [[] for f in range(F)]
     for t in range(TILES):
         scale = scales[0, t]
@@ -462,16 +487,18 @@
             face = list_face[pl.ds(g, 1), :]
             last = jnp.minimum(g * 128 + 127, count[0] - 1)
 
-            def place(b, carry):
-                onehot = ((rows_iota((128, 128)) + b * 128) == face).astype(jnp.bfloat16)
-                total = lax.dot_general(
-                    parts, onehot, (((1,), (1,)), ((), ())), preferred_element_type=jnp.float32)
-                for j in range(INST):
-                    rows = [total[n : n + 8, :] for n in (j * 8, 64 + j * 8)]
-                    placed[j, b] = placed[j, b] + (rows[0] + rows[1])
+            def place(quad, carry):
+                onehot = ((rows_iota((512, 128)) + quad * 512) == face).astype(jnp.bfloat16)
+                total = times_transposed(parts, onehot)
+                for q in range(4):
+                    cols = slice(q * 128, (q + 1) * 128)
+                    for j in range(INST):
+                        rows = [total[n : n + 8, cols] for n in (j * 8, 64 + j * 8)]
+                        at = quad * 4 + q
+                        placed[j, at] = placed[j, at] + (rows[0] + rows[1])
                 return carry
 
-            lax.fori_loop(faces[g * 128] >> 7, (faces[last] >> 7) + 1, place, 0)
+            lax.fori_loop(faces[g * 128] >> 9, (faces[last] >> 9) + 1, place, 0)
             return carry
 
         lax.fori_loop(0, groups, pick, 0)
@@ -481,14 +508,14 @@
                 out[j, STATE + b] = jnp.where(row < F, placed[j, b], rest)
 
 
-def last_state(count, side, most, psi, scales, halo, list_cell, list_face):
+def last_state(count, most, psi, scales, halo, list_cell, list_face):
     block = one(STATE, 8, 128)
     faces = full((GROUPS, 128))
     shape = (INST, STATE + PACKED, 8, 128)
     return pl.pallas_call(
         last_kernel,
         grid=(INST,),
-        in_specs=[pl.BlockSpec(memory_space=pltpu.SMEM)] * 3 + [block, block,
+        in_specs=[pl.BlockSpec(memory_space=pltpu.SMEM)] * 2 + [block, block,
                   one(2 * TILES, 8, 128)] + HALO_SPECS + [faces, faces],
         out_specs=full(shape),
         out_shape=f32(*shape),
@@ -496,7 +523,7 @@
         + [pltpu.VMEM((INST, STATE * 8, 128), jnp.bfloat16)] * 2,
         compiler_params=params(),
         cost_estimate=cost(10**8, 7 * 10**6),
-    )(count, list_face, side, most, psi, scales, *halo, list_cell.reshape(GROUPS, 128), list_face.reshape(GROUPS, 128))
+    )(count, list_face, most, psi, scales, *halo, list_cell.reshape(GROUPS, 128), list_face.reshape(GROUPS, 128))
 
 
 def unpack_kernel(flip, got, psi):
@@ -605,22 +632,21 @@
     block = lax.axis_index("blk").astype(jnp.int32)
     flip = ((block >> 1) & 1).reshape(1)
     chunk = lax.axis_index("inst").astype(jnp.int32).reshape(1) ^ flip
-    side = jnp.concatenate([(block & 1).reshape(1), chunk & 1])
 
     got = lax.all_to_all(
-        pack(psi_start[0], center[0], spread[0], coupling, flip), "inst", 0, 0, tiled=True)
+        pack(psi_start[0], center[0], spread[0], coupling), "inst", 0, 0, tiled=True)
     faces = sort_faces(wall_cell, wall_dest[:, 0], chunk)
-    sent = pack_source(source[0], flip)
+    sent = pack_source(source[0])
     got, sent, (list_cell, list_face, slot, count) = lax.optimization_barrier((got, sent, faces))
     got_source = lax.all_to_all(sent, "inst", 0, 0, tiled=True)
 
-    inner, *edges, psi, scales = first_fluxes(side, got)
+    inner, *edges, psi, scales = first_fluxes(got)
     halo = halos(edges)
     most = most_of_sweep(psi, scales, inner)
-    psi, source, inner, *edges = second_fluxes(side, got_source, most, scales, halo)
+    psi, source, inner, *edges = second_fluxes(got_source, most, scales, halo)
     halo = halos(edges)
     most = most_of_sweep(psi, scales, inner, source)
-    back = last_state(count, side, most, psi, scales, halo, list_cell, list_face)
+    back = last_state(count, most, psi, scales, halo, list_cell, list_face)
 
     home = lax.all_to_all(back, "inst", 0, 0, tiled=True)
     slots = pack_slots(home, wall_geo[0], slot, wall_node)

time: 140 us -> 138 us (0.986)
  Pallas kernels: 52.3 us -> 50.1 us
  waiting for transfers between devices: 45.9 us -> 47.5 us
where the time goes in v4:
time: 138 us; the launch traced here: 137 us
  Pallas kernels  50.1 us (36%)
  waiting for transfers between devices  47.5 us (34%)
  starting transfers between devices  37.7 us (27%)
    all_to_all x1, waiting for transfers between devices, local(): home = lax.all_to_all(back, 'inst', 0, 0, tiled=True)  22.3 us
    pallas_call x1, Pallas kernels, sort_faces(): pl.pallas_call(faces_kernel, in_specs=[smem] * 3, out_specs=[smem] * 4, o...  19.9 us
    all_to_all x1, starting transfers between devices, local(): owned = lax.all_to_all(slots, ('inst', 'blk'), 0, 0, tiled=True)  10.8 us
    all_to_all x1, waiting for transfers between devices, local(): owned = lax.all_to_all(slots, ('inst', 'blk'), 0, 0, tiled=True)  10.8 us
    all_to_all x1, starting transfers between devices, local(): lax.all_to_all(pack(psi_start[0], center[0], spread[0], coupling), 'inst'...  6.8 us
    pallas_call x1, Pallas kernels, first_fluxes(): pl.pallas_call(first_kernel, in_specs=[pl.BlockSpec(memory_space=pl.ANY)]...  6.02 us
    ppermute x2, waiting for transfers between devices, halos(): lax.ppermute(near_side, axes, sides_in_pair)  5.47 us
    ppermute x2, starting transfers between devices, halos(): lax.ppermute(near, axes, in_pair)  5.46 us
  transfers between devices with their start and end apart: 12, of which 7 were waited for; matrix products, arithmetic and copies ran while one was open for 0% of the time, Pallas kernels for 25%

profile of v4, /device:TPU:1, one launch (start us, length us, event | category | flops | bytes accessed | tf_op | source)
XLA Modules:
  0.0 137.4 jit_solution(15287729876862015782)
XLA Ops:
  0.6 3.5 %shard_map.104 = f32[8,65,8,128]{3,2,1,0:T(8,128)} custom-call(f32[6,64,8,128]{3,2,1,0:T(8,128)} %bitcast.29, f32[64,8,128]{2,1,0:T(8,128)} %bitcast.31, f32[64,8,128]{2,1,0:T(8,128)} %bitcast.32, f32[6,1,6]{2,1,0:T(1,128)} %bitcast.33), custom_call_target="tpu_custom_call" | custom-call | flops 1000000 | bytes 5000000 | tf_op jit(solution)/shard_map/pallas_call | solution.py:111
  4.2 6.8 %all-to-all-start = ((f32[8,65,8,128]{3,2,1,0:T(8,128)}), f32[8,65,8,128]{3,2,1,0:T(8,128)S(1)}, u32[]{:S(2)}, u32[]{:S(2)}) async-start(f32[8,65,8,128]{3,2,1,0:T(8,128)} %shard_map.104), calls=%async_computation | async-start | bytes 4259840 | tf_op jit(solution)/shard_map/all_to_all | solution.py:636
  11.0 0.0 copy-start.2
  11.0 0.0 copy-start.3
  11.0 2.5 %shard_map.105 = f32[8,48,8,128]{3,2,1,0:T(8,128)} custom-call(f32[6,64,8,128]{3,2,1,0:T(8,128)} %bitcast.30), custom_call_target="tpu_custom_call" | custom-call | flops 1000000 | bytes 4000000 | tf_op jit(solution)/shard_map/pallas_call | solution.py:151
  13.5 0.0 copy-done.2
  13.5 0.0 copy-done.3
  13.5 19.9 %shard_map.106 = (s32[2048]{0:T(1024)S(1)}, s32[2048]{0:T(1024)S(1)}, s32[2048]{0:T(1024)S(1)}, s32[1]{0:T(128)}) custom-call(s32[2048]{0:T(1024)S(1)} %copy-done.2, s32[2048]{0:T(1024)S(1)} %bitcast.28, s32[1]{0:T(128)S(6)} %xor.3.chunk), custom_call_target="tpu_custom_call" | custom-call | flops 1000000000 | bytes 10000000 | tf_op jit(solution)/shard_map/pallas_call | solution.py:195
  33.4 4.0 %all-to-all-done.got = f32[8,65,8,128]{3,2,1,0:T(8,128)S(1)} async-done(((f32[8,65,8,128]{3,2,1,0:T(8,128)}), f32[8,65,8,128]{3,2,1,0:T(8,128)S(1)}, u32[]{:S(2)}, u32[]{:S(2)}) %all-to-all-start) | async-done | bytes 2129952 | tf_op jit(solution)/shard_map/all_to_all | solution.py:636
  37.4 4.3 %all-to-all-start.1 = ((f32[8,48,8,128]{3,2,1,0:T(8,128)}), f32[8,48,8,128]{3,2,1,0:T(8,128)}, u32[]{:S(2)}, u32[]{:S(2)}) async-start(f32[8,48,8,128]{3,2,1,0:T(8,128)} %shard_map.105), calls=%async_computation.1 | async-start | bytes 3145728 | tf_op jit(solution)/shard_map/all_to_all | solution.py:641
  41.7 6.0 %shard_map.107 = (f32[8,48,8,128]{3,2,1,0:T(8,128)S(1)}, f32[8,6,8,128]{3,2,1,0:T(8,128)S(1)}, f32[8,6,8,128]{3,2,1,0:T(8,128)S(1)}, f32[8,8,128]{2,1,0:T(8,128)...) custom-call(f32[8,65,8,128]{3,2,1,0:T(8,128)S(1)} %all-to-all-done.got), custom_call_target="tpu_custom_call" | custom-call | flops 10000000 | bytes 7000000 | tf_op jit(solution)/shard_map/pallas_call | solution.py:283
  47.7 1.9 %collective-permute-start = (f32[8,6,8,128]{3,2,1,0:T(8,128)S(1)}, f32[8,6,8,128]{3,2,1,0:T(8,128)S(1)}, u32[]{:S(2)}, u32[]{:S(2)}) collective-permute-start(f32[8,6,8,128]{3,2,1,0:T(8,128)S(1)} %get-tuple-element.37), channel_id=1, source_target_pairs={{0,1},{1,0},{18,19},{19,18},{4,5},{5,4},{22,23},{23,22},{8,9},{9,8... | collective-permute-start | bytes 589832 | tf_op jit(solution)/shard_map/ppermute | solution.py:425
  49.6 2.8 %collective-permute-start.1 = (f32[8,6,8,128]{3,2,1,0:T(8,128)S(1)}, f32[8,6,8,128]{3,2,1,0:T(8,128)S(1)}, u32[]{:S(2)}, u32[]{:S(2)}) collective-permute-start(f32[8,6,8,128]{3,2,1,0:T(8,128)S(1)} %get-tuple-element.38), channel_id=1, source_target_pairs={{0,31},{1,18},{18,1},{19,4},{4,19},{5,22},{22,5},{23,8},{8,23},{9,... | collective-permute-start | bytes 589832 | tf_op jit(solution)/shard_map/ppermute | solution.py:426
  52.5 0.0 collective-permute-start.2
  52.5 0.7 collective-permute-start.3
  53.1 1.2 shard_map.108.most
  54.3 5.4 %collective-permute-done.2.c = f32[8,8,128]{2,1,0:T(8,128)S(1)} collective-permute-done((f32[8,8,128]{2,1,0:T(8,128)S(1)}, f32[8,8,128]{2,1,0:T(8,128)S(1)}, u32[]{:S(2)}, u32[]{:S(2)}) %collective-permute-start.2) | collective-permute-done | bytes 32800 | tf_op jit(solution)/shard_map/ppermute | solution.py:427
  59.7 0.0 collective-permute-done.3.d
  59.7 0.0 collective-permute-done.a
  59.7 0.0 collective-permute-done.1.b
  59.7 1.1 all-to-all-done.1.got
  60.9 4.7 %shard_map.109 = (f32[8,48,8,128]{3,2,1,0:T(8,128)S(1)}, f32[8,48,8,128]{3,2,1,0:T(8,128)S(1)}, f32[8,48,8,128]{3,2,1,0:T(8,128)S(1)}, f32[8,6,8,128]{3,2,1,0:T(...) custom-call(f32[8,48,8,128]{3,2,1,0:T(8,128)} %all-to-all-done.1.got, ...), custom_call_target="tpu_custom_call" | custom-call | flops 10000000 | bytes 7000000 | tf_op jit(solution)/shard_map/pallas_call | solution.py:351
  65.6 3.5 %collective-permute-start.4 = (f32[8,6,8,128]{3,2,1,0:T(8,128)S(1)}, f32[8,6,8,128]{3,2,1,0:T(8,128)S(1)}, u32[]{:S(2)}, u32[]{:S(2)}) collective-permute-start(f32[8,6,8,128]{3,2,1,0:T(8,128)S(1)} %get-tuple-element.44), channel_id=1, source_target_pairs={{0,1},{1,0},{18,19},{19,18},{4,5},{5,4},{22,23},{23,22},{8,9},{9,8... | collective-permute-start | bytes 589832 | tf_op jit(solution)/shard_map/ppermute | solution.py:425
  69.1 1.8 %collective-permute-start.5 = (f32[8,6,8,128]{3,2,1,0:T(8,128)S(1)}, f32[8,6,8,128]{3,2,1,0:T(8,128)S(1)}, u32[]{:S(2)}, u32[]{:S(2)}) collective-permute-start(f32[8,6,8,128]{3,2,1,0:T(8,128)S(1)} %get-tuple-element.45), channel_id=1, source_target_pairs={{0,31},{1,18},{18,1},{19,4},{4,19},{5,22},{22,5},{23,8},{8,23},{9,... | collective-permute-start | bytes 589832 | tf_op jit(solution)/shard_map/ppermute | solution.py:426
  70.9 0.6 collective-permute-start.6
  71.5 0.7 collective-permute-start.7
  72.2 1.4 shard_map.110.most
  73.6 0.1 collective-permute-done.6.c
  73.6 0.0 collective-permute-done.7.d
  73.7 0.0 collective-permute-done.4.a
  73.7 3.8 %collective-permute-done.5.b = f32[8,6,8,128]{3,2,1,0:T(8,128)S(1)} collective-permute-done((f32[8,6,8,128]{3,2,1,0:T(8,128)S(1)}, f32[8,6,8,128]{3,2,1,0:T(8,128)S(1)}, u32[]{:S(2)}, u32[]{:S(2)}) %collective-permute-start.5) | collective-permute-done | bytes 196640 | tf_op jit(solution)/shard_map/ppermute | solution.py:426
  77.4 5.1 %shard_map.111 = f32[8,60,8,128]{3,2,1,0:T(8,128)S(1)} custom-call(s32[1]{0:T(128)} %get-tuple-element.30.count, s32[2048]{0:T(1024)S(1)} %get-tuple-element.31.faces, f32[8,48,8,128]{3,2,1,0:T(8,128)S(1)} %shard_map.110.most, f32[8,48,8,128]{3,2,1,0:T(8,128)S(1)} %get-tuple-element.41.psi, f32[8,17,8,128]{3,2,1,0:T(8,128)S(1)} %get-tuple-element.35.scale.scales, ...), custom_call_target="tpu_custom_call" | custom-call | flops 100000000 | bytes 7000000 | tf_op jit(solution)/shard_map/pallas_call | solution.py:515
  82.5 0.0 copy-start
  82.5 1.3 copy-done
  83.8 0.0 copy-start.4
  83.8 0.0 copy-start.1
  83.8 3.7 %all-to-all-start.2 = ((f32[8,60,8,128]{3,2,1,0:T(8,128)}), f32[8,60,8,128]{3,2,1,0:T(8,128)S(1)}, u32[]{:S(2)}, u32[]{:S(2)}) async-start(f32[8,60,8,128]{3,2,1,0:T(8,128)} %copy-done), calls=%async_computation.2 | async-start | bytes 3932160 | tf_op jit(solution)/shard_map/all_to_all | solution.py:651
  87.6 0.0 copy-done.4
  87.6 0.1 copy.13
  87.6 22.3 %all-to-all-done.2.got = f32[8,60,8,128]{3,2,1,0:T(8,128)S(1)} async-done(((f32[8,60,8,128]{3,2,1,0:T(8,128)}), f32[8,60,8,128]{3,2,1,0:T(8,128)S(1)}, u32[]{:S(2)}, u32[]{:S(2)}) %all-to-all-start.2) | async-done | bytes 1966112 | tf_op jit(solution)/shard_map/all_to_all | solution.py:651
  110.0 0.0 copy-done.1
  110.0 1.5 %shard_map.113 = f32[128,8,128]{2,1,0:T(8,128)} custom-call(f32[8,60,8,128]{3,2,1,0:T(8,128)S(1)} %all-to-all-done.2.got, f32[18,2048]{1,0:T(8,128)S(1)} %bitcast.23, s32[1,2048]{1,0:T(1,128)S(1)} %bitcast.26, s32[1,2048]{1,0:T(1,128)S(1)} %bitcast.25), custom_call_target="tpu_custom_call" | custom-call | flops 100000000 | bytes 2000000 | tf_op jit(solution)/shard_map/pallas_call | solution.py:587
  111.5 10.8 %all-to-all-start.3 = ((f32[128,8,128]{2,1,0:T(8,128)}), f32[128,8,128]{2,1,0:T(8,128)S(1)}, u32[]{:S(2)}, u32[]{:S(2)}) async-start(f32[128,8,128]{2,1,0:T(8,128)} %shard_map.113), calls=%async_computation.3 | async-start | bytes 1048576 | tf_op jit(solution)/shard_map/all_to_all | solution.py:653
  122.4 2.9 %shard_map.112 = f32[1,6,8,8192]{3,2,1,0:T(8,128)} custom-call(s32[1]{0:T(128)} %bitcast.flip, f32[8,60,8,128]{3,2,1,0:T(8,128)S(1)} %all-to-all-done.2.got), custom_call_target="tpu_custom_call" | custom-call | flops 1000000 | bytes 4000000 | tf_op jit(solution)/shard_map/pallas_call | solution.py:536
  125.2 10.8 %all-to-all-done.3.got = f32[128,8,128]{2,1,0:T(8,128)S(1)} async-done(((f32[128,8,128]{2,1,0:T(8,128)}), f32[128,8,128]{2,1,0:T(8,128)S(1)}, u32[]{:S(2)}, u32[]{:S(2)}) %all-to-all-start.3) | async-done | bytes 524320 | tf_op jit(solution)/shard_map/all_to_all | solution.py:653
  136.0 1.5 %shard_map.114 = f32[3,4096]{1,0:T(4,128)} custom-call(f32[128,8,128]{2,1,0:T(8,128)S(1)} %all-to-all-done.3.got), custom_call_target="tpu_custom_call" | custom-call | flops 100000000 | bytes 1000000 | tf_op jit(solution)/shard_map/pallas_call | solution.py:621
Async XLA Ops:
  4.2 33.2 %all-to-all-start = ((f32[8,65,8,128]{3,2,1,0:T(8,128)}), f32[8,65,8,128]{3,2,1,0:T(8,128)S(1)}, u32[]{:S(2)}, u32[]{:S(2)}) async-start(f32[8,65,8,128]{3,2,1,0:T(8,128)} %shard_map.104), calls=%async_computation | async-start | bytes 4259840 | tf_op jit(solution)/shard_map/all_to_all | solution.py:636
  11.0 2.6 %copy-start.2 = (s32[2048]{0:T(1024)S(1)}, s32[2048]{0:T(1024)}, u32[]{:S(2)}) copy-start(s32[2048]{0:T(1024)} %cell.1) | copy-start | bytes 24580
  11.0 2.6 %copy-start.3 = (s32[2048,1]{0,1:T(1,128)S(1)}, s32[2048,1]{0,1:T(1,128)}, u32[]{:S(2)}) copy-start(s32[2048,1]{0,1:T(1,128)} %param.16) | copy-start | bytes 24580
  37.4 23.5 %all-to-all-start.1 = ((f32[8,48,8,128]{3,2,1,0:T(8,128)}), f32[8,48,8,128]{3,2,1,0:T(8,128)}, u32[]{:S(2)}, u32[]{:S(2)}) async-start(f32[8,48,8,128]{3,2,1,0:T(8,128)} %shard_map.105), calls=%async_computation.1 | async-start | bytes 3145728 | tf_op jit(solution)/shard_map/all_to_all | solution.py:641
  47.7 12.0 %collective-permute-start = (f32[8,6,8,128]{3,2,1,0:T(8,128)S(1)}, f32[8,6,8,128]{3,2,1,0:T(8,128)S(1)}, u32[]{:S(2)}, u32[]{:S(2)}) collective-permute-start(f32[8,6,8,128]{3,2,1,0:T(8,128)S(1)} %get-tuple-element.37), channel_id=1, source_target_pairs={{0,1},{1,0},{18,19},{19,18},{4,5},{5,4},{22,23},{23,22},{8,9},{9,8... | collective-permute-start | bytes 589832 | tf_op jit(solution)/shard_map/ppermute | solution.py:425
  49.6 10.1 %collective-permute-start.1 = (f32[8,6,8,128]{3,2,1,0:T(8,128)S(1)}, f32[8,6,8,128]{3,2,1,0:T(8,128)S(1)}, u32[]{:S(2)}, u32[]{:S(2)}) collective-permute-start(f32[8,6,8,128]{3,2,1,0:T(8,128)S(1)} %get-tuple-element.38), channel_id=1, source_target_pairs={{0,31},{1,18},{18,1},{19,4},{4,19},{5,22},{22,5},{23,8},{8,23},{9,... | collective-permute-start | bytes 589832 | tf_op jit(solution)/shard_map/ppermute | solution.py:426
  52.5 7.3 %collective-permute-start.2 = (f32[8,8,128]{2,1,0:T(8,128)S(1)}, f32[8,8,128]{2,1,0:T(8,128)S(1)}, u32[]{:S(2)}, u32[]{:S(2)}) collective-permute-start(f32[8,8,128]{2,1,0:T(8,128)S(1)} %get-tuple-element.39), channel_id=1, source_target_pairs={{0,16},{1,17},{18,2},{19,3},{4,20},{5,21},{22,6},{23,7},{8,24},{9,... | collective-permute-start | bytes 98312 | tf_op jit(solution)/shard_map/ppermute | solution.py:427
  52.5 7.3 %collective-permute-start.3 = (f32[8,8,128]{2,1,0:T(8,128)S(1)}, f32[8,8,128]{2,1,0:T(8,128)S(1)}, u32[]{:S(2)}, u32[]{:S(2)}) collective-permute-start(f32[8,8,128]{2,1,0:T(8,128)S(1)} %get-tuple-element.40), channel_id=1, source_target_pairs={{16,32},{17,33},{2,50},{3,51},{20,36},{21,37},{6,54},{7,55},{24,40... | collective-permute-start | bytes 98312 | tf_op jit(solution)/shard_map/ppermute | solution.py:428
  65.6 8.1 %collective-permute-start.4 = (f32[8,6,8,128]{3,2,1,0:T(8,128)S(1)}, f32[8,6,8,128]{3,2,1,0:T(8,128)S(1)}, u32[]{:S(2)}, u32[]{:S(2)}) collective-permute-start(f32[8,6,8,128]{3,2,1,0:T(8,128)S(1)} %get-tuple-element.44), channel_id=1, source_target_pairs={{0,1},{1,0},{18,19},{19,18},{4,5},{5,4},{22,23},{23,22},{8,9},{9,8... | collective-permute-start | bytes 589832 | tf_op jit(solution)/shard_map/ppermute | solution.py:425
  69.1 8.4 %collective-permute-start.5 = (f32[8,6,8,128]{3,2,1,0:T(8,128)S(1)}, f32[8,6,8,128]{3,2,1,0:T(8,128)S(1)}, u32[]{:S(2)}, u32[]{:S(2)}) collective-permute-start(f32[8,6,8,128]{3,2,1,0:T(8,128)S(1)} %get-tuple-element.45), channel_id=1, source_target_pairs={{0,31},{1,18},{18,1},{19,4},{4,19},{5,22},{22,5},{23,8},{8,23},{9,... | collective-permute-start | bytes 589832 | tf_op jit(solution)/shard_map/ppermute | solution.py:426
  70.9 2.8 %collective-permute-start.6 = (f32[8,8,128]{2,1,0:T(8,128)S(1)}, f32[8,8,128]{2,1,0:T(8,128)S(1)}, u32[]{:S(2)}, u32[]{:S(2)}) collective-permute-start(f32[8,8,128]{2,1,0:T(8,128)S(1)} %get-tuple-element.46), channel_id=1, source_target_pairs={{0,16},{1,17},{18,2},{19,3},{4,20},{5,21},{22,6},{23,7},{8,24},{9,... | collective-permute-start | bytes 98312 | tf_op jit(solution)/shard_map/ppermute | solution.py:427
  71.5 2.1 %collective-permute-start.7 = (f32[8,8,128]{2,1,0:T(8,128)S(1)}, f32[8,8,128]{2,1,0:T(8,128)S(1)}, u32[]{:S(2)}, u32[]{:S(2)}) collective-permute-start(f32[8,8,128]{2,1,0:T(8,128)S(1)} %get-tuple-element.47), channel_id=1, source_target_pairs={{16,32},{17,33},{2,50},{3,51},{20,36},{21,37},{6,54},{7,55},{24,40... | collective-permute-start | bytes 98312 | tf_op jit(solution)/shard_map/ppermute | solution.py:428
  82.5 1.3 copy-start
  83.8 3.7 %copy-start.4 = (f32[1,18,2048]{2,0,1:T(1,128)S(1)}, f32[1,18,2048]{2,0,1:T(1,128)}, u32[]{:S(2)}) copy-start(f32[1,18,2048]{2,0,1:T(1,128)} %param.14) | copy-start | bytes 442372
  83.8 26.1 %copy-start.1 = (s32[2048]{0:T(1024)S(1)}, s32[2048]{0:T(1024)}, u32[]{:S(2)}) copy-start(s32[2048]{0:T(1024)} %param.17) | copy-start | bytes 24580
  83.8 26.1 %all-to-all-start.2 = ((f32[8,60,8,128]{3,2,1,0:T(8,128)}), f32[8,60,8,128]{3,2,1,0:T(8,128)S(1)}, u32[]{:S(2)}, u32[]{:S(2)}) async-start(f32[8,60,8,128]{3,2,1,0:T(8,128)} %copy-done), calls=%async_computation.2 | async-start | bytes 3932160 | tf_op jit(solution)/shard_map/all_to_all | solution.py:651
  111.5 24.5 %all-to-all-start.3 = ((f32[128,8,128]{2,1,0:T(8,128)}), f32[128,8,128]{2,1,0:T(8,128)S(1)}, u32[]{:S(2)}, u32[]{:S(2)}) async-start(f32[128,8,128]{2,1,0:T(8,128)} %shard_map.113), calls=%async_computation.3 | async-start | bytes 1048576 | tf_op jit(solution)/shard_map/all_to_all | solution.py:653

commit v5 on v4

--- a/solution.py
+++ b/solution.py
@@ -74,9 +74,9 @@
 def pack_kernel(psi, center, spread, coupling, out, flat, factors, held, sems, more):
     flip = flipped()
 
-    def load(d, f):
-        start = psi.at[f, tiles_of(d, flip)]
-        return pltpu.make_async_copy(start, held.at[d, pl.ds(f * TILES, TILES)], sems.at[d, f])
+    def load(d):
+        state = held.at[d, pl.ds(0, STATE)].reshape(F, TILES, 8, 128)
+        return pltpu.make_async_copy(psi.at[:, tiles_of(d, flip)], state, sems.at[d])
 
     def send(d):
         return pltpu.make_async_copy(held.at[d], out.at[d], more.at[2 + d])
@@ -89,8 +89,7 @@
     for copy in flats:
         copy.start()
     for d in range(INST):
-        for f in range(F):
-            load(d, f).start()
+        load(d).start()
     for copy in flats:
         copy.wait()
     for d in range(INST):
@@ -99,8 +98,7 @@
         held[d, SENT - 1] = jnp.zeros((8, 128), jnp.float32)
         for g in range(F):
             held[d, SENT - 1, g : g + 1, 0:F] = factors[g]
-        for f in range(F):
-            load(d, f).wait()
+        load(d).wait()
         send(d).start()
     for d in range(INST):
         send(d).wait()
@@ -117,7 +115,7 @@
             pltpu.VMEM((2, INST * TILES, 8, 128), jnp.float32),
             pltpu.VMEM((F, 1, F), jnp.float32),
             pltpu.VMEM((INST, SENT, 8, 128), jnp.float32),
-            pltpu.SemaphoreType.DMA((INST, F)),
+            pltpu.SemaphoreType.DMA((INST,)),
             pltpu.SemaphoreType.DMA((3 + INST,)),
         ],
         compiler_params=params(60 * 1024 * 1024),

time: 138 us -> 138 us (level)
  no operation moved by 1% of the time
where the time goes in v5:
time: 138 us; the launch traced here: 137 us
  Pallas kernels  49.9 us (36%)
  waiting for transfers between devices  47.6 us (34%)
  starting transfers between devices  37.4 us (27%)
    all_to_all x1, waiting for transfers between devices, local(): home = lax.all_to_all(back, 'inst', 0, 0, tiled=True)  22.4 us
    pallas_call x1, Pallas kernels, sort_faces(): pl.pallas_call(faces_kernel, in_specs=[smem] * 3, out_specs=[smem] * 4, o...  19.9 us
    all_to_all x1, waiting for transfers between devices, local(): owned = lax.all_to_all(slots, ('inst', 'blk'), 0, 0, tiled=True)  10.8 us
    all_to_all x1, starting transfers between devices, local(): owned = lax.all_to_all(slots, ('inst', 'blk'), 0, 0, tiled=True)  10.6 us
    all_to_all x1, starting transfers between devices, local(): lax.all_to_all(pack(psi_start[0], center[0], spread[0], coupling), 'inst'...  6.8 us
    pallas_call x1, Pallas kernels, first_fluxes(): pl.pallas_call(first_kernel, in_specs=[pl.BlockSpec(memory_space=pl.ANY)]...  6.02 us
    ppermute x2, waiting for transfers between devices, halos(): lax.ppermute(near_side, axes, sides_in_pair)  5.47 us
    ppermute x2, starting transfers between devices, halos(): lax.ppermute(near, axes, in_pair)  5.46 us
  transfers between devices with their start and end apart: 12, of which 7 were waited for; matrix products, arithmetic and copies ran while one was open for 0% of the time, Pallas kernels for 25%

profile of v5, /device:TPU:1, one launch (start us, length us, event | category | flops | bytes accessed | tf_op | source)
XLA Modules:
  0.0 137.0 jit_solution(13286243934568764166)
XLA Ops:
  0.6 3.1 %shard_map.104 = f32[8,65,8,128]{3,2,1,0:T(8,128)} custom-call(f32[6,64,8,128]{3,2,1,0:T(8,128)} %bitcast.29, f32[64,8,128]{2,1,0:T(8,128)} %bitcast.31, f32[64,8,128]{2,1,0:T(8,128)} %bitcast.32, f32[6,1,6]{2,1,0:T(1,128)} %bitcast.33), custom_call_target="tpu_custom_call" | custom-call | flops 1000000 | bytes 5000000 | tf_op jit(solution)/shard_map/pallas_call | solution.py:109
  3.7 6.8 %all-to-all-start = ((f32[8,65,8,128]{3,2,1,0:T(8,128)}), f32[8,65,8,128]{3,2,1,0:T(8,128)S(1)}, u32[]{:S(2)}, u32[]{:S(2)}) async-start(f32[8,65,8,128]{3,2,1,0:T(8,128)} %shard_map.104), calls=%async_computation | async-start | bytes 4259840 | tf_op jit(solution)/shard_map/all_to_all | solution.py:634
  10.6 0.0 copy-start.2
  10.6 0.0 copy-start.3
  10.6 2.5 %shard_map.105 = f32[8,48,8,128]{3,2,1,0:T(8,128)} custom-call(f32[6,64,8,128]{3,2,1,0:T(8,128)} %bitcast.30), custom_call_target="tpu_custom_call" | custom-call | flops 1000000 | bytes 4000000 | tf_op jit(solution)/shard_map/pallas_call | solution.py:149
  13.1 0.0 copy-done.2
  13.1 0.0 copy-done.3
  13.1 19.9 %shard_map.106 = (s32[2048]{0:T(1024)S(1)}, s32[2048]{0:T(1024)S(1)}, s32[2048]{0:T(1024)S(1)}, s32[1]{0:T(128)}) custom-call(s32[2048]{0:T(1024)S(1)} %copy-done.2, s32[2048]{0:T(1024)S(1)} %bitcast.28, s32[1]{0:T(128)S(6)} %xor.3.chunk), custom_call_target="tpu_custom_call" | custom-call | flops 1000000000 | bytes 10000000 | tf_op jit(solution)/shard_map/pallas_call | solution.py:193
  33.0 4.0 %all-to-all-done.got = f32[8,65,8,128]{3,2,1,0:T(8,128)S(1)} async-done(((f32[8,65,8,128]{3,2,1,0:T(8,128)}), f32[8,65,8,128]{3,2,1,0:T(8,128)S(1)}, u32[]{:S(2)}, u32[]{:S(2)}) %all-to-all-start) | async-done | bytes 2129952 | tf_op jit(solution)/shard_map/all_to_all | solution.py:634
  37.0 4.3 %all-to-all-start.1 = ((f32[8,48,8,128]{3,2,1,0:T(8,128)}), f32[8,48,8,128]{3,2,1,0:T(8,128)}, u32[]{:S(2)}, u32[]{:S(2)}) async-start(f32[8,48,8,128]{3,2,1,0:T(8,128)} %shard_map.105), calls=%async_computation.1 | async-start | bytes 3145728 | tf_op jit(solution)/shard_map/all_to_all | solution.py:639
  41.3 6.0 %shard_map.107 = (f32[8,48,8,128]{3,2,1,0:T(8,128)S(1)}, f32[8,6,8,128]{3,2,1,0:T(8,128)S(1)}, f32[8,6,8,128]{3,2,1,0:T(8,128)S(1)}, f32[8,8,128]{2,1,0:T(8,128)...) custom-call(f32[8,65,8,128]{3,2,1,0:T(8,128)S(1)} %all-to-all-done.got), custom_call_target="tpu_custom_call" | custom-call | flops 10000000 | bytes 7000000 | tf_op jit(solution)/shard_map/pallas_call | solution.py:281
  47.3 1.9 %collective-permute-start = (f32[8,6,8,128]{3,2,1,0:T(8,128)S(1)}, f32[8,6,8,128]{3,2,1,0:T(8,128)S(1)}, u32[]{:S(2)}, u32[]{:S(2)}) collective-permute-start(f32[8,6,8,128]{3,2,1,0:T(8,128)S(1)} %get-tuple-element.37), channel_id=1, source_target_pairs={{0,1},{1,0},{18,19},{19,18},{4,5},{5,4},{22,23},{23,22},{8,9},{9,8... | collective-permute-start | bytes 589832 | tf_op jit(solution)/shard_map/ppermute | solution.py:423
  49.2 2.8 %collective-permute-start.1 = (f32[8,6,8,128]{3,2,1,0:T(8,128)S(1)}, f32[8,6,8,128]{3,2,1,0:T(8,128)S(1)}, u32[]{:S(2)}, u32[]{:S(2)}) collective-permute-start(f32[8,6,8,128]{3,2,1,0:T(8,128)S(1)} %get-tuple-element.38), channel_id=1, source_target_pairs={{0,31},{1,18},{18,1},{19,4},{4,19},{5,22},{22,5},{23,8},{8,23},{9,... | collective-permute-start | bytes 589832 | tf_op jit(solution)/shard_map/ppermute | solution.py:424
  52.1 0.0 collective-permute-start.2
  52.1 0.7 collective-permute-start.3
  52.7 1.2 shard_map.108.most
  53.9 5.4 %collective-permute-done.2.c = f32[8,8,128]{2,1,0:T(8,128)S(1)} collective-permute-done((f32[8,8,128]{2,1,0:T(8,128)S(1)}, f32[8,8,128]{2,1,0:T(8,128)S(1)}, u32[]{:S(2)}, u32[]{:S(2)}) %collective-permute-start.2) | collective-permute-done | bytes 32800 | tf_op jit(solution)/shard_map/ppermute | solution.py:425
  59.3 0.0 collective-permute-done.3.d
  59.3 0.0 collective-permute-done.a
  59.3 0.0 collective-permute-done.1.b
  59.3 1.1 all-to-all-done.1.got
  60.5 4.7 %shard_map.109 = (f32[8,48,8,128]{3,2,1,0:T(8,128)S(1)}, f32[8,48,8,128]{3,2,1,0:T(8,128)S(1)}, f32[8,48,8,128]{3,2,1,0:T(8,128)S(1)}, f32[8,6,8,128]{3,2,1,0:T(...) custom-call(f32[8,48,8,128]{3,2,1,0:T(8,128)} %all-to-all-done.1.got, ...), custom_call_target="tpu_custom_call" | custom-call | flops 10000000 | bytes 7000000 | tf_op jit(solution)/shard_map/pallas_call | solution.py:349
  65.1 3.5 %collective-permute-start.4 = (f32[8,6,8,128]{3,2,1,0:T(8,128)S(1)}, f32[8,6,8,128]{3,2,1,0:T(8,128)S(1)}, u32[]{:S(2)}, u32[]{:S(2)}) collective-permute-start(f32[8,6,8,128]{3,2,1,0:T(8,128)S(1)} %get-tuple-element.44), channel_id=1, source_target_pairs={{0,1},{1,0},{18,19},{19,18},{4,5},{5,4},{22,23},{23,22},{8,9},{9,8... | collective-permute-start | bytes 589832 | tf_op jit(solution)/shard_map/ppermute | solution.py:423
  68.7 1.8 %collective-permute-start.5 = (f32[8,6,8,128]{3,2,1,0:T(8,128)S(1)}, f32[8,6,8,128]{3,2,1,0:T(8,128)S(1)}, u32[]{:S(2)}, u32[]{:S(2)}) collective-permute-start(f32[8,6,8,128]{3,2,1,0:T(8,128)S(1)} %get-tuple-element.45), channel_id=1, source_target_pairs={{0,31},{1,18},{18,1},{19,4},{4,19},{5,22},{22,5},{23,8},{8,23},{9,... | collective-permute-start | bytes 589832 | tf_op jit(solution)/shard_map/ppermute | solution.py:424
  70.5 0.6 collective-permute-start.6
  71.1 0.7 collective-permute-start.7
  71.8 1.4 shard_map.110.most
  73.2 0.1 collective-permute-done.6.c
  73.2 0.0 collective-permute-done.7.d
  73.2 0.0 collective-permute-done.4.a
  73.2 3.8 %collective-permute-done.5.b = f32[8,6,8,128]{3,2,1,0:T(8,128)S(1)} collective-permute-done((f32[8,6,8,128]{3,2,1,0:T(8,128)S(1)}, f32[8,6,8,128]{3,2,1,0:T(8,128)S(1)}, u32[]{:S(2)}, u32[]{:S(2)}) %collective-permute-start.5) | collective-permute-done | bytes 196640 | tf_op jit(solution)/shard_map/ppermute | solution.py:424
  77.0 5.3 %shard_map.111 = f32[8,60,8,128]{3,2,1,0:T(8,128)S(1)} custom-call(s32[1]{0:T(128)} %get-tuple-element.30.count, s32[2048]{0:T(1024)S(1)} %get-tuple-element.31.faces, f32[8,48,8,128]{3,2,1,0:T(8,128)S(1)} %shard_map.110.most, f32[8,48,8,128]{3,2,1,0:T(8,128)S(1)} %get-tuple-element.41.psi, f32[8,17,8,128]{3,2,1,0:T(8,128)S(1)} %get-tuple-element.35.scale.scales, ...), custom_call_target="tpu_custom_call" | custom-call | flops 100000000 | bytes 7000000 | tf_op jit(solution)/shard_map/pallas_call | solution.py:513
  82.3 0.0 copy-start
  82.3 1.3 copy-done
  83.6 0.0 copy-start.4
  83.6 0.0 copy-start.1
  83.6 3.7 %all-to-all-start.2 = ((f32[8,60,8,128]{3,2,1,0:T(8,128)}), f32[8,60,8,128]{3,2,1,0:T(8,128)S(1)}, u32[]{:S(2)}, u32[]{:S(2)}) async-start(f32[8,60,8,128]{3,2,1,0:T(8,128)} %copy-done), calls=%async_computation.2 | async-start | bytes 3932160 | tf_op jit(solution)/shard_map/all_to_all | solution.py:649
  87.4 0.0 copy-done.4
  87.4 0.1 copy.13
  87.4 22.4 %all-to-all-done.2.got = f32[8,60,8,128]{3,2,1,0:T(8,128)S(1)} async-done(((f32[8,60,8,128]{3,2,1,0:T(8,128)}), f32[8,60,8,128]{3,2,1,0:T(8,128)S(1)}, u32[]{:S(2)}, u32[]{:S(2)}) %all-to-all-start.2) | async-done | bytes 1966112 | tf_op jit(solution)/shard_map/all_to_all | solution.py:649
  109.9 0.0 copy-done.1
  109.9 1.5 %shard_map.113 = f32[128,8,128]{2,1,0:T(8,128)} custom-call(f32[8,60,8,128]{3,2,1,0:T(8,128)S(1)} %all-to-all-done.2.got, f32[18,2048]{1,0:T(8,128)S(1)} %bitcast.23, s32[1,2048]{1,0:T(1,128)S(1)} %bitcast.26, s32[1,2048]{1,0:T(1,128)S(1)} %bitcast.25), custom_call_target="tpu_custom_call" | custom-call | flops 100000000 | bytes 2000000 | tf_op jit(solution)/shard_map/pallas_call | solution.py:585
  111.4 10.6 %all-to-all-start.3 = ((f32[128,8,128]{2,1,0:T(8,128)}), f32[128,8,128]{2,1,0:T(8,128)S(1)}, u32[]{:S(2)}, u32[]{:S(2)}) async-start(f32[128,8,128]{2,1,0:T(8,128)} %shard_map.113), calls=%async_computation.3 | async-start | bytes 1048576 | tf_op jit(solution)/shard_map/all_to_all | solution.py:651
  122.0 2.9 %shard_map.112 = f32[1,6,8,8192]{3,2,1,0:T(8,128)} custom-call(s32[1]{0:T(128)} %bitcast.flip, f32[8,60,8,128]{3,2,1,0:T(8,128)S(1)} %all-to-all-done.2.got), custom_call_target="tpu_custom_call" | custom-call | flops 1000000 | bytes 4000000 | tf_op jit(solution)/shard_map/pallas_call | solution.py:534
  124.8 10.8 %all-to-all-done.3.got = f32[128,8,128]{2,1,0:T(8,128)S(1)} async-done(((f32[128,8,128]{2,1,0:T(8,128)}), f32[128,8,128]{2,1,0:T(8,128)S(1)}, u32[]{:S(2)}, u32[]{:S(2)}) %all-to-all-start.3) | async-done | bytes 524320 | tf_op jit(solution)/shard_map/all_to_all | solution.py:651
  135.6 1.5 %shard_map.114 = f32[3,4096]{1,0:T(4,128)} custom-call(f32[128,8,128]{2,1,0:T(8,128)S(1)} %all-to-all-done.3.got), custom_call_target="tpu_custom_call" | custom-call | flops 100000000 | bytes 1000000 | tf_op jit(solution)/shard_map/pallas_call | solution.py:619
Async XLA Ops:
  3.7 33.2 %all-to-all-start = ((f32[8,65,8,128]{3,2,1,0:T(8,128)}), f32[8,65,8,128]{3,2,1,0:T(8,128)S(1)}, u32[]{:S(2)}, u32[]{:S(2)}) async-start(f32[8,65,8,128]{3,2,1,0:T(8,128)} %shard_map.104), calls=%async_computation | async-start | bytes 4259840 | tf_op jit(solution)/shard_map/all_to_all | solution.py:634
  10.6 2.6 %copy-start.2 = (s32[2048]{0:T(1024)S(1)}, s32[2048]{0:T(1024)}, u32[]{:S(2)}) copy-start(s32[2048]{0:T(1024)} %cell.1) | copy-start | bytes 24580
  10.6 2.6 %copy-start.3 = (s32[2048,1]{0,1:T(1,128)S(1)}, s32[2048,1]{0,1:T(1,128)}, u32[]{:S(2)}) copy-start(s32[2048,1]{0,1:T(1,128)} %param.16) | copy-start | bytes 24580
  37.0 23.5 %all-to-all-start.1 = ((f32[8,48,8,128]{3,2,1,0:T(8,128)}), f32[8,48,8,128]{3,2,1,0:T(8,128)}, u32[]{:S(2)}, u32[]{:S(2)}) async-start(f32[8,48,8,128]{3,2,1,0:T(8,128)} %shard_map.105), calls=%async_computation.1 | async-start | bytes 3145728 | tf_op jit(solution)/shard_map/all_to_all | solution.py:639
  47.3 12.0 %collective-permute-start = (f32[8,6,8,128]{3,2,1,0:T(8,128)S(1)}, f32[8,6,8,128]{3,2,1,0:T(8,128)S(1)}, u32[]{:S(2)}, u32[]{:S(2)}) collective-permute-start(f32[8,6,8,128]{3,2,1,0:T(8,128)S(1)} %get-tuple-element.37), channel_id=1, source_target_pairs={{0,1},{1,0},{18,19},{19,18},{4,5},{5,4},{22,23},{23,22},{8,9},{9,8... | collective-permute-start | bytes 589832 | tf_op jit(solution)/shard_map/ppermute | solution.py:423
  49.2 10.1 %collective-permute-start.1 = (f32[8,6,8,128]{3,2,1,0:T(8,128)S(1)}, f32[8,6,8,128]{3,2,1,0:T(8,128)S(1)}, u32[]{:S(2)}, u32[]{:S(2)}) collective-permute-start(f32[8,6,8,128]{3,2,1,0:T(8,128)S(1)} %get-tuple-element.38), channel_id=1, source_target_pairs={{0,31},{1,18},{18,1},{19,4},{4,19},{5,22},{22,5},{23,8},{8,23},{9,... | collective-permute-start | bytes 589832 | tf_op jit(solution)/shard_map/ppermute | solution.py:424
  52.1 7.3 %collective-permute-start.2 = (f32[8,8,128]{2,1,0:T(8,128)S(1)}, f32[8,8,128]{2,1,0:T(8,128)S(1)}, u32[]{:S(2)}, u32[]{:S(2)}) collective-permute-start(f32[8,8,128]{2,1,0:T(8,128)S(1)} %get-tuple-element.39), channel_id=1, source_target_pairs={{0,16},{1,17},{18,2},{19,3},{4,20},{5,21},{22,6},{23,7},{8,24},{9,... | collective-permute-start | bytes 98312 | tf_op jit(solution)/shard_map/ppermute | solution.py:425
  52.1 7.3 %collective-permute-start.3 = (f32[8,8,128]{2,1,0:T(8,128)S(1)}, f32[8,8,128]{2,1,0:T(8,128)S(1)}, u32[]{:S(2)}, u32[]{:S(2)}) collective-permute-start(f32[8,8,128]{2,1,0:T(8,128)S(1)} %get-tuple-element.40), channel_id=1, source_target_pairs={{16,32},{17,33},{2,50},{3,51},{20,36},{21,37},{6,54},{7,55},{24,40... | collective-permute-start | bytes 98312 | tf_op jit(solution)/shard_map/ppermute | solution.py:426
  65.1 8.1 %collective-permute-start.4 = (f32[8,6,8,128]{3,2,1,0:T(8,128)S(1)}, f32[8,6,8,128]{3,2,1,0:T(8,128)S(1)}, u32[]{:S(2)}, u32[]{:S(2)}) collective-permute-start(f32[8,6,8,128]{3,2,1,0:T(8,128)S(1)} %get-tuple-element.44), channel_id=1, source_target_pairs={{0,1},{1,0},{18,19},{19,18},{4,5},{5,4},{22,23},{23,22},{8,9},{9,8... | collective-permute-start | bytes 589832 | tf_op jit(solution)/shard_map/ppermute | solution.py:423
  68.7 8.4 %collective-permute-start.5 = (f32[8,6,8,128]{3,2,1,0:T(8,128)S(1)}, f32[8,6,8,128]{3,2,1,0:T(8,128)S(1)}, u32[]{:S(2)}, u32[]{:S(2)}) collective-permute-start(f32[8,6,8,128]{3,2,1,0:T(8,128)S(1)} %get-tuple-element.45), channel_id=1, source_target_pairs={{0,31},{1,18},{18,1},{19,4},{4,19},{5,22},{22,5},{23,8},{8,23},{9,... | collective-permute-start | bytes 589832 | tf_op jit(solution)/shard_map/ppermute | solution.py:424
  70.5 2.8 %collective-permute-start.6 = (f32[8,8,128]{2,1,0:T(8,128)S(1)}, f32[8,8,128]{2,1,0:T(8,128)S(1)}, u32[]{:S(2)}, u32[]{:S(2)}) collective-permute-start(f32[8,8,128]{2,1,0:T(8,128)S(1)} %get-tuple-element.46), channel_id=1, source_target_pairs={{0,16},{1,17},{18,2},{19,3},{4,20},{5,21},{22,6},{23,7},{8,24},{9,... | collective-permute-start | bytes 98312 | tf_op jit(solution)/shard_map/ppermute | solution.py:425
  71.1 2.1 %collective-permute-start.7 = (f32[8,8,128]{2,1,0:T(8,128)S(1)}, f32[8,8,128]{2,1,0:T(8,128)S(1)}, u32[]{:S(2)}, u32[]{:S(2)}) collective-permute-start(f32[8,8,128]{2,1,0:T(8,128)S(1)} %get-tuple-element.47), channel_id=1, source_target_pairs={{16,32},{17,33},{2,50},{3,51},{20,36},{21,37},{6,54},{7,55},{24,40... | collective-permute-start | bytes 98312 | tf_op jit(solution)/shard_map/ppermute | solution.py:426
  82.3 1.3 copy-start
  83.6 3.7 %copy-start.4 = (f32[1,18,2048]{2,0,1:T(1,128)S(1)}, f32[1,18,2048]{2,0,1:T(1,128)}, u32[]{:S(2)}) copy-start(f32[1,18,2048]{2,0,1:T(1,128)} %param.14) | copy-start | bytes 442372
  83.6 26.2 %copy-start.1 = (s32[2048]{0:T(1024)S(1)}, s32[2048]{0:T(1024)}, u32[]{:S(2)}) copy-start(s32[2048]{0:T(1024)} %param.17) | copy-start | bytes 24580
  83.6 26.2 %all-to-all-start.2 = ((f32[8,60,8,128]{3,2,1,0:T(8,128)}), f32[8,60,8,128]{3,2,1,0:T(8,128)S(1)}, u32[]{:S(2)}, u32[]{:S(2)}) async-start(f32[8,60,8,128]{3,2,1,0:T(8,128)} %copy-done), calls=%async_computation.2 | async-start | bytes 3932160 | tf_op jit(solution)/shard_map/all_to_all | solution.py:649
  111.4 24.2 %all-to-all-start.3 = ((f32[128,8,128]{2,1,0:T(8,128)}), f32[128,8,128]{2,1,0:T(8,128)S(1)}, u32[]{:S(2)}, u32[]{:S(2)}) async-start(f32[128,8,128]{2,1,0:T(8,128)} %shard_map.113), calls=%async_computation.3 | async-start | bytes 1048576 | tf_op jit(solution)/shard_map/all_to_all | solution.py:651
